TPU v7x, 512 devices: a whole 4x4x16 slice. The times are simulated.
512 devices in a mesh: outer: 32 (over x, y, core), inner: 16 (over z).
Axes of the slice: x: 4, y: 4, z: 16, core: 2. Of those that a mesh axis runs over, the one named last changes fastest.
Arguments:
- right_side: float32 [256, 512, 128], P('outer', 'inner'), may hold values from -8 to 8
- codes: int32 [256, 512, 128], P('outer', 'inner'), may hold values from 0 to 7
Outputs:
- solution_field: float32 [256, 512, 128], P('outer', 'inner')
- residual: float32 [256, 512, 128], P('outer', 'inner')
All inputs are finite; a program needn't handle non-finite values.
Results may differ from a plain program's by a relative error of at most 0.000062.
Values sent between devices are 32-bit elements; how exact they have to be, the bound alone decides.
No kernel may reach another device: no remote copies, remote signals or barrier semaphores. Data moves between devices by JAX's collectives and lax.ppermute only.
A program may use at most 64 MiB of HBM per device.

v0:
```python
import jax
import jax.numpy as jnp
from jax import lax
from jax.sharding import PartitionSpec as P

LEVELS = 4
NU_PRE = 2
NU_POST = 2
NU_COARSE = 6


OMEGA = 0.8


def with_halo(cells, sides, width):
    for axis, dim in sides:
        count = lax.axis_size(axis)
        ends = count - 1
        head = lax.slice_in_dim(cells, 0, width, axis=dim)
        tail = lax.slice_in_dim(cells, cells.shape[dim] - width, cells.shape[dim], axis=dim)
        cells = jnp.concatenate(
            [
                lax.ppermute(tail, axis, [(i, (i + 1) % count) for i in range(ends)]),
                cells,
                lax.ppermute(head, axis, [((i + 1) % count, i) for i in range(ends)]),
            ],
            axis=dim,
        )
    return cells


def neighbours(ext, center):
    zeros = jnp.zeros_like(center[:, :, :1])
    return [
        ext[2:, 1:-1],
        ext[:-2, 1:-1],
        ext[1:-1, 2:],
        ext[1:-1, :-2],
        jnp.concatenate([center[:, :, 1:], zeros], axis=2),
        jnp.concatenate([zeros, center[:, :, :-1]], axis=2),
    ]


def face_terms(kappa_ext, kappa):
    return [0.5 * (kappa + other) for other in neighbours(kappa_ext, kappa)]


def apply_op(ext, field, faces, scale):
    total = jnp.zeros_like(field)
    for face, other in zip(faces, neighbours(ext, field)):
        total = total + face * (field - other)
    return total * scale


def diagonal_of(faces, scale):
    total = jnp.zeros_like(faces[0])
    for face in faces:
        total = total + face
    return total * scale


def smooth(extend, field, source, faces, diag, scale, count):
    for sweep in range(count):
        field = field + OMEGA * (source - apply_op(extend(field), field, faces, scale)) / diag
    return field


def restrict(field):
    a, b, c = field.shape
    return field.reshape(a // 2, 2, b // 2, 2, c // 2, 2).mean(axis=(1, 3, 5))


def prolong(field):
    a, b, c = field.shape
    wide = jnp.broadcast_to(field[:, None, :, None, :, None], (a, 2, b, 2, c, 2))
    return wide.reshape(2 * a, 2 * b, 2 * c)


def box_extend(field):
    return with_halo(field, (("outer", 0), ("inner", 1)), 1)


def slab_extend(field):
    ext = with_halo(field, (("outer", 0),), 1)
    return jnp.pad(ext, ((0, 0), (1, 1), (0, 0)))


def extender(layout):
    if layout == "box":
        return box_extend
    return slab_extend


def level_shift(extend, field, source, faces, scale):
    leftover = source - apply_op(extend(field), field, faces, scale)
    ones = jnp.ones_like(field)
    weight = apply_op(extend(ones), ones, faces, scale)
    totals = (jnp.sum(leftover), jnp.sum(weight))
    totals = lax.psum((totals[0], totals[1]), "outer")
    return totals[0] / totals[1]


def cycle(level, source, kappa, layout, joined_at):
    extend = extender(layout)
    scale = 0.25**level
    faces = face_terms(extend(kappa), kappa)
    diag = diagonal_of(faces, scale)
    field = OMEGA * source / diag
    if level == LEVELS - 1:
        field = smooth(extend, field, source, faces, diag, scale, NU_COARSE - 1)
        return field + level_shift(extend, field, source, faces, scale)
    field = smooth(extend, field, source, faces, diag, scale, NU_PRE - 1)
    remainder = source - apply_op(extend(field), field, faces, scale)
    small_source = restrict(remainder)
    small_kappa = restrict(kappa)
    if layout == "box" and level + 1 == joined_at:
        width = small_source.shape[1]
        group_source, group_kappa = (
            lax.all_gather(small_source, "inner", axis=1, tiled=True),
            lax.all_gather(small_kappa, "inner", axis=1, tiled=True),
        )
        group_corr = cycle(level + 1, group_source, group_kappa, "slab", joined_at)
        correction = lax.dynamic_slice_in_dim(group_corr, lax.axis_index("inner") * width, width, 1)
    else:
        correction = cycle(level + 1, small_source, small_kappa, layout, joined_at)
    field = field + prolong(correction)
    return smooth(extend, field, source, faces, diag, scale, NU_POST)


def body(right_side, codes):
    kappa = jnp.exp(0.5 * codes.astype(jnp.float32))
    joined_at = 2
    solution_field = cycle(0, right_side, kappa, "box", joined_at)
    faces = face_terms(box_extend(kappa), kappa)
    residual = right_side - apply_op(box_extend(solution_field), solution_field, faces, 1.0)
    return (solution_field, residual)


def solution(mesh):
    placed = (P("outer", "inner", None), P("outer", "inner", None))
    return jax.shard_map(
        body,
        mesh=mesh,
        in_specs=placed,
        out_specs=(P("outer", "inner", None), P("outer", "inner", None)),
        check_vma=False,
    )
```

profile of v0, /device:TPU:134, one launch (start us, length us, event | category | flops | bytes accessed | tf_op | source)
XLA Modules:
  0.0 466.1 jit_solution(14534040674350204930)
XLA Ops:
  1.6 9.8 %reshape.67 = f32[4,2,16,2,64,2]{5,4,3,2,1,0:T(8,128)} reshape(f32[8,32,128]{2,1,0:T(8,128)S(1)} %multiply_exponential_fusion) | data formatting | bytes 262144 | tf_op jit(solution)/shard_map/reshape | solution.py:70
  16.7 30.0 %all_gather.7 = f32[2,128,32]{2,0,1:T(2,128)S(1)} all-gather(f32[2,8,32]{2,0,1:T(2,128)S(1)} %copy.108), channel_id=1, replica_groups=mesh['outer'=32,'inner'=16] {'inner'}, dimensions={1}, use_global_device_ids=true | all-gather | bytes 34816 | tf_op jit(solution)/shard_map/all_gather | solution.py:120
  52.6 5.3 %collective-permute-start = (f32[1,32,128]{2,1,0:T(8,128)S(1)}, f32[1,32,128]{2,1,0:T(8,128)S(1)}, u32[]{:S(2)}, u32[]{:S(2)}) collective-permute-start(f32[1,32,128]{2,1,0:T(8,128)S(1)} %get-tuple-element.60), channel_id=1, source_target_pairs={{16,0},{32,16},{48,32},{64,48},{80,64},{96,80},{112,96},{128,112},... | collective-permute-start | bytes 49160 | tf_op jit(solution)/shard_map/ppermute | solution.py:25
  59.8 5.8 %collective-permute-start.44 = (f32[1,64,16]{1,2,0:T(8,128)S(1)}, f32[1,64,16]{1,2,0:T(8,128)S(1)}, u32[]{:S(2)}, u32[]{:S(2)}) collective-permute-start(f32[1,64,16]{1,2,0:T(8,128)S(1)} %broadcast_in_dim.27), channel_id=1, source_target_pairs={{16,0},{32,16},{48,32},{64,48},{80,64},{96,80},{112,96},{128,112},... | collective-permute-start | bytes 12296 | tf_op jit(solution)/shard_map/ppermute | solution.py:25
  67.8 5.8 %collective-permute-start.12 = (f32[1,16,64]{2,1,0:T(8,128)S(1)}, f32[1,16,64]{2,1,0:T(8,128)S(1)}, u32[]{:S(2)}, u32[]{:S(2)}) collective-permute-start(f32[1,16,64]{2,1,0:T(8,128)S(1)} %get-tuple-element.112), channel_id=1, source_target_pairs={{16,0},{32,16},{48,32},{64,48},{80,64},{96,80},{112,96},{128,112},... | collective-permute-start | bytes 12296 | tf_op jit(solution)/shard_map/ppermute | solution.py:25
  91.8 4.7 %collective-permute-done.5 = f32[1,32,128]{2,1,0:T(8,128)S(1)} collective-permute-done((f32[1,32,128]{2,1,0:T(8,128)S(1)}, f32[1,32,128]{2,1,0:T(8,128)S(1)}, u32[]{:S(2)}, u32[]{:S(2)}) %collective-permute-start.5) | collective-permute-done | bytes 16416 | tf_op jit(solution)/shard_map/ppermute | solution.py:23
  110.1 5.5 %collective-permute-start.8 = (f32[1,32,128]{2,1,0:T(8,128)S(1)}, f32[1,32,128]{2,1,0:T(8,128)S(1)}, u32[]{:S(2)}, u32[]{:S(2)}) collective-permute-start(f32[1,32,128]{2,1,0:T(8,128)S(1)} %get-tuple-element.52), channel_id=1, source_target_pairs={{16,0},{32,16},{48,32},{64,48},{80,64},{96,80},{112,96},{128,112},... | collective-permute-start | bytes 49160 | tf_op jit(solution)/shard_map/ppermute | solution.py:25
  117.6 5.2 %collective-permute-done.9 = f32[1,32,128]{2,1,0:T(8,128)S(1)} collective-permute-done((f32[1,32,128]{2,1,0:T(8,128)S(1)}, f32[1,32,128]{2,1,0:T(8,128)S(1)}, u32[]{:S(2)}, u32[]{:S(2)}) %collective-permute-start.9) | collective-permute-done | bytes 16416 | tf_op jit(solution)/shard_map/ppermute | solution.py:23
  131.9 9.8 %reshape.66 = f32[4,2,16,2,64,2]{5,4,3,2,1,0:T(8,128)} reshape(f32[8,32,128]{2,1,0:T(8,128)S(1)} %fusion.53) | data formatting | bytes 262144 | tf_op jit(solution)/shard_map/reshape | solution.py:70
  161.0 4.7 %collective-permute-done.19 = f32[6,1,64]{2,1,0:T(1,128)S(1)} collective-permute-done((f32[6,1,64]{2,1,0:T(1,128)S(1)}, f32[6,1,64]{2,1,0:T(1,128)S(1)}, u32[]{:S(2)}, u32[]{:S(2)}) %collective-permute-start.19) | collective-permute-done | bytes 1568 | tf_op jit(solution)/shard_map/ppermute | solution.py:23
  184.8 27.4 %all_gather.6 = f32[2,128,32]{2,0,1:T(2,128)S(1)} all-gather(f32[2,8,32]{2,0,1:T(2,128)S(1)} %copy.106), channel_id=1, replica_groups=mesh['outer'=32,'inner'=16] {'inner'}, dimensions={1}, use_global_device_ids=true | all-gather | bytes 34816 | tf_op jit(solution)/shard_map/all_gather | solution.py:119
  216.8 4.7 %collective-permute-done.27 = f32[1,128,32]{1,2,0:T(8,128)S(1)} collective-permute-done((f32[1,128,32]{1,2,0:T(8,128)S(1)}, f32[1,128,32]{1,2,0:T(8,128)S(1)}, u32[]{:S(2)}, u32[]{:S(2)}) %collective-permute-start.27) | collective-permute-done | bytes 16416 | tf_op jit(solution)/shard_map/ppermute | solution.py:23
  226.1 4.7 %collective-permute-done.29 = f32[1,128,32]{1,2,0:T(8,128)S(1)} collective-permute-done((f32[1,128,32]{1,2,0:T(8,128)S(1)}, f32[1,128,32]{1,2,0:T(8,128)S(1)}, u32[]{:S(2)}, u32[]{:S(2)}) %collective-permute-start.29) | collective-permute-done | bytes 16416 | tf_op jit(solution)/shard_map/ppermute | solution.py:23
  236.6 4.6 collective-permute-done.33
  245.8 4.6 collective-permute-done.35
  288.0 53.6 %all-reduce.59 = (f32[]{:T(128)}, f32[]{:T(128)}) all-reduce(f32[]{:T(128)} %fusion.246, f32[]{:T(128)} %get-tuple-element.4), channel_id=1, replica_groups=mesh['outer'=32,'inner'=16] {'outer'}, use_global_device_ids=true, to_apply=%region_9.10 | all-reduce | flops 2 | bytes 16 | tf_op jit(solution)/shard_map/psum | solution.py:99
  348.1 4.7 %collective-permute-done.47 = f32[1,128,32]{1,2,0:T(8,128)S(1)} collective-permute-done((f32[1,128,32]{1,2,0:T(8,128)S(1)}, f32[1,128,32]{1,2,0:T(8,128)S(1)}, u32[]{:S(2)}, u32[]{:S(2)}) %collective-permute-start.47) | collective-permute-done | bytes 16416 | tf_op jit(solution)/shard_map/ppermute | solution.py:23
  357.4 4.7 %collective-permute-done.49 = f32[1,128,32]{1,2,0:T(8,128)S(1)} collective-permute-done((f32[1,128,32]{1,2,0:T(8,128)S(1)}, f32[1,128,32]{1,2,0:T(8,128)S(1)}, u32[]{:S(2)}, u32[]{:S(2)}) %collective-permute-start.49) | collective-permute-done | bytes 16416 | tf_op jit(solution)/shard_map/ppermute | solution.py:23
  367.7 4.7 collective-permute-done.51
  386.7 4.7 collective-permute-done.55
  404.0 6.9 %reshape.70 = f32[8,32,128]{2,1,0:T(8,128)S(1)} reshape(f32[4,2,16,2,64,2]{5,4,3,2,1,0:T(8,128)} %broadcast_in_dim.33) | data formatting | bytes 262144 | tf_op jit(solution)/shard_map/reshape | solution.py:76
  415.3 4.7 %collective-permute-done.59 = f32[1,32,128]{2,1,0:T(8,128)S(1)} collective-permute-done((f32[1,32,128]{2,1,0:T(8,128)S(1)}, f32[1,32,128]{2,1,0:T(8,128)S(1)}, u32[]{:S(2)}, u32[]{:S(2)}) %collective-permute-start.59) | collective-permute-done | bytes 16416 | tf_op jit(solution)/shard_map/ppermute | solution.py:23
  433.3 4.7 %collective-permute-done.63 = f32[1,32,128]{2,1,0:T(8,128)S(1)} collective-permute-done((f32[1,32,128]{2,1,0:T(8,128)S(1)}, f32[1,32,128]{2,1,0:T(8,128)S(1)}, u32[]{:S(2)}, u32[]{:S(2)}) %collective-permute-start.63) | collective-permute-done | bytes 16416 | tf_op jit(solution)/shard_map/ppermute | solution.py:23
  451.9 4.7 %collective-permute-done.67 = f32[1,32,128]{2,1,0:T(8,128)S(1)} collective-permute-done((f32[1,32,128]{2,1,0:T(8,128)S(1)}, f32[1,32,128]{2,1,0:T(8,128)S(1)}, u32[]{:S(2)}, u32[]{:S(2)}) %collective-permute-start.67) | collective-permute-done | bytes 16416 | tf_op jit(solution)/shard_map/ppermute | solution.py:23
  (252 shorter events, 236.5 us)
Async XLA Ops:
  48.2 25.4 %collective-permute-start.30 = (f32[1,64,16]{1,2,0:T(8,128)S(1)}, f32[1,64,16]{1,2,0:T(8,128)S(1)}, u32[]{:S(2)}, u32[]{:S(2)}) collective-permute-start(f32[1,64,16]{1,2,0:T(8,128)S(1)} %multiply_bitcast_fusion), channel_id=1, source_target_pairs={{16,0},{32,16},{48,32},{64,48},{80,64},{96,80},{112,96},{128,112},... | collective-permute-start | bytes 12296 | tf_op jit(solution)/shard_map/ppermute | solution.py:25
  50.2 26.4 %collective-permute-start.31 = (f32[1,64,16]{1,2,0:T(8,128)S(1)}, f32[1,64,16]{1,2,0:T(8,128)S(1)}, u32[]{:S(2)}, u32[]{:S(2)}) collective-permute-start(f32[1,64,16]{1,2,0:T(8,128)S(1)} %multiply_bitcast_fusion), channel_id=1, source_target_pairs={{0,16},{16,32},{32,48},{48,64},{64,80},{80,96},{96,112},{112,128},... | collective-permute-start | bytes 12296 | tf_op jit(solution)/shard_map/ppermute | solution.py:23
  52.6 13.3 %collective-permute-start = (f32[1,32,128]{2,1,0:T(8,128)S(1)}, f32[1,32,128]{2,1,0:T(8,128)S(1)}, u32[]{:S(2)}, u32[]{:S(2)}) collective-permute-start(f32[1,32,128]{2,1,0:T(8,128)S(1)} %get-tuple-element.60), channel_id=1, source_target_pairs={{16,0},{32,16},{48,32},{64,48},{80,64},{96,80},{112,96},{128,112},... | collective-permute-start | bytes 49160 | tf_op jit(solution)/shard_map/ppermute | solution.py:25
  57.9 9.9 %collective-permute-start.1 = (f32[1,32,128]{2,1,0:T(8,128)S(1)}, f32[1,32,128]{2,1,0:T(8,128)S(1)}, u32[]{:S(2)}, u32[]{:S(2)}) collective-permute-start(f32[1,32,128]{2,1,0:T(8,128)S(1)} %get-tuple-element.59), channel_id=1, source_target_pairs={{0,16},{16,32},{32,48},{48,64},{64,80},{80,96},{96,112},{112,128},... | collective-permute-start | bytes 49160 | tf_op jit(solution)/shard_map/ppermute | solution.py:23
  59.8 50.3 %collective-permute-start.44 = (f32[1,64,16]{1,2,0:T(8,128)S(1)}, f32[1,64,16]{1,2,0:T(8,128)S(1)}, u32[]{:S(2)}, u32[]{:S(2)}) collective-permute-start(f32[1,64,16]{1,2,0:T(8,128)S(1)} %broadcast_in_dim.27), channel_id=1, source_target_pairs={{16,0},{32,16},{48,32},{64,48},{80,64},{96,80},{112,96},{128,112},... | collective-permute-start | bytes 12296 | tf_op jit(solution)/shard_map/ppermute | solution.py:25
  65.9 49.7 %collective-permute-start.45 = (f32[1,64,16]{1,2,0:T(8,128)S(1)}, f32[1,64,16]{1,2,0:T(8,128)S(1)}, u32[]{:S(2)}, u32[]{:S(2)}) collective-permute-start(f32[1,64,16]{1,2,0:T(8,128)S(1)} %broadcast_in_dim.27), channel_id=1, source_target_pairs={{0,16},{16,32},{32,48},{48,64},{64,80},{80,96},{96,112},{112,128},... | collective-permute-start | bytes 12296 | tf_op jit(solution)/shard_map/ppermute | solution.py:23
  67.8 19.6 %collective-permute-start.12 = (f32[1,16,64]{2,1,0:T(8,128)S(1)}, f32[1,16,64]{2,1,0:T(8,128)S(1)}, u32[]{:S(2)}, u32[]{:S(2)}) collective-permute-start(f32[1,16,64]{2,1,0:T(8,128)S(1)} %get-tuple-element.112), channel_id=1, source_target_pairs={{16,0},{32,16},{48,32},{64,48},{80,64},{96,80},{112,96},{128,112},... | collective-permute-start | bytes 12296 | tf_op jit(solution)/shard_map/ppermute | solution.py:25
  79.6 9.8 %collective-permute-start.13 = (f32[1,16,64]{2,1,0:T(8,128)S(1)}, f32[1,16,64]{2,1,0:T(8,128)S(1)}, u32[]{:S(2)}, u32[]{:S(2)}) collective-permute-start(f32[1,16,64]{2,1,0:T(8,128)S(1)} %get-tuple-element.111), channel_id=1, source_target_pairs={{0,16},{16,32},{32,48},{48,64},{64,80},{80,96},{96,112},{112,128},... | collective-permute-start | bytes 12296 | tf_op jit(solution)/shard_map/ppermute | solution.py:23
  83.3 86.9 %collective-permute-start.24 = (f32[1,128,32]{1,2,0:T(8,128)S(1)}, f32[1,128,32]{1,2,0:T(8,128)S(1)}, u32[]{:S(2)}, u32[]{:S(2)}) collective-permute-start(f32[1,128,32]{1,2,0:T(8,128)S(1)} %get-tuple-element.99), channel_id=1, source_target_pairs={{16,0},{32,16},{48,32},{64,48},{80,64},{96,80},{112,96},{128,112},... | collective-permute-start | bytes 49160 | tf_op jit(solution)/shard_map/ppermute | solution.py:25
  89.4 7.2 %collective-permute-start.5 = (f32[1,32,128]{2,1,0:T(8,128)S(1)}, f32[1,32,128]{2,1,0:T(8,128)S(1)}, u32[]{:S(2)}, u32[]{:S(2)}) collective-permute-start(f32[1,32,128]{2,1,0:T(8,128)S(1)} %get-tuple-element.55), channel_id=1, source_target_pairs={{0,16},{16,32},{32,48},{48,64},{64,80},{80,96},{96,112},{112,128},... | collective-permute-start | bytes 49160 | tf_op jit(solution)/shard_map/ppermute | solution.py:23
  102.8 67.4 %collective-permute-start.25 = (f32[1,128,32]{1,2,0:T(8,128)S(1)}, f32[1,128,32]{1,2,0:T(8,128)S(1)}, u32[]{:S(2)}, u32[]{:S(2)}) collective-permute-start(f32[1,128,32]{1,2,0:T(8,128)S(1)} %get-tuple-element.100), channel_id=1, source_target_pairs={{0,16},{16,32},{32,48},{48,64},{64,80},{80,96},{96,112},{112,128},... | collective-permute-start | bytes 49160 | tf_op jit(solution)/shard_map/ppermute | solution.py:23
  107.4 38.3 %collective-permute-start.14 = (f32[6,1,64]{2,1,0:T(1,128)S(1)}, f32[6,1,64]{2,1,0:T(1,128)S(1)}, u32[]{:S(2)}, u32[]{:S(2)}) collective-permute-start(f32[6,1,64]{2,1,0:T(1,128)S(1)} %get-tuple-element.70), channel_id=1, source_target_pairs={{1,0},{2,1},{3,2},{4,3},{5,4},{6,5},{7,6},{8,7},{9,8},{10,9},{11,1... | collective-permute-start | bytes 4616 | tf_op jit(solution)/shard_map/ppermute | solution.py:25
  110.1 7.5 %collective-permute-start.8 = (f32[1,32,128]{2,1,0:T(8,128)S(1)}, f32[1,32,128]{2,1,0:T(8,128)S(1)}, u32[]{:S(2)}, u32[]{:S(2)}) collective-permute-start(f32[1,32,128]{2,1,0:T(8,128)S(1)} %get-tuple-element.52), channel_id=1, source_target_pairs={{16,0},{32,16},{48,32},{64,48},{80,64},{96,80},{112,96},{128,112},... | collective-permute-start | bytes 49160 | tf_op jit(solution)/shard_map/ppermute | solution.py:25
  115.6 7.2 %collective-permute-start.9 = (f32[1,32,128]{2,1,0:T(8,128)S(1)}, f32[1,32,128]{2,1,0:T(8,128)S(1)}, u32[]{:S(2)}, u32[]{:S(2)}) collective-permute-start(f32[1,32,128]{2,1,0:T(8,128)S(1)} %get-tuple-element.51), channel_id=1, source_target_pairs={{0,16},{16,32},{32,48},{48,64},{64,80},{80,96},{96,112},{112,128},... | collective-permute-start | bytes 49160 | tf_op jit(solution)/shard_map/ppermute | solution.py:23
  128.7 17.0 %collective-permute-start.15 = (f32[6,1,64]{2,1,0:T(1,128)S(1)}, f32[6,1,64]{2,1,0:T(1,128)S(1)}, u32[]{:S(2)}, u32[]{:S(2)}) collective-permute-start(f32[6,1,64]{2,1,0:T(1,128)S(1)} %get-tuple-element.69), channel_id=1, source_target_pairs={{0,1},{1,2},{2,3},{3,4},{4,5},{5,6},{6,7},{7,8},{8,9},{9,10},{10,1... | collective-permute-start | bytes 4616 | tf_op jit(solution)/shard_map/ppermute | solution.py:23
  167.7 7.1 %collective-permute-start.21 = (f32[1,16,64]{2,1,0:T(8,128)S(1)}, f32[1,16,64]{2,1,0:T(8,128)S(1)}, u32[]{:S(2)}, u32[]{:S(2)}) collective-permute-start(f32[1,16,64]{2,1,0:T(8,128)S(1)} %get-tuple-element.103), channel_id=1, source_target_pairs={{0,16},{16,32},{32,48},{48,64},{64,80},{80,96},{96,112},{112,128},... | collective-permute-start | bytes 12296 | tf_op jit(solution)/shard_map/ppermute | solution.py:23
  214.3 7.2 %collective-permute-start.27 = (f32[1,128,32]{1,2,0:T(8,128)S(1)}, f32[1,128,32]{1,2,0:T(8,128)S(1)}, u32[]{:S(2)}, u32[]{:S(2)}) collective-permute-start(f32[1,128,32]{1,2,0:T(8,128)S(1)} %get-tuple-element.95), channel_id=1, source_target_pairs={{0,16},{16,32},{32,48},{48,64},{64,80},{80,96},{96,112},{112,128},... | collective-permute-start | bytes 49160 | tf_op jit(solution)/shard_map/ppermute | solution.py:23
  223.6 7.2 %collective-permute-start.29 = (f32[1,128,32]{1,2,0:T(8,128)S(1)}, f32[1,128,32]{1,2,0:T(8,128)S(1)}, u32[]{:S(2)}, u32[]{:S(2)}) collective-permute-start(f32[1,128,32]{1,2,0:T(8,128)S(1)} %get-tuple-element.91), channel_id=1, source_target_pairs={{0,16},{16,32},{32,48},{48,64},{64,80},{80,96},{96,112},{112,128},... | collective-permute-start | bytes 49160 | tf_op jit(solution)/shard_map/ppermute | solution.py:23
  234.2 7.1 %collective-permute-start.33 = (f32[1,64,16]{1,2,0:T(8,128)S(1)}, f32[1,64,16]{1,2,0:T(8,128)S(1)}, u32[]{:S(2)}, u32[]{:S(2)}) collective-permute-start(f32[1,64,16]{1,2,0:T(8,128)S(1)} %bitcast_divide_fusion), channel_id=1, source_target_pairs={{0,16},{16,32},{32,48},{48,64},{64,80},{80,96},{96,112},{112,128},... | collective-permute-start | bytes 12296 | tf_op jit(solution)/shard_map/ppermute | solution.py:23
  345.6 7.2 %collective-permute-start.47 = (f32[1,128,32]{1,2,0:T(8,128)S(1)}, f32[1,128,32]{1,2,0:T(8,128)S(1)}, u32[]{:S(2)}, u32[]{:S(2)}) collective-permute-start(f32[1,128,32]{1,2,0:T(8,128)S(1)} %get-tuple-element.87), channel_id=1, source_target_pairs={{0,16},{16,32},{32,48},{48,64},{64,80},{80,96},{96,112},{112,128},... | collective-permute-start | bytes 49160 | tf_op jit(solution)/shard_map/ppermute | solution.py:23
  354.9 7.2 %collective-permute-start.49 = (f32[1,128,32]{1,2,0:T(8,128)S(1)}, f32[1,128,32]{1,2,0:T(8,128)S(1)}, u32[]{:S(2)}, u32[]{:S(2)}) collective-permute-start(f32[1,128,32]{1,2,0:T(8,128)S(1)} %get-tuple-element.83), channel_id=1, source_target_pairs={{0,16},{16,32},{32,48},{48,64},{64,80},{80,96},{96,112},{112,128},... | collective-permute-start | bytes 49160 | tf_op jit(solution)/shard_map/ppermute | solution.py:23
  412.9 7.2 %collective-permute-start.59 = (f32[1,32,128]{2,1,0:T(8,128)S(1)}, f32[1,32,128]{2,1,0:T(8,128)S(1)}, u32[]{:S(2)}, u32[]{:S(2)}) collective-permute-start(f32[1,32,128]{2,1,0:T(8,128)S(1)} %get-tuple-element.47), channel_id=1, source_target_pairs={{0,16},{16,32},{32,48},{48,64},{64,80},{80,96},{96,112},{112,128},... | collective-permute-start | bytes 49160 | tf_op jit(solution)/shard_map/ppermute | solution.py:23
  430.9 7.2 %collective-permute-start.63 = (f32[1,32,128]{2,1,0:T(8,128)S(1)}, f32[1,32,128]{2,1,0:T(8,128)S(1)}, u32[]{:S(2)}, u32[]{:S(2)}) collective-permute-start(f32[1,32,128]{2,1,0:T(8,128)S(1)} %get-tuple-element.43), channel_id=1, source_target_pairs={{0,16},{16,32},{32,48},{48,64},{64,80},{80,96},{96,112},{112,128},... | collective-permute-start | bytes 49160 | tf_op jit(solution)/shard_map/ppermute | solution.py:23
  449.4 7.2 %collective-permute-start.67 = (f32[1,32,128]{2,1,0:T(8,128)S(1)}, f32[1,32,128]{2,1,0:T(8,128)S(1)}, u32[]{:S(2)}, u32[]{:S(2)}) collective-permute-start(f32[1,32,128]{2,1,0:T(8,128)S(1)} %get-tuple-element.39), channel_id=1, source_target_pairs={{0,16},{16,32},{32,48},{48,64},{64,80},{80,96},{96,112},{112,128},... | collective-permute-start | bytes 49160 | tf_op jit(solution)/shard_map/ppermute | solution.py:23
  (51 other events, 470.1 us)
where the time goes:
time: 468 us; the launch traced here: 466 us
  starting transfers between devices  181 us (39%)
  waiting for transfers between devices  117 us (25%)
  blocking collectives  111 us (24%)
  local copies, waits for them, and re-layouts  37.5 us (8%)
  other arithmetic  15.8 us (3%)
    ppermute x35, waiting for transfers between devices, with_halo(): lax.ppermute(tail, axis, [(i, (i + 1) % count) for i in range(ends)])  117 us
    ppermute x35, starting transfers between devices, with_halo(): lax.ppermute(head, axis, [((i + 1) % count, i) for i in range(ends)])  91.9 us
    ppermute x35, starting transfers between devices, with_halo(): lax.ppermute(tail, axis, [(i, (i + 1) % count) for i in range(ends)])  89.4 us
    psum x1, blocking collectives, level_shift(): totals = lax.psum((totals[0], totals[1]), 'outer')  53.6 us
    all_gather x1, blocking collectives, cycle(): lax.all_gather(small_kappa, 'inner', axis=1, tiled=True)  30 us
    all_gather x1, blocking collectives, cycle(): lax.all_gather(small_source, 'inner', axis=1, tiled=True)  27.4 us
    reshape x3, local copies, waits for them, and re-layouts, restrict(): return field.reshape(a // 2, 2, b // 2, 2, c // 2, 2).mean(axis=(1, 3, 5))  20.7 us
  transfers between devices with their start and end apart: 70, of which 29 were waited for; matrix products, arithmetic and copies ran while one was open for 4% of the time, Pallas kernels for 0%

commit v1 on v0

v1 whole, which is shorter than its diff:
```python
import jax
import jax.numpy as jnp
from jax import lax
from jax.experimental import pallas as pl
from jax.experimental.pallas import tpu as pltpu
from jax.sharding import PartitionSpec as P


OMEGA = 0.8
F32 = jnp.float32
VMEM_LIMIT = 48 * 1024 * 1024


def iota(shape, dim):
    return lax.broadcasted_iota(jnp.int32, shape, dim)


def roll(x, shift, axis):
    return pltpu.roll(x, shift % x.shape[axis], axis)


def dot(a, b):
    return jnp.dot(a, b, precision=lax.Precision.HIGHEST, preferred_element_type=F32)


def lane_consts(rows, group, domain_rows=False):
    lane = iota((rows, 128), 1) % group
    zm = jnp.where(lane == group - 1, 0.0, 0.5).astype(F32)
    em = jnp.where((lane == 0) | (lane == group - 1), 0.5, 0.0).astype(F32)
    ym = None
    if domain_rows:
        row = iota((rows, 128), 0)
        ym = jnp.where(row == rows - 1, 0.0, 0.5).astype(F32)
        em = em + jnp.where((row == 0) | (row == rows - 1), 0.5, 0.0).astype(F32)
    return zm, em, ym


def make_faces(n, k, ax, ay, az, consts, inv=None, extra=None):
    zm, em, ym = consts

    def step(p, before):
        here = k[p]
        x = 0.5 * (here + k[p + 1])
        y = here + roll(here, -1, 0)
        y = 0.5 * y if ym is None else ym * y
        z = zm * (here + roll(here, -1, 1))
        ax[p] = x
        ay[p] = y
        az[p] = z
        if inv is not None:
            diag = em * here + x + before + y + roll(y, 1, 0) + z + roll(z, 1, 1)
            scaled = jnp.where(here > 0.0, OMEGA / diag, 0.0)
            inv[p] = scaled
            if extra is not None:
                extra(p, scaled)
        return x

    lax.fori_loop(0, n - 1, step, jnp.zeros(k.shape[1:], F32))


def apply_planes(first, last, v, k, ax, ay, az, consts, use, carry=None):
    em = consts[1]

    def step(p, state):
        before, carry = state
        here = v[p]
        x = ax[p] * (here - v[p + 1])
        y = ay[p] * (here - roll(here, -1, 0))
        z = az[p] * (here - roll(here, -1, 1))
        total = em * k[p] * here + (x - before) + (y - roll(y, 1, 0)) + (z - roll(z, 1, 1))
        return x, use(p, here, total, carry)

    start = ax[first - 1] * (v[first - 1] - v[first])
    return lax.fori_loop(first, last, step, (start, carry))[1]


def sweep(first, last, v, out, b, inv, k, ax, ay, az, consts):
    def use(p, here, total, _):
        out[p] = here + inv[p] * (b[p] - total)
        return 0

    apply_planes(first, last, v, k, ax, ay, az, consts, use, 0)


def ghosts(ref, n, width):
    lane = iota(ref.shape[1:], 1)
    ref[0] = jnp.where(lane < width, 0.0, roll(ref[n - 2], width, 1))
    ref[n - 1] = jnp.where(lane >= 128 - width, 0.0, roll(ref[1], -width, 1))


def pair_rows(tmp, x):
    half = x.shape[0] // 2
    tmp[...] = x
    return tmp[pl.ds(0, half, 2), :] + tmp[pl.ds(1, half, 2), :]


def twice_rows(tmp, x):
    n = x.shape[0]
    tmp[pl.ds(0, n, 2), :] = x
    tmp[pl.ds(1, n, 2), :] = x
    return tmp[...]


def gather_matrix(source, weight):
    return jnp.where(iota((128, 128), 0) == source(iota((128, 128), 1)), weight, 0.0).astype(F32)


def pair_matrix(target, weight):
    return jnp.where(iota((128, 128), 1) == target(iota((128, 128), 0)), weight, 0.0).astype(F32)


def prep_kernel(b_ref, codes_ref, low_ref, high_ref):
    kappa = jnp.exp(0.5 * codes_ref[...].astype(F32))
    low_ref[0] = kappa[:, :16]
    high_ref[0] = kappa[:, 16:]
    low_ref[1] = b_ref[:, :16]
    high_ref[1] = b_ref[:, 16:]


def fine_kernel(
    own_ref, even_ref, odd_ref,
    pay_ref, vb_ref, k1_ref, inv1_ref, k0_ref, b0_ref, v0_ref, inv0_ref,
    kb, ax, ay, az, inv, va, vb, tmp64, tmp32, s1, sk, b1, ax1, ay1, az1, va1, vb1, sems,
):
    right_first = lax.axis_index("outer") % 2 == 0

    @pl.when(right_first)
    def _():
        pltpu.make_async_copy(odd_ref, kb.at[:, pl.ds(0, 8)], sems.at[0]).start()
        pltpu.make_async_copy(even_ref, kb.at[:, pl.ds(16, 8)], sems.at[1]).start()

    @pl.when(jnp.logical_not(right_first))
    def _():
        pltpu.make_async_copy(even_ref, kb.at[:, pl.ds(0, 8)], sems.at[0]).start()
        pltpu.make_async_copy(odd_ref, kb.at[:, pl.ds(16, 8)], sems.at[1]).start()

    own = pltpu.make_async_copy(own_ref, kb.at[:, pl.ds(8, 8)], sems.at[2])
    own.start()
    pltpu.make_async_copy(odd_ref, kb.at[:, pl.ds(0, 8)], sems.at[0]).wait()
    pltpu.make_async_copy(odd_ref, kb.at[:, pl.ds(16, 8)], sems.at[1]).wait()
    own.wait()

    k, b = kb.at[0], kb.at[1]
    consts = lane_consts(64, 128)

    def first_sweep(p, scaled):
        va[p] = scaled * b[p]

    make_faces(24, k, ax, ay, az, consts, inv, first_sweep)
    sweep(2, 22, va, vb, b, inv, k, ax, ay, az, consts)

    def keep(p, _):
        k0_ref[p] = k[p + 4, pl.ds(8, 48), :]
        b0_ref[p] = b[p + 4, pl.ds(8, 48), :]
        v0_ref[p] = vb[p + 4, pl.ds(8, 48), :]
        inv0_ref[p] = inv[p + 4, pl.ds(8, 48), :]
        return 0

    lax.fori_loop(0, 16, keep, 0)

    def use(p, here, total, _):
        va[p] = b[p] - total
        return 0

    apply_planes(4, 20, vb, k, ax, ay, az, consts, use, 0)

    def coarsen_b(q, _):
        s1[pl.ds((q - 2) * 32, 32), :] = pair_rows(tmp64, va[2 * q] + va[2 * q + 1])
        return 0

    def coarsen_k(q, _):
        sk[pl.ds(q * 32, 32), :] = pair_rows(tmp64, k[2 * q] + k[2 * q + 1])
        return 0

    lax.fori_loop(2, 10, coarsen_b, 0)
    lax.fori_loop(0, 12, coarsen_k, 0)
    b1[pl.ds(2, 8)] = dot(s1[...], pair_matrix(lambda i: i // 2, 0.125)).reshape(8, 32, 128)
    k1_ref[...] = dot(sk[...], pair_matrix(lambda i: i // 2, 0.03125)).reshape(12, 32, 128)

    consts1 = lane_consts(32, 64)
    make_faces(12, k1_ref, ax1, ay1, az1, consts1, inv1_ref)
    va1[pl.ds(2, 8)] = inv1_ref[pl.ds(2, 8)] * b1[pl.ds(2, 8)]
    sweep(3, 9, va1, vb1, b1, inv1_ref, k1_ref, ax1, ay1, az1, consts1)

    def use1(p, here, total, _):
        va1[p] = b1[p] - total
        return 0

    apply_planes(4, 8, vb1, k1_ref, ax1, ay1, az1, consts1, use1, 0)
    for p in range(4):
        vb_ref[p] = vb1[4 + p] + roll(b1[4 + p], 64, 1)

    pay = jnp.zeros((16, 128), F32)
    for part, (field, weight) in enumerate(((va1, 0.125), (k1_ref, 0.03125))):
        for half in range(2):
            place = 64 * part + 32 * half
            rows = pair_rows(tmp32, field[4 + 2 * half] + field[5 + 2 * half])
            pay = pay + dot(rows, pair_matrix(lambda i: jnp.where(i < 64, place + i // 2, -1), weight))
    for i in range(32):
        pay_ref[i] = pay


def middle_kernel(
    all_ref, pay_ref, up_ref, down_ref, k_ref, inv_ref, b_ref, v_ref, ax, ay, az, va, vb, tmp16, s, sk
):
    group = iota((16, 128), 1) // 32
    for xl in range(16):
        for part, field in enumerate((b_ref, k_ref)):
            place = 2 * part + xl % 2
            plane = None
            for xh in range(4):
                block = all_ref[xl // 2 + 8 * xh]
                moved = block if xh == place else roll(block, 32 * (xh - place), 1)
                plane = moved if plane is None else jnp.where(group == xh, moved, plane)
            field[xl + 1] = plane
    ghosts(k_ref, 18, 32)
    consts = lane_consts(16, 32)
    inv_ref[0] = jnp.zeros((16, 128), F32)
    inv_ref[17] = jnp.zeros((16, 128), F32)
    b_ref[0] = jnp.zeros((16, 128), F32)
    b_ref[17] = jnp.zeros((16, 128), F32)

    def first_sweep(p, scaled):
        va[p] = scaled * b_ref[p]

    make_faces(18, k_ref, ax, ay, az, consts, inv_ref, first_sweep)
    ghosts(va, 18, 32)
    sweep(1, 17, va, v_ref, b_ref, inv_ref, k_ref, ax, ay, az, consts)
    ghosts(v_ref, 18, 32)

    def use(p, here, total, _):
        vb[p] = b_ref[p] - total
        return 0

    apply_planes(1, 17, v_ref, k_ref, ax, ay, az, consts, use, 0)
    for p in range(16):
        down_ref[p, 0:4] = v_ref[p + 1, 4:8, :]
        down_ref[p, 4:8] = b_ref[p + 1, 4:8, :]
        up_ref[p, 0:4] = v_ref[p + 1, 8:12, :]
        up_ref[p, 4:8] = b_ref[p + 1, 8:12, :]
    for t in range(8):
        s[t] = pair_rows(tmp16, vb[2 * t + 1] + vb[2 * t + 2])
        sk[t] = pair_rows(tmp16, k_ref[2 * t + 1] + k_ref[2 * t + 2])

    for part, (field, weight) in enumerate(((s, 0.125), (sk, 0.03125))):
        small = jnp.zeros((32, 128), F32)
        for u in range(2):
            m = pair_matrix(lambda i: (i // 32) * 32 + u * 16 + (i % 32) // 2, weight)
            small = small + dot(field[pl.ds(4 * u, 4)].reshape(32, 128), m)
        for t in range(4):
            vb[0, 4 * t : 4 * t + 4, :] = small[8 * t + 2 : 8 * t + 6, :]
        piece = vb[0]
        for i in range(16):
            pay_ref[i, 16 * part : 16 * part + 16, :] = piece


def coarse_kernel(
    all_ref, below_ref, above_ref, k2_ref, inv2_ref, b2_ref, v2_ref, vb1_ref, even_ref, odd_ref, k1_ref, inv1_ref,
    k0_any, b0_any, v0_any, inv0_any, v_out, r_out,
    k3, b3, ax3, ay3, az3, inv3, va3, vb3, c3, tmp16, ax2, ay2, az2, va2, vb2, b2,
    tmp32, s1, b1, va1, vb1, ax1, ay1, az1, tmp64, c1, k0, b0, v0, inv0, ax0, ay0, az0, w0, sems,
):
    outer, inner = lax.axis_index("outer"), lax.axis_index("inner")
    copies = [
        pltpu.make_async_copy(source, target, sems.at[i])
        for i, (source, target) in enumerate(((k0_any, k0), (b0_any, b0), (v0_any, v0), (inv0_any, inv0)))
    ]
    for copy in copies:
        copy.start()

    for i in range(16):
        for t in range(4):
            b3[t + 1, 4 * i : 4 * i + 4, :] = all_ref[i, 4 * t : 4 * t + 4, :]
            k3[t + 1, 4 * i : 4 * i + 4, :] = all_ref[i, 16 + 4 * t : 20 + 4 * t, :]
    ghosts(k3, 6, 16)
    b3[0] = jnp.zeros((64, 128), F32)
    consts3 = lane_consts(64, 16, True)

    def first_sweep(p, scaled):
        va3[p] = scaled * b3[p]

    make_faces(6, k3, ax3, ay3, az3, consts3, inv3, first_sweep)
    now, later = va3, vb3
    ghosts(now, 6, 16)
    for _ in range(5):
        sweep(1, 5, now, later, b3, inv3, k3, ax3, ay3, az3, consts3)
        now, later = later, now
        ghosts(now, 6, 16)

    def leftover(p, here, total, carry):
        return carry + (b3[p] - total)

    rest = apply_planes(1, 5, now, k3, ax3, ay3, az3, consts3, leftover, jnp.zeros((64, 128), F32))
    lane = iota((64, 128), 1)
    border = jnp.where(lane < 16, 0.5 * k3[1], 0.0) + jnp.where(lane >= 112, 0.5 * k3[4], 0.0)
    for p in range(1, 5):
        border = border + consts3[1] * k3[p]
    shift = jnp.sum(rest, keepdims=True) / jnp.sum(border, keepdims=True)
    for t in range(4):
        c3[t, 0:8, :] = jnp.zeros((8, 128), F32)
        c3[t, 8:72, :] = now[t + 1] + shift
        c3[t, 72:80, :] = jnp.zeros((8, 128), F32)

    near = jnp.concatenate([c3[t, pl.ds(4 * inner + 6, 8), :] for t in range(4)], axis=0)
    for u in range(2):
        wide = dot(near, gather_matrix(lambda j: (j // 32) * 32 + u * 16 + (j % 32) // 2, 1.0))
        for t in range(4):
            rows = twice_rows(tmp16, wide[8 * t : 8 * t + 8])
            for x in (2 * (4 * u + t), 2 * (4 * u + t) + 1):
                v2 = jnp.concatenate([below_ref[x, 0:4, :], v2_ref[x + 1, 4:12, :], above_ref[x, 0:4, :]], axis=0)
                b2[x + 1] = jnp.concatenate([below_ref[x, 4:8, :], b2_ref[x + 1, 4:12, :], above_ref[x, 4:8, :]], axis=0)
                va2[x + 1] = jnp.where(k2_ref[x + 1] > 0.0, v2 + rows, 0.0)
    consts2 = lane_consts(16, 32)
    make_faces(18, k2_ref, ax2, ay2, az2, consts2)
    ghosts(va2, 18, 32)
    sweep(1, 17, va2, vb2, b2, inv2_ref, k2_ref, ax2, ay2, az2, consts2)
    ghosts(vb2, 18, 32)
    sweep(1, 17, vb2, va2, b2, inv2_ref, k2_ref, ax2, ay2, az2, consts2)

    for q in range(6):
        x = lax.rem(2 * outer + 62 + q, 64)
        s1[pl.ds(16 * q, 16), :] = pltpu.roll(va2[lax.rem(x, 16) + 1], 128 - 32 * (x // 16), 1)
    wide = dot(s1[...], gather_matrix(lambda j: jnp.where(j < 64, j // 2, -1), 1.0))
    left_is_odd = outer % 2 == 0
    low = iota((32, 128), 1) < 64
    for q in range(6):
        rows = twice_rows(tmp32, wide[16 * q : 16 * q + 16])
        for p in (2 * q, 2 * q + 1):
            if p < 4:
                both = jnp.where(left_is_odd, odd_ref[p], even_ref[p])
            elif p < 8:
                both = vb1_ref[p - 4]
            else:
                both = jnp.where(left_is_odd, even_ref[p - 8], odd_ref[p - 8])
            b1[p] = roll(both, 64, 1)
            va1[p] = jnp.where(low & (k1_ref[p] > 0.0), both + rows, 0.0)
    consts1 = lane_consts(32, 64)
    make_faces(12, k1_ref, ax1, ay1, az1, consts1)
    sweep(1, 11, va1, vb1, b1, inv1_ref, k1_ref, ax1, ay1, az1, consts1)
    sweep(2, 10, vb1, va1, b1, inv1_ref, k1_ref, ax1, ay1, az1, consts1)

    c1[...] = dot(va1[pl.ds(2, 8)].reshape(256, 128), gather_matrix(lambda j: j // 2, 1.0))
    for copy in copies:
        copy.wait()

    def correct(q, _):
        twice_rows(tmp64, c1[pl.ds(32 * q, 32), :])
        rows = tmp64[pl.ds(8, 48), :]
        for p in (2 * q, 2 * q + 1):
            v0[p] = jnp.where(k0[p] > 0.0, v0[p] + rows, 0.0)
        return 0

    lax.fori_loop(0, 8, correct, 0)
    consts0 = lane_consts(48, 128)
    make_faces(16, k0, ax0, ay0, az0, consts0)
    sweep(2, 14, v0, w0, b0, inv0, k0, ax0, ay0, az0, consts0)
    sweep(3, 13, w0, v0, b0, inv0, k0, ax0, ay0, az0, consts0)

    def use(p, here, total, _):
        v_out[p - 4] = here[8:40]
        r_out[p - 4] = (b0[p] - total)[8:40]
        return 0

    apply_planes(4, 12, v0, k0, ax0, ay0, az0, consts0, use, 0)


def vmem(*shape):
    return pltpu.VMEM(shape, F32)


def out(*shape):
    return jax.ShapeDtypeStruct(shape, F32)


def call(kernel, name, ins, outs, scratch, args):
    spec = {"v": pl.BlockSpec(memory_space=pltpu.VMEM), "a": pl.BlockSpec(memory_space=pl.ANY)}
    return pl.pallas_call(
        kernel,
        name=name,
        out_shape=outs,
        in_specs=[spec[c] for c in ins],
        out_specs=[spec["v"]] * len(outs),
        scratch_shapes=scratch,
        compiler_params=pltpu.CompilerParams(vmem_limit_bytes=VMEM_LIMIT),
    )(*args)


def body(right_side, codes):
    groups, boxes = lax.axis_size("outer"), lax.axis_size("inner")
    evens = [(i, i ^ 1) for i in range(groups)]
    odds = [(i, ((i + 1) ^ 1) - 1) for i in range(1, groups - 1)]
    ups = [(i, i + 1) for i in range(boxes - 1)]
    downs = [(i + 1, i) for i in range(boxes - 1)]

    low, high = call(prep_kernel, "prep", "vv", [out(2, 8, 16, 128)] * 2, [], (right_side, codes))
    below = lax.ppermute(high, "inner", ups)
    above = lax.ppermute(low, "inner", downs)
    own = jnp.concatenate([below, low, high, above], axis=2)
    even = lax.ppermute(own, "outer", evens)
    odd = lax.ppermute(own, "outer", odds)

    fine, level1 = (24, 64, 128), (12, 32, 128)
    pay, vb1, k1, inv1, k0, b0, v0, inv0 = call(
        fine_kernel, "fine", "aaa",
        [out(32, 16, 128), out(4, 32, 128), out(*level1), out(*level1)] + [out(16, 48, 128)] * 4,
        [vmem(2, *fine)] + [vmem(*fine)] * 6 + [vmem(64, 128), vmem(32, 128), vmem(256, 128), vmem(384, 128)]
        + [vmem(*level1)] * 6 + [pltpu.SemaphoreType.DMA((3,))],
        (own, even, odd),
    )
    even1 = lax.ppermute(vb1, "outer", evens)
    odd1 = lax.ppermute(vb1, "outer", odds)
    slab = lax.all_to_all(pay, "outer", 0, 0, tiled=True)

    level2 = (18, 16, 128)
    pay3, up, down, k2, inv2, b2, v2 = call(
        middle_kernel, "middle", "v",
        [out(16, 32, 128), out(16, 8, 128), out(16, 8, 128)] + [out(*level2)] * 4,
        [vmem(*level2)] * 5 + [vmem(16, 128), vmem(8, 8, 128), vmem(8, 8, 128)],
        (slab,),
    )
    below2 = lax.ppermute(up, "inner", ups)
    above2 = lax.ppermute(down, "inner", downs)
    whole = lax.all_to_all(pay3, "inner", 0, 0, tiled=True)

    level3, window = (6, 64, 128), (16, 48, 128)
    return call(
        coarse_kernel, "coarse", "v" * 12 + "a" * 4,
        [out(8, 32, 128)] * 2,
        [vmem(*level3)] * 8 + [vmem(4, 80, 128), vmem(16, 128)] + [vmem(*level2)] * 6
        + [vmem(32, 128), vmem(96, 128)] + [vmem(*level1)] * 6 + [vmem(64, 128), vmem(256, 128)]
        + [vmem(*window)] * 8 + [pltpu.SemaphoreType.DMA((4,))],
        (whole, below2, above2, k2, inv2, b2, v2, vb1, even1, odd1, k1, inv1, k0, b0, v0, inv0),
    )


def solution(mesh):
    placed = P("outer", "inner", None)
    return jax.shard_map(
        lambda right_side, codes: tuple(body(right_side, codes)),
        mesh=mesh,
        in_specs=(placed, placed),
        out_specs=(placed, placed),
        check_vma=False,
    )
```

time: 468 us -> 119 us (0.25)
  the two profiles are of different devices: /device:TPU:134 before, /device:TPU:32 now
where the time goes in v1:
time: 119 us
  Pallas kernels  45.3 us (38%)
  starting transfers between devices  38.3 us (32%)
  blocking collectives  19.9 us (17%)
  waiting for transfers between devices  12.5 us (11%)
  local copies, waits for them, and re-layouts  1.84 us (2%)
    pallas_call x4, Pallas kernels, call(): pl.pallas_call(kernel, name=name, out_shape=outs, in_specs=[spec[c] for c...  45.3 us
    all_to_all x1, blocking collectives, body(): slab = lax.all_to_all(pay, 'outer', 0, 0, tiled=True)  19.9 us
    all_to_all x1, starting transfers between devices, body(): whole = lax.all_to_all(pay3, 'inner', 0, 0, tiled=True)  14.5 us
    ppermute x1, starting transfers between devices, body(): above = lax.ppermute(low, 'inner', downs)  4.86 us
    ppermute x1, starting transfers between devices, body(): even = lax.ppermute(own, 'outer', evens)  4.48 us
    ppermute x1, starting transfers between devices, body(): below = lax.ppermute(high, 'inner', ups)  3.83 us
    all_to_all x1, waiting for transfers between devices, body(): whole = lax.all_to_all(pay3, 'inner', 0, 0, tiled=True)  3.82 us
    ppermute x1, starting transfers between devices, body(): even1 = lax.ppermute(vb1, 'outer', evens)  3.46 us
  transfers between devices with their start and end apart: 9, of which 6 were waited for; matrix products, arithmetic and copies ran while one was open for 0% of the time, Pallas kernels for 0%

profile of v1, /device:TPU:32, one launch (start us, length us, event | category | flops | bytes accessed | tf_op | source)
XLA Modules:
  0.0 118.6 jit_solution(2353418279408446997)
XLA Ops:
  0.6 0.9 copy-done
  1.5 0.9 copy-done.1
  2.5 3.8 %collective-permute-start = (f32[2,8,16,128]{3,2,1,0:T(8,128)S(1)}, f32[2,8,16,128]{3,2,1,0:T(8,128)S(1)}, u32[]{:S(2)}, u32[]{:S(2)}) collective-permute-start(f32[2,8,16,128]{3,2,1,0:T(8,128)S(1)} %get-tuple-element.19), channel_id=1, source_target_pairs={{0,1},{1,2},{2,3},{3,4},{4,5},{5,6},{6,7},{7,8},{8,9},{9,10},{10,1... | collective-permute-start | bytes 393224 | tf_op jit(solution)/shard_map/ppermute | solution.py:396
  6.3 4.9 %collective-permute-start.1 = (f32[2,8,16,128]{3,2,1,0:T(8,128)S(1)}, f32[2,8,16,128]{3,2,1,0:T(8,128)S(1)}, u32[]{:S(2)}, u32[]{:S(2)}) collective-permute-start(f32[2,8,16,128]{3,2,1,0:T(8,128)S(1)} %get-tuple-element.20), channel_id=1, source_target_pairs={{1,0},{2,1},{3,2},{4,3},{5,4},{6,5},{7,6},{8,7},{9,8},{10,9},{11,1... | collective-permute-start | bytes 393224 | tf_op jit(solution)/shard_map/ppermute | solution.py:397
  11.2 1.0 collective-permute-done
  12.2 1.4 %collective-permute-done.1 = f32[2,8,16,128]{3,2,1,0:T(8,128)S(1)} collective-permute-done((f32[2,8,16,128]{3,2,1,0:T(8,128)S(1)}, f32[2,8,16,128]{3,2,1,0:T(8,128)S(1)}, u32[]{:S(2)}, u32[]{:S(2)}) %collective-permute-start.1) | collective-permute-done | bytes 131104 | tf_op jit(solution)/shard_map/ppermute | solution.py:397
  13.7 0.7 collective-permute-start.3
  14.4 4.5 %collective-permute-start.2 = (f32[2,8,64,128]{3,2,1,0:T(8,128)S(1)}, f32[2,8,64,128]{3,2,1,0:T(8,128)S(1)}, u32[]{:S(2)}, u32[]{:S(2)}) collective-permute-start(f32[2,8,64,128]{3,2,1,0:T(8,128)S(1)} %constant_dynamic-update-slice_fusion.own_ref), channel_id=1, source_target_pairs={{0,16},{16,0},{32,48},{48,32},{64,80},{80,64},{96,112},{112,96},{1... | collective-permute-start | bytes 1572872 | tf_op jit(solution)/shard_map/ppermute | solution.py:399
  18.9 0.0 collective-permute-done.3.odd_ref
  18.9 1.5 %collective-permute-done.2.even_ref = f32[2,8,64,128]{3,2,1,0:T(8,128)S(1)} collective-permute-done((f32[2,8,64,128]{3,2,1,0:T(8,128)S(1)}, f32[2,8,64,128]{3,2,1,0:T(8,128)S(1)}, u32[]{:S(2)}, u32[]{:S(2)}) %collective-permute-start.2) | collective-permute-done | bytes 524320 | tf_op jit(solution)/shard_map/ppermute | solution.py:399
  20.4 13.6 %fine.1 = (f32[32,16,128]{2,1,0:T(8,128)S(1)}, f32[4,32,128]{2,1,0:T(8,128)S(1)}, f32[12,32,128]{2,1,0:T(8,128)S(1)}, f32[12,32,128]{2,1,0:T(8,128)S(1)}, f32[16...) custom-call(f32[2,8,64,128]{3,2,1,0:T(8,128)S(1)} %constant_dynamic-, ...), custom_call_target="tpu_custom_call" | custom-call | tf_op jit(solution)/shard_map/fine/pallas_call | solution.py:377
  34.0 19.9 %all_to_all.10.all_ref = f32[32,16,128]{2,1,0:T(8,128)S(1)} all-to-all(f32[32,16,128]{2,1,0:T(8,128)S(1)} %get-tuple-element.21), channel_id=1, replica_groups=mesh['outer'=32,'inner'=16] {'outer'}, dimensions={0} | all-to-all | bytes 524288 | tf_op jit(solution)/shard_map/all_to_all | solution.py:412
  53.9 8.8 %middle.1 = (f32[16,32,128]{2,1,0:T(8,128)}, f32[16,8,128]{2,1,0:T(8,128)S(1)}, f32[16,8,128]{2,1,0:T(8,128)S(1)}, f32[18,16,128]{2,1,0:T(8,128)S(1)}, f32[18,16...) custom-call(f32[32,16,128]{2,1,0:T(8,128)S(1)} %all_to_all.10.all_ref), custom_call_target="tpu_custom_call" | custom-call | tf_op jit(solution)/shard_map/middle/pallas_call | solution.py:377
  62.7 14.5 %all-to-all-start.1 = ((f32[16,32,128]{2,1,0:T(8,128)}), f32[16,32,128]{2,1,0:T(8,128)S(1)}, u32[]{:S(2)}, u32[]{:S(2)}) async-start(f32[16,32,128]{2,1,0:T(8,128)} %get-tuple-element.22), calls=%async_computation.1 | async-start | bytes 524288 | tf_op jit(solution)/shard_map/all_to_all | solution.py:423
  77.2 0.7 collective-permute-start.7
  77.9 3.5 %collective-permute-start.6 = (f32[4,32,128]{2,1,0:T(8,128)S(1)}, f32[4,32,128]{2,1,0:T(8,128)S(1)}, u32[]{:S(2)}, u32[]{:S(2)}) collective-permute-start(f32[4,32,128]{2,1,0:T(8,128)S(1)} %get-tuple-element.29.vb1_ref), channel_id=1, source_target_pairs={{0,16},{16,0},{32,48},{48,32},{64,80},{80,64},{96,112},{112,96},{1... | collective-permute-start | bytes 196616 | tf_op jit(solution)/shard_map/ppermute | solution.py:410
  81.3 3.4 %collective-permute-start.4 = (f32[16,8,128]{2,1,0:T(8,128)S(1)}, f32[16,8,128]{2,1,0:T(8,128)S(1)}, u32[]{:S(2)}, u32[]{:S(2)}) collective-permute-start(f32[16,8,128]{2,1,0:T(8,128)S(1)} %get-tuple-element.23), channel_id=1, source_target_pairs={{0,1},{1,2},{2,3},{3,4},{4,5},{5,6},{6,7},{7,8},{8,9},{9,10},{10,1... | collective-permute-start | bytes 196616 | tf_op jit(solution)/shard_map/ppermute | solution.py:421
  84.7 2.5 %collective-permute-start.5 = (f32[16,8,128]{2,1,0:T(8,128)S(1)}, f32[16,8,128]{2,1,0:T(8,128)S(1)}, u32[]{:S(2)}, u32[]{:S(2)}) collective-permute-start(f32[16,8,128]{2,1,0:T(8,128)S(1)} %get-tuple-element.24), channel_id=1, source_target_pairs={{1,0},{2,1},{3,2},{4,3},{5,4},{6,5},{7,6},{8,7},{9,8},{10,9},{11,1... | collective-permute-start | bytes 196616 | tf_op jit(solution)/shard_map/ppermute | solution.py:422
  87.2 0.0 collective-permute-done.7.odd_ref
  87.2 0.0 collective-permute-done.6.even_ref
  87.2 2.5 %collective-permute-done.4.below_ref = f32[16,8,128]{2,1,0:T(8,128)S(1)} collective-permute-done((f32[16,8,128]{2,1,0:T(8,128)S(1)}, f32[16,8,128]{2,1,0:T(8,128)S(1)}, u32[]{:S(2)}, u32[]{:S(2)}) %collective-permute-start.4) | collective-permute-done | bytes 65568 | tf_op jit(solution)/shard_map/ppermute | solution.py:421
  89.7 2.2 %collective-permute-done.5.above_ref = f32[16,8,128]{2,1,0:T(8,128)S(1)} collective-permute-done((f32[16,8,128]{2,1,0:T(8,128)S(1)}, f32[16,8,128]{2,1,0:T(8,128)S(1)}, u32[]{:S(2)}, u32[]{:S(2)}) %collective-permute-start.5) | collective-permute-done | bytes 65568 | tf_op jit(solution)/shard_map/ppermute | solution.py:422
  91.9 3.8 %all-to-all-done.1.all_ref = f32[16,32,128]{2,1,0:T(8,128)S(1)} async-done(((f32[16,32,128]{2,1,0:T(8,128)}), f32[16,32,128]{2,1,0:T(8,128)S(1)}, u32[]{:S(2)}, u32[]{:S(2)}) %all-to-all-start.1) | async-done | bytes 262176 | tf_op jit(solution)/shard_map/all_to_all | solution.py:423
  95.7 22.9 %coarse.1 = (f32[8,32,128]{2,1,0:T(8,128)}, f32[8,32,128]{2,1,0:T(8,128)}) custom-call(f32[16,32,128]{2,1,0:T(8,128)S(1)} %all-to-all-done.1.all_ref, f32[16,8,128]{2,1,0:T(8,128)S(1)} %collective-permute-done.4.below_ref, f32[16,8,128]{2,1,0:T(8,128)S(1)} %collective-permute-done.5.above_ref, f32[18,16,128]{2,1,0:T(8,128)S(1)} %get-tuple-element.25.k2_ref, ...), custom_call_target="tpu_custom_call" | custom-call | tf_op jit(solution)/shard_map/coarse/pallas_call | solution.py:377
  (7 shorter events, 0.1 us)
Async XLA Ops:
  0.6 0.9 copy-start
  1.5 0.9 copy-start.1
  2.5 9.7 %collective-permute-start = (f32[2,8,16,128]{3,2,1,0:T(8,128)S(1)}, f32[2,8,16,128]{3,2,1,0:T(8,128)S(1)}, u32[]{:S(2)}, u32[]{:S(2)}) collective-permute-start(f32[2,8,16,128]{3,2,1,0:T(8,128)S(1)} %get-tuple-element.19), channel_id=1, source_target_pairs={{0,1},{1,2},{2,3},{3,4},{4,5},{5,6},{6,7},{7,8},{8,9},{9,10},{10,1... | collective-permute-start | bytes 393224 | tf_op jit(solution)/shard_map/ppermute | solution.py:396
  6.3 7.4 %collective-permute-start.1 = (f32[2,8,16,128]{3,2,1,0:T(8,128)S(1)}, f32[2,8,16,128]{3,2,1,0:T(8,128)S(1)}, u32[]{:S(2)}, u32[]{:S(2)}) collective-permute-start(f32[2,8,16,128]{3,2,1,0:T(8,128)S(1)} %get-tuple-element.20), channel_id=1, source_target_pairs={{1,0},{2,1},{3,2},{4,3},{5,4},{6,5},{7,6},{8,7},{9,8},{10,9},{11,1... | collective-permute-start | bytes 393224 | tf_op jit(solution)/shard_map/ppermute | solution.py:397
  13.7 5.2 %collective-permute-start.3 = (f32[2,8,64,128]{3,2,1,0:T(8,128)S(1)}, f32[2,8,64,128]{3,2,1,0:T(8,128)S(1)}, u32[]{:S(2)}, u32[]{:S(2)}) collective-permute-start(f32[2,8,64,128]{3,2,1,0:T(8,128)S(1)} %constant_dynamic-update-slice_fusion.own_ref), channel_id=1, source_target_pairs={{16,32},{32,16},{48,64},{64,48},{80,96},{96,80},{112,128},{128,112... | collective-permute-start | bytes 1572872 | tf_op jit(solution)/shard_map/ppermute | solution.py:400
  14.4 6.0 %collective-permute-start.2 = (f32[2,8,64,128]{3,2,1,0:T(8,128)S(1)}, f32[2,8,64,128]{3,2,1,0:T(8,128)S(1)}, u32[]{:S(2)}, u32[]{:S(2)}) collective-permute-start(f32[2,8,64,128]{3,2,1,0:T(8,128)S(1)} %constant_dynamic-update-slice_fusion.own_ref), channel_id=1, source_target_pairs={{0,16},{16,0},{32,48},{48,32},{64,80},{80,64},{96,112},{112,96},{1... | collective-permute-start | bytes 1572872 | tf_op jit(solution)/shard_map/ppermute | solution.py:399
  62.7 33.1 %all-to-all-start.1 = ((f32[16,32,128]{2,1,0:T(8,128)}), f32[16,32,128]{2,1,0:T(8,128)S(1)}, u32[]{:S(2)}, u32[]{:S(2)}) async-start(f32[16,32,128]{2,1,0:T(8,128)} %get-tuple-element.22), calls=%async_computation.1 | async-start | bytes 524288 | tf_op jit(solution)/shard_map/all_to_all | solution.py:423
  77.2 10.0 %collective-permute-start.7 = (f32[4,32,128]{2,1,0:T(8,128)S(1)}, f32[4,32,128]{2,1,0:T(8,128)S(1)}, u32[]{:S(2)}, u32[]{:S(2)}) collective-permute-start(f32[4,32,128]{2,1,0:T(8,128)S(1)} %get-tuple-element.29.vb1_ref), channel_id=1, source_target_pairs={{16,32},{32,16},{48,64},{64,48},{80,96},{96,80},{112,128},{128,112... | collective-permute-start | bytes 196616 | tf_op jit(solution)/shard_map/ppermute | solution.py:411
  77.9 9.3 %collective-permute-start.6 = (f32[4,32,128]{2,1,0:T(8,128)S(1)}, f32[4,32,128]{2,1,0:T(8,128)S(1)}, u32[]{:S(2)}, u32[]{:S(2)}) collective-permute-start(f32[4,32,128]{2,1,0:T(8,128)S(1)} %get-tuple-element.29.vb1_ref), channel_id=1, source_target_pairs={{0,16},{16,0},{32,48},{48,32},{64,80},{80,64},{96,112},{112,96},{1... | collective-permute-start | bytes 196616 | tf_op jit(solution)/shard_map/ppermute | solution.py:410
  81.3 8.4 %collective-permute-start.4 = (f32[16,8,128]{2,1,0:T(8,128)S(1)}, f32[16,8,128]{2,1,0:T(8,128)S(1)}, u32[]{:S(2)}, u32[]{:S(2)}) collective-permute-start(f32[16,8,128]{2,1,0:T(8,128)S(1)} %get-tuple-element.23), channel_id=1, source_target_pairs={{0,1},{1,2},{2,3},{3,4},{4,5},{5,6},{6,7},{7,8},{8,9},{9,10},{10,1... | collective-permute-start | bytes 196616 | tf_op jit(solution)/shard_map/ppermute | solution.py:421
  84.7 7.2 %collective-permute-start.5 = (f32[16,8,128]{2,1,0:T(8,128)S(1)}, f32[16,8,128]{2,1,0:T(8,128)S(1)}, u32[]{:S(2)}, u32[]{:S(2)}) collective-permute-start(f32[16,8,128]{2,1,0:T(8,128)S(1)} %get-tuple-element.24), channel_id=1, source_target_pairs={{1,0},{2,1},{3,2},{4,3},{5,4},{6,5},{7,6},{8,7},{9,8},{10,9},{11,1... | collective-permute-start | bytes 196616 | tf_op jit(solution)/shard_map/ppermute | solution.py:422

commit v2 on v1

--- a/solution.py
+++ b/solution.py
@@ -8,7 +8,8 @@
 
 OMEGA = 0.8
 F32 = jnp.float32
-VMEM_LIMIT = 48 * 1024 * 1024
+VMEM_LIMIT = 24 * 1024 * 1024
+UNROLL = 96
 
 
 def iota(shape, dim):
@@ -33,6 +34,25 @@
         ym = jnp.where(row == rows - 1, 0.0, 0.5).astype(F32)
         em = em + jnp.where((row == 0) | (row == rows - 1), 0.5, 0.0).astype(F32)
     return zm, em, ym
+
+
+def loop(first, last, rows, step, carry):
+    count = last - first
+    width = max(1, min(count, UNROLL // (rows // 8)))
+    whole = count // width
+
+    def block(i, carry):
+        for u in range(width):
+            carry = step(first + i * width + u, carry)
+        return carry
+
+    if whole == 1:
+        carry = block(0, carry)
+    else:
+        carry = lax.fori_loop(0, whole, block, carry)
+    for p in range(first + whole * width, last):
+        carry = step(p, carry)
+    return carry
 
 
 def make_faces(n, k, ax, ay, az, consts, inv=None, extra=None):
@@ -55,7 +75,7 @@
                 extra(p, scaled)
         return x
 
-    lax.fori_loop(0, n - 1, step, jnp.zeros(k.shape[1:], F32))
+    loop(0, n - 1, k.shape[1], step, jnp.zeros(k.shape[1:], F32))
 
 
 def apply_planes(first, last, v, k, ax, ay, az, consts, use, carry=None):
@@ -71,7 +91,7 @@
         return x, use(p, here, total, carry)
 
     start = ax[first - 1] * (v[first - 1] - v[first])
-    return lax.fori_loop(first, last, step, (start, carry))[1]
+    return loop(first, last, v.shape[1], step, (start, carry))[1]
 
 
 def sweep(first, last, v, out, b, inv, k, ax, ay, az, consts):
@@ -156,7 +176,7 @@
         inv0_ref[p] = inv[p + 4, pl.ds(8, 48), :]
         return 0
 
-    lax.fori_loop(0, 16, keep, 0)
+    loop(0, 16, 32, keep, 0)
 
     def use(p, here, total, _):
         va[p] = b[p] - total
@@ -172,8 +192,8 @@
         sk[pl.ds(q * 32, 32), :] = pair_rows(tmp64, k[2 * q] + k[2 * q + 1])
         return 0
 
-    lax.fori_loop(2, 10, coarsen_b, 0)
-    lax.fori_loop(0, 12, coarsen_k, 0)
+    loop(2, 10, 64, coarsen_b, 0)
+    loop(0, 12, 64, coarsen_k, 0)
     b1[pl.ds(2, 8)] = dot(s1[...], pair_matrix(lambda i: i // 2, 0.125)).reshape(8, 32, 128)
     k1_ref[...] = dot(sk[...], pair_matrix(lambda i: i // 2, 0.03125)).reshape(12, 32, 128)
 
@@ -201,7 +221,8 @@
 
 
 def middle_kernel(
-    all_ref, pay_ref, up_ref, down_ref, k_ref, inv_ref, b_ref, v_ref, ax, ay, az, va, vb, tmp16, s, sk
+    all_ref, _even1, _odd1, pay_ref, up_ref, down_ref, kw_ref, invw_ref, bw_ref, vw_ref,
+    k_ref, inv_ref, b_ref, v_ref, ax, ay, az, va, vb, tmp16, s, sk,
 ):
     group = iota((16, 128), 1) // 32
     for xl in range(16):
@@ -233,11 +254,20 @@
         return 0
 
     apply_planes(1, 17, v_ref, k_ref, ax, ay, az, consts, use, 0)
-    for p in range(16):
-        down_ref[p, 0:4] = v_ref[p + 1, 4:8, :]
-        down_ref[p, 4:8] = b_ref[p + 1, 4:8, :]
-        up_ref[p, 0:4] = v_ref[p + 1, 8:12, :]
-        up_ref[p, 4:8] = b_ref[p + 1, 8:12, :]
+    first = 2 * lax.axis_index("outer") + 60
+    near = []
+    for q in range(10):
+        x = lax.rem(first + q, 64)
+        place = lax.rem(x, 16) + 1
+        back = lax.rem(128 - 32 * (x // 16), 128)
+        kept = (group == 0) & (first + q >= 64) & (first + q < 128)
+        for field, window in ((k_ref, kw_ref), (inv_ref, invw_ref), (b_ref, bw_ref), (v_ref, vw_ref)):
+            window[q] = jnp.where(kept, pltpu.roll(field[place], back, 1), 0.0)
+        near.append(vw_ref[q] + roll(bw_ref[q], 32, 1))
+    for q in range(5):
+        both = near[q] + roll(near[q + 5], 64, 1)
+        down_ref[4 * q : 4 * q + 4, :] = both[4:8]
+        up_ref[4 * q : 4 * q + 4, :] = both[8:12]
     for t in range(8):
         s[t] = pair_rows(tmp16, vb[2 * t + 1] + vb[2 * t + 2])
         sk[t] = pair_rows(tmp16, k_ref[2 * t + 1] + k_ref[2 * t + 2])
@@ -256,18 +286,11 @@
 
 def coarse_kernel(
     all_ref, below_ref, above_ref, k2_ref, inv2_ref, b2_ref, v2_ref, vb1_ref, even_ref, odd_ref, k1_ref, inv1_ref,
-    k0_any, b0_any, v0_any, inv0_any, v_out, r_out,
+    k0, b0, v0_ref, inv0, v_out, r_out,
     k3, b3, ax3, ay3, az3, inv3, va3, vb3, c3, tmp16, ax2, ay2, az2, va2, vb2, b2,
-    tmp32, s1, b1, va1, vb1, ax1, ay1, az1, tmp64, c1, k0, b0, v0, inv0, ax0, ay0, az0, w0, sems,
+    tmp32, b1, va1, vb1, ax1, ay1, az1, tmp64, c1, v0, ax0, ay0, az0, w0,
 ):
     outer, inner = lax.axis_index("outer"), lax.axis_index("inner")
-    copies = [
-        pltpu.make_async_copy(source, target, sems.at[i])
-        for i, (source, target) in enumerate(((k0_any, k0), (b0_any, b0), (v0_any, v0), (inv0_any, inv0)))
-    ]
-    for copy in copies:
-        copy.start()
-
     for i in range(16):
         for t in range(4):
             b3[t + 1, 4 * i : 4 * i + 4, :] = all_ref[i, 4 * t : 4 * t + 4, :]
@@ -301,26 +324,27 @@
         c3[t, 8:72, :] = now[t + 1] + shift
         c3[t, 72:80, :] = jnp.zeros((8, 128), F32)
 
-    near = jnp.concatenate([c3[t, pl.ds(4 * inner + 6, 8), :] for t in range(4)], axis=0)
-    for u in range(2):
-        wide = dot(near, gather_matrix(lambda j: (j // 32) * 32 + u * 16 + (j % 32) // 2, 1.0))
-        for t in range(4):
-            rows = twice_rows(tmp16, wide[8 * t : 8 * t + 8])
-            for x in (2 * (4 * u + t), 2 * (4 * u + t) + 1):
-                v2 = jnp.concatenate([below_ref[x, 0:4, :], v2_ref[x + 1, 4:12, :], above_ref[x, 0:4, :]], axis=0)
-                b2[x + 1] = jnp.concatenate([below_ref[x, 4:8, :], b2_ref[x + 1, 4:12, :], above_ref[x, 4:8, :]], axis=0)
-                va2[x + 1] = jnp.where(k2_ref[x + 1] > 0.0, v2 + rows, 0.0)
+    near = []
+    for q in range(5):
+        x = lax.rem(outer + 30 + q, 32)
+        back = lax.rem(128 - 16 * (x // 4), 128)
+        near.append(pltpu.roll(c3[lax.rem(x, 4), pl.ds(4 * inner + 6, 8), :], back, 1))
+    wide = dot(jnp.concatenate(near, axis=0), gather_matrix(lambda j: jnp.where(j < 32, j // 2, -1), 1.0))
+    lane = iota((16, 128), 1)
+    for q in range(10):
+        rows = twice_rows(tmp16, wide[8 * (q // 2) : 8 * (q // 2) + 8])
+        below, above = (ref[4 * (q % 5) : 4 * (q % 5) + 4, :] for ref in (below_ref, above_ref))
+        if q >= 5:
+            below, above = roll(below, 64, 1), roll(above, 64, 1)
+        v2 = jnp.concatenate([below, v2_ref[q, 4:12, :], above], axis=0)
+        b2[q] = jnp.concatenate([roll(below, 96, 1), b2_ref[q, 4:12, :], roll(above, 96, 1)], axis=0)
+        va2[q] = jnp.where((lane < 32) & (k2_ref[q] > 0.0), v2 + rows, 0.0)
     consts2 = lane_consts(16, 32)
-    make_faces(18, k2_ref, ax2, ay2, az2, consts2)
-    ghosts(va2, 18, 32)
-    sweep(1, 17, va2, vb2, b2, inv2_ref, k2_ref, ax2, ay2, az2, consts2)
-    ghosts(vb2, 18, 32)
-    sweep(1, 17, vb2, va2, b2, inv2_ref, k2_ref, ax2, ay2, az2, consts2)
-
-    for q in range(6):
-        x = lax.rem(2 * outer + 62 + q, 64)
-        s1[pl.ds(16 * q, 16), :] = pltpu.roll(va2[lax.rem(x, 16) + 1], 128 - 32 * (x // 16), 1)
-    wide = dot(s1[...], gather_matrix(lambda j: jnp.where(j < 64, j // 2, -1), 1.0))
+    make_faces(10, k2_ref, ax2, ay2, az2, consts2)
+    sweep(1, 9, va2, vb2, b2, inv2_ref, k2_ref, ax2, ay2, az2, consts2)
+    sweep(2, 8, vb2, va2, b2, inv2_ref, k2_ref, ax2, ay2, az2, consts2)
+
+    wide = dot(va2[pl.ds(2, 6)].reshape(96, 128), gather_matrix(lambda j: jnp.where(j < 64, j // 2, -1), 1.0))
     left_is_odd = outer % 2 == 0
     low = iota((32, 128), 1) < 64
     for q in range(6):
@@ -340,17 +364,15 @@
     sweep(2, 10, vb1, va1, b1, inv1_ref, k1_ref, ax1, ay1, az1, consts1)
 
     c1[...] = dot(va1[pl.ds(2, 8)].reshape(256, 128), gather_matrix(lambda j: j // 2, 1.0))
-    for copy in copies:
-        copy.wait()
 
     def correct(q, _):
         twice_rows(tmp64, c1[pl.ds(32 * q, 32), :])
         rows = tmp64[pl.ds(8, 48), :]
         for p in (2 * q, 2 * q + 1):
-            v0[p] = jnp.where(k0[p] > 0.0, v0[p] + rows, 0.0)
-        return 0
-
-    lax.fori_loop(0, 8, correct, 0)
+            v0[p] = jnp.where(k0[p] > 0.0, v0_ref[p] + rows, 0.0)
+        return 0
+
+    loop(0, 8, 64, correct, 0)
     consts0 = lane_consts(48, 128)
     make_faces(16, k0, ax0, ay0, az0, consts0)
     sweep(2, 14, v0, w0, b0, inv0, k0, ax0, ay0, az0, consts0)
@@ -411,12 +433,12 @@
     odd1 = lax.ppermute(vb1, "outer", odds)
     slab = lax.all_to_all(pay, "outer", 0, 0, tiled=True)
 
-    level2 = (18, 16, 128)
+    level2, window2 = (18, 16, 128), (10, 16, 128)
     pay3, up, down, k2, inv2, b2, v2 = call(
-        middle_kernel, "middle", "v",
-        [out(16, 32, 128), out(16, 8, 128), out(16, 8, 128)] + [out(*level2)] * 4,
-        [vmem(*level2)] * 5 + [vmem(16, 128), vmem(8, 8, 128), vmem(8, 8, 128)],
-        (slab,),
+        middle_kernel, "middle", "vaa",
+        [out(16, 32, 128), out(24, 128), out(24, 128)] + [out(*window2)] * 4,
+        [vmem(*level2)] * 9 + [vmem(16, 128), vmem(8, 8, 128), vmem(8, 8, 128)],
+        (slab, even1, odd1),
     )
     below2 = lax.ppermute(up, "inner", ups)
     above2 = lax.ppermute(down, "inner", downs)
@@ -424,11 +446,11 @@
 
     level3, window = (6, 64, 128), (16, 48, 128)
     return call(
-        coarse_kernel, "coarse", "v" * 12 + "a" * 4,
+        coarse_kernel, "coarse", "v" * 16,
         [out(8, 32, 128)] * 2,
-        [vmem(*level3)] * 8 + [vmem(4, 80, 128), vmem(16, 128)] + [vmem(*level2)] * 6
-        + [vmem(32, 128), vmem(96, 128)] + [vmem(*level1)] * 6 + [vmem(64, 128), vmem(256, 128)]
-        + [vmem(*window)] * 8 + [pltpu.SemaphoreType.DMA((4,))],
+        [vmem(*level3)] * 8 + [vmem(4, 80, 128), vmem(16, 128)] + [vmem(*window2)] * 6
+        + [vmem(32, 128)] + [vmem(*level1)] * 6 + [vmem(64, 128), vmem(256, 128)]
+        + [vmem(*window)] * 5,
         (whole, below2, above2, k2, inv2, b2, v2, vb1, even1, odd1, k1, inv1, k0, b0, v0, inv0),
     )
 

time: 119 us -> 84.1 us (0.71)
  the two profiles are of different devices: /device:TPU:32 before, /device:TPU:24 now
where the time goes in v2:
time: 84.1 us; the launch traced here: 83.5 us
  starting transfers between devices  42.9 us (51%)
  waiting for transfers between devices  28.6 us (34%)
  Pallas kernels  9.41 us (11%)
  local copies, waits for them, and re-layouts  1.84 us (2%)
    all_to_all x1, starting transfers between devices, body(): whole = lax.all_to_all(pay3, 'inner', 0, 0, tiled=True)  14.5 us
    pallas_call x4, Pallas kernels, call(): pl.pallas_call(kernel, name=name, out_shape=outs, in_specs=[spec[c] for c...  9.41 us
    all_to_all x1, starting transfers between devices, body(): slab = lax.all_to_all(pay, 'outer', 0, 0, tiled=True)  7.69 us
    ppermute x1, waiting for transfers between devices, body(): above2 = lax.ppermute(down, 'inner', downs)  7.23 us
    all_to_all x1, waiting for transfers between devices, body(): whole = lax.all_to_all(pay3, 'inner', 0, 0, tiled=True)  7.1 us
    ppermute x1, waiting for transfers between devices, body(): odd = lax.ppermute(own, 'outer', odds)  5.4 us
    ppermute x1, waiting for transfers between devices, body(): above = lax.ppermute(low, 'inner', downs)  4.25 us
    ppermute x1, starting transfers between devices, body(): below2 = lax.ppermute(up, 'inner', ups)  3.83 us
  transfers between devices with their start and end apart: 10, of which 8 were waited for; matrix products, arithmetic and copies ran while one was open for 0% of the time, Pallas kernels for 0%

profile of v2, /device:TPU:24, one launch (start us, length us, event | category | flops | bytes accessed | tf_op | source)
XLA Modules:
  0.0 83.5 jit_solution(8565206679956553520)
XLA Ops:
  0.6 0.9 %copy-done = f32[8,32,128]{2,1,0:T(8,128)S(1)} copy-done((f32[8,32,128]{2,1,0:T(8,128)S(1)}, f32[8,32,128]{2,1,0:T(8,128)}, u32[]{:S(2)}) %copy-start) | copy-done | bytes 131096
  1.5 0.9 %copy-done.1 = s32[8,32,128]{2,1,0:T(8,128)S(1)} copy-done((s32[8,32,128]{2,1,0:T(8,128)S(1)}, s32[8,32,128]{2,1,0:T(8,128)}, u32[]{:S(2)}) %copy-start.1) | copy-done | bytes 131096
  2.5 3.8 %collective-permute-start = (f32[2,8,16,128]{3,2,1,0:T(8,128)S(1)}, f32[2,8,16,128]{3,2,1,0:T(8,128)S(1)}, u32[]{:S(2)}, u32[]{:S(2)}) collective-permute-start(f32[2,8,16,128]{3,2,1,0:T(8,128)S(1)} %get-tuple-element.19), channel_id=1, source_target_pairs={{0,1},{1,2},{2,3},{3,4},{4,5},{5,6},{6,7},{7,8},{8,9},{9,10},{10,1... | collective-permute-start | bytes 393224 | tf_op jit(solution)/shard_map/ppermute | solution.py:418
  6.3 1.3 %collective-permute-start.1 = (f32[2,8,16,128]{3,2,1,0:T(8,128)S(1)}, f32[2,8,16,128]{3,2,1,0:T(8,128)S(1)}, u32[]{:S(2)}, u32[]{:S(2)}) collective-permute-start(f32[2,8,16,128]{3,2,1,0:T(8,128)S(1)} %get-tuple-element.20), channel_id=1, source_target_pairs={{1,0},{2,1},{3,2},{4,3},{5,4},{6,5},{7,6},{8,7},{9,8},{10,9},{11,1... | collective-permute-start | bytes 393224 | tf_op jit(solution)/shard_map/ppermute | solution.py:419
  7.6 1.4 %collective-permute-done = f32[2,8,16,128]{3,2,1,0:T(8,128)S(1)} collective-permute-done((f32[2,8,16,128]{3,2,1,0:T(8,128)S(1)}, f32[2,8,16,128]{3,2,1,0:T(8,128)S(1)}, u32[]{:S(2)}, u32[]{:S(2)}) %collective-permute-start) | collective-permute-done | bytes 131104 | tf_op jit(solution)/shard_map/ppermute | solution.py:418
  9.1 4.2 %collective-permute-done.1 = f32[2,8,16,128]{3,2,1,0:T(8,128)S(1)} collective-permute-done((f32[2,8,16,128]{3,2,1,0:T(8,128)S(1)}, f32[2,8,16,128]{3,2,1,0:T(8,128)S(1)}, u32[]{:S(2)}, u32[]{:S(2)}) %collective-permute-start.1) | collective-permute-done | bytes 131104 | tf_op jit(solution)/shard_map/ppermute | solution.py:419
  13.4 1.9 %collective-permute-start.3 = (f32[2,8,64,128]{3,2,1,0:T(8,128)S(1)}, f32[2,8,64,128]{3,2,1,0:T(8,128)S(1)}, u32[]{:S(2)}, u32[]{:S(2)}) collective-permute-start(f32[2,8,64,128]{3,2,1,0:T(8,128)S(1)} %constant_dynamic-update-slice_fusion.own_ref), channel_id=1, source_target_pairs={{16,32},{32,16},{48,64},{64,48},{80,96},{96,80},{112,128},{128,112... | collective-permute-start | bytes 1572872 | tf_op jit(solution)/shard_map/ppermute | solution.py:422
  15.3 3.2 %collective-permute-start.2 = (f32[2,8,64,128]{3,2,1,0:T(8,128)S(1)}, f32[2,8,64,128]{3,2,1,0:T(8,128)S(1)}, u32[]{:S(2)}, u32[]{:S(2)}) collective-permute-start(f32[2,8,64,128]{3,2,1,0:T(8,128)S(1)} %constant_dynamic-update-slice_fusion.own_ref), channel_id=1, source_target_pairs={{0,16},{16,0},{32,48},{48,32},{64,80},{80,64},{96,112},{112,96},{1... | collective-permute-start | bytes 1572872 | tf_op jit(solution)/shard_map/ppermute | solution.py:421
  18.4 5.4 %collective-permute-done.3.odd_ref = f32[2,8,64,128]{3,2,1,0:T(8,128)S(1)} collective-permute-done((f32[2,8,64,128]{3,2,1,0:T(8,128)S(1)}, f32[2,8,64,128]{3,2,1,0:T(8,128)S(1)}, u32[]{:S(2)}, u32[]{:S(2)}) %collective-permute-start.3) | collective-permute-done | bytes 524320 | tf_op jit(solution)/shard_map/ppermute | solution.py:422
  23.9 3.6 %fine.1 = (f32[32,16,128]{2,1,0:T(8,128)}, f32[4,32,128]{2,1,0:T(8,128)S(1)}, f32[12,32,128]{2,1,0:T(8,128)S(1)}, f32[12,32,128]{2,1,0:T(8,128)S(1)}, f32[16,48,...) custom-call(f32[2,8,64,128]{3,2,1,0:T(8,128)S(1)} %constant_dynamic-upda, ...), custom_call_target="tpu_custom_call" | custom-call | tf_op jit(solution)/shard_map/fine/pallas_call | solution.py:399
  27.5 7.7 %all-to-all-start = ((f32[32,16,128]{2,1,0:T(8,128)}), f32[32,16,128]{2,1,0:T(8,128)S(1)}, u32[]{:S(2)}, u32[]{:S(2)}) async-start(f32[32,16,128]{2,1,0:T(8,128)} %get-tuple-element.21), calls=%async_computation | async-start | bytes 524288 | tf_op jit(solution)/shard_map/all_to_all | solution.py:434
  35.2 2.5 %collective-permute-start.5 = (f32[4,32,128]{2,1,0:T(8,128)S(1)}, f32[4,32,128]{2,1,0:T(8,128)S(1)}, u32[]{:S(2)}, u32[]{:S(2)}) collective-permute-start(f32[4,32,128]{2,1,0:T(8,128)S(1)} %get-tuple-element.22.vb1_ref), channel_id=1, source_target_pairs={{16,32},{32,16},{48,64},{64,48},{80,96},{96,80},{112,128},{128,112... | collective-permute-start | bytes 196616 | tf_op jit(solution)/shard_map/ppermute | solution.py:433
  37.7 2.9 %collective-permute-start.4 = (f32[4,32,128]{2,1,0:T(8,128)S(1)}, f32[4,32,128]{2,1,0:T(8,128)S(1)}, u32[]{:S(2)}, u32[]{:S(2)}) collective-permute-start(f32[4,32,128]{2,1,0:T(8,128)S(1)} %get-tuple-element.22.vb1_ref), channel_id=1, source_target_pairs={{0,16},{16,0},{32,48},{48,32},{64,80},{80,64},{96,112},{112,96},{1... | collective-permute-start | bytes 196616 | tf_op jit(solution)/shard_map/ppermute | solution.py:432
  40.6 1.3 %collective-permute-done.5._odd1.odd_ref = f32[4,32,128]{2,1,0:T(8,128)S(1)} collective-permute-done((f32[4,32,128]{2,1,0:T(8,128)S(1)}, f32[4,32,128]{2,1,0:T(8,128)S(1)}, u32[]{:S(2)}, u32[]{:S(2)}) %collective-permute-start.5) | collective-permute-done | bytes 65568 | tf_op jit(solution)/shard_map/ppermute | solution.py:433
  41.9 0.0 collective-permute-done.4._even1.even_ref
  41.9 0.3 all-to-all-done.all_ref
  42.2 1.8 %middle.1 = (f32[16,32,128]{2,1,0:T(8,128)}, f32[24,128]{1,0:T(8,128)S(1)}, f32[24,128]{1,0:T(8,128)S(1)}, f32[10,16,128]{2,1,0:T(8,128)S(1)}, f32[10,16,128]{2,...) custom-call(f32[32,16,128]{2,1,0:T(8,128)S(1)} %all-to-all-done.all_ref, ...), custom_call_target="tpu_custom_call" | custom-call | tf_op jit(solution)/shard_map/middle/pallas_call | solution.py:399
  44.0 14.5 %all-to-all-start.1 = ((f32[16,32,128]{2,1,0:T(8,128)}), f32[16,32,128]{2,1,0:T(8,128)S(1)}, u32[]{:S(2)}, u32[]{:S(2)}) async-start(f32[16,32,128]{2,1,0:T(8,128)} %get-tuple-element.23), calls=%async_computation.1 | async-start | bytes 524288 | tf_op jit(solution)/shard_map/all_to_all | solution.py:445
  58.6 3.8 %collective-permute-start.6 = (f32[24,128]{1,0:T(8,128)S(1)}, f32[24,128]{1,0:T(8,128)S(1)}, u32[]{:S(2)}, u32[]{:S(2)}) collective-permute-start(f32[24,128]{1,0:T(8,128)S(1)} %get-tuple-element.24), channel_id=1, source_target_pairs={{0,1},{1,2},{2,3},{3,4},{4,5},{5,6},{6,7},{7,8},{8,9},{9,10},{10,1... | collective-permute-start | bytes 36872 | tf_op jit(solution)/shard_map/ppermute | solution.py:443
  62.4 1.3 %collective-permute-start.7 = (f32[24,128]{1,0:T(8,128)S(1)}, f32[24,128]{1,0:T(8,128)S(1)}, u32[]{:S(2)}, u32[]{:S(2)}) collective-permute-start(f32[24,128]{1,0:T(8,128)S(1)} %get-tuple-element.25), channel_id=1, source_target_pairs={{1,0},{2,1},{3,2},{4,3},{5,4},{6,5},{7,6},{8,7},{9,8},{10,9},{11,1... | collective-permute-start | bytes 36872 | tf_op jit(solution)/shard_map/ppermute | solution.py:444
  63.7 1.6 %collective-permute-done.6.below_ref = f32[24,128]{1,0:T(8,128)S(1)} collective-permute-done((f32[24,128]{1,0:T(8,128)S(1)}, f32[24,128]{1,0:T(8,128)S(1)}, u32[]{:S(2)}, u32[]{:S(2)}) %collective-permute-start.6) | collective-permute-done | bytes 12320 | tf_op jit(solution)/shard_map/ppermute | solution.py:443
  65.3 7.2 %collective-permute-done.7.above_ref = f32[24,128]{1,0:T(8,128)S(1)} collective-permute-done((f32[24,128]{1,0:T(8,128)S(1)}, f32[24,128]{1,0:T(8,128)S(1)}, u32[]{:S(2)}, u32[]{:S(2)}) %collective-permute-start.7) | collective-permute-done | bytes 12320 | tf_op jit(solution)/shard_map/ppermute | solution.py:444
  72.5 7.1 %all-to-all-done.1.all_ref = f32[16,32,128]{2,1,0:T(8,128)S(1)} async-done(((f32[16,32,128]{2,1,0:T(8,128)}), f32[16,32,128]{2,1,0:T(8,128)S(1)}, u32[]{:S(2)}, u32[]{:S(2)}) %all-to-all-start.1) | async-done | bytes 262176 | tf_op jit(solution)/shard_map/all_to_all | solution.py:445
  79.6 3.9 %coarse.1 = (f32[8,32,128]{2,1,0:T(8,128)}, f32[8,32,128]{2,1,0:T(8,128)}) custom-call(f32[16,32,128]{2,1,0:T(8,128)S(1)} %all-to-all-done.1.all_ref, f32[24,128]{1,0:T(8,128)S(1)} %collective-permute-done.6.below_ref, f32[24,128]{1,0:T(8,128)S(1)} %collective-permute-done.7.above_ref, f32[10,16,128]{2,1,0:T(8,128)S(1)} %get-tuple-element.26.k2_ref, ...), custom_call_target="tpu_custom_call" | custom-call | tf_op jit(solution)/shard_map/coarse/pallas_call | solution.py:399
  (8 shorter events, 0.1 us)
Async XLA Ops:
  0.6 0.9 %copy-start = (f32[8,32,128]{2,1,0:T(8,128)S(1)}, f32[8,32,128]{2,1,0:T(8,128)}, u32[]{:S(2)}) copy-start(f32[8,32,128]{2,1,0:T(8,128)} %b_ref.1) | copy-start | bytes 393220
  1.5 0.9 %copy-start.1 = (s32[8,32,128]{2,1,0:T(8,128)S(1)}, s32[8,32,128]{2,1,0:T(8,128)}, u32[]{:S(2)}) copy-start(s32[8,32,128]{2,1,0:T(8,128)} %codes_ref.1) | copy-start | bytes 393220
  2.5 6.6 %collective-permute-start = (f32[2,8,16,128]{3,2,1,0:T(8,128)S(1)}, f32[2,8,16,128]{3,2,1,0:T(8,128)S(1)}, u32[]{:S(2)}, u32[]{:S(2)}) collective-permute-start(f32[2,8,16,128]{3,2,1,0:T(8,128)S(1)} %get-tuple-element.19), channel_id=1, source_target_pairs={{0,1},{1,2},{2,3},{3,4},{4,5},{5,6},{6,7},{7,8},{8,9},{9,10},{10,1... | collective-permute-start | bytes 393224 | tf_op jit(solution)/shard_map/ppermute | solution.py:418
  6.3 7.0 %collective-permute-start.1 = (f32[2,8,16,128]{3,2,1,0:T(8,128)S(1)}, f32[2,8,16,128]{3,2,1,0:T(8,128)S(1)}, u32[]{:S(2)}, u32[]{:S(2)}) collective-permute-start(f32[2,8,16,128]{3,2,1,0:T(8,128)S(1)} %get-tuple-element.20), channel_id=1, source_target_pairs={{1,0},{2,1},{3,2},{4,3},{5,4},{6,5},{7,6},{8,7},{9,8},{10,9},{11,1... | collective-permute-start | bytes 393224 | tf_op jit(solution)/shard_map/ppermute | solution.py:419
  13.4 10.5 %collective-permute-start.3 = (f32[2,8,64,128]{3,2,1,0:T(8,128)S(1)}, f32[2,8,64,128]{3,2,1,0:T(8,128)S(1)}, u32[]{:S(2)}, u32[]{:S(2)}) collective-permute-start(f32[2,8,64,128]{3,2,1,0:T(8,128)S(1)} %constant_dynamic-update-slice_fusion.own_ref), channel_id=1, source_target_pairs={{16,32},{32,16},{48,64},{64,48},{80,96},{96,80},{112,128},{128,112... | collective-permute-start | bytes 1572872 | tf_op jit(solution)/shard_map/ppermute | solution.py:422
  15.3 8.6 %collective-permute-start.2 = (f32[2,8,64,128]{3,2,1,0:T(8,128)S(1)}, f32[2,8,64,128]{3,2,1,0:T(8,128)S(1)}, u32[]{:S(2)}, u32[]{:S(2)}) collective-permute-start(f32[2,8,64,128]{3,2,1,0:T(8,128)S(1)} %constant_dynamic-update-slice_fusion.own_ref), channel_id=1, source_target_pairs={{0,16},{16,0},{32,48},{48,32},{64,80},{80,64},{96,112},{112,96},{1... | collective-permute-start | bytes 1572872 | tf_op jit(solution)/shard_map/ppermute | solution.py:421
  27.5 14.7 %all-to-all-start = ((f32[32,16,128]{2,1,0:T(8,128)}), f32[32,16,128]{2,1,0:T(8,128)S(1)}, u32[]{:S(2)}, u32[]{:S(2)}) async-start(f32[32,16,128]{2,1,0:T(8,128)} %get-tuple-element.21), calls=%async_computation | async-start | bytes 524288 | tf_op jit(solution)/shard_map/all_to_all | solution.py:434
  35.2 6.7 %collective-permute-start.5 = (f32[4,32,128]{2,1,0:T(8,128)S(1)}, f32[4,32,128]{2,1,0:T(8,128)S(1)}, u32[]{:S(2)}, u32[]{:S(2)}) collective-permute-start(f32[4,32,128]{2,1,0:T(8,128)S(1)} %get-tuple-element.22.vb1_ref), channel_id=1, source_target_pairs={{16,32},{32,16},{48,64},{64,48},{80,96},{96,80},{112,128},{128,112... | collective-permute-start | bytes 196616 | tf_op jit(solution)/shard_map/ppermute | solution.py:433
  37.7 4.2 %collective-permute-start.4 = (f32[4,32,128]{2,1,0:T(8,128)S(1)}, f32[4,32,128]{2,1,0:T(8,128)S(1)}, u32[]{:S(2)}, u32[]{:S(2)}) collective-permute-start(f32[4,32,128]{2,1,0:T(8,128)S(1)} %get-tuple-element.22.vb1_ref), channel_id=1, source_target_pairs={{0,16},{16,0},{32,48},{48,32},{64,80},{80,64},{96,112},{112,96},{1... | collective-permute-start | bytes 196616 | tf_op jit(solution)/shard_map/ppermute | solution.py:432
  44.0 35.5 %all-to-all-start.1 = ((f32[16,32,128]{2,1,0:T(8,128)}), f32[16,32,128]{2,1,0:T(8,128)S(1)}, u32[]{:S(2)}, u32[]{:S(2)}) async-start(f32[16,32,128]{2,1,0:T(8,128)} %get-tuple-element.23), calls=%async_computation.1 | async-start | bytes 524288 | tf_op jit(solution)/shard_map/all_to_all | solution.py:445
  58.6 6.7 %collective-permute-start.6 = (f32[24,128]{1,0:T(8,128)S(1)}, f32[24,128]{1,0:T(8,128)S(1)}, u32[]{:S(2)}, u32[]{:S(2)}) collective-permute-start(f32[24,128]{1,0:T(8,128)S(1)} %get-tuple-element.24), channel_id=1, source_target_pairs={{0,1},{1,2},{2,3},{3,4},{4,5},{5,6},{6,7},{7,8},{8,9},{9,10},{10,1... | collective-permute-start | bytes 36872 | tf_op jit(solution)/shard_map/ppermute | solution.py:443
  62.4 10.1 %collective-permute-start.7 = (f32[24,128]{1,0:T(8,128)S(1)}, f32[24,128]{1,0:T(8,128)S(1)}, u32[]{:S(2)}, u32[]{:S(2)}) collective-permute-start(f32[24,128]{1,0:T(8,128)S(1)} %get-tuple-element.25), channel_id=1, source_target_pairs={{1,0},{2,1},{3,2},{4,3},{5,4},{6,5},{7,6},{8,7},{9,8},{10,9},{11,1... | collective-permute-start | bytes 36872 | tf_op jit(solution)/shard_map/ppermute | solution.py:444

commit v3 on v2

--- a/solution.py
+++ b/solution.py
@@ -129,36 +129,77 @@
     return jnp.where(iota((128, 128), 1) == target(iota((128, 128), 0)), weight, 0.0).astype(F32)
 
 
-def prep_kernel(b_ref, codes_ref, low_ref, high_ref):
+def prep_kernel(b_ref, codes_ref, even_ref, odd_ref):
     kappa = jnp.exp(0.5 * codes_ref[...].astype(F32))
-    low_ref[0] = kappa[:, :16]
-    high_ref[0] = kappa[:, 16:]
-    low_ref[1] = b_ref[:, :16]
-    high_ref[1] = b_ref[:, 16:]
+    up_first = lax.axis_index("inner") % 2 == 0
+    for part, field in enumerate((kappa, b_ref[...])):
+        low, high = field[:, :16], field[:, 16:]
+        even_ref[part] = jnp.where(up_first, high, low)
+        odd_ref[part] = jnp.where(up_first, low, high)
+
+
+SENT = [(0, d, 16 if d <= 6 else 8) for d in range(1, 9)] + [(1, d, 16 if d <= 5 else 8) for d in range(1, 7)]
+SENT_ROWS = sum(32 + 2 * halo for _, _, halo in SENT)
+
+
+def sent_places():
+    first = 0
+    for field, d, halo in SENT:
+        yield field, d, halo, first
+        first += 32 + 2 * halo
+
+
+def in_order(refs):
+    even_ref, odd_ref, from_even_ref, from_odd_ref = refs
+    up_first = lax.axis_index("inner") % 2 == 0
+
+    def group(i, *place):
+        one, other = ((from_odd_ref, from_even_ref), (odd_ref, even_ref), (even_ref, odd_ref), (from_even_ref, from_odd_ref))[i]
+        return jnp.where(up_first, one[place], other[place])
+
+    return group
+
+
+def pack_kernel(*refs):
+    group, out_ref = in_order(refs[:4]), refs[4]
+    right = lax.axis_index("outer") % 2 == 1
+    for field, d, halo, first in sent_places():
+        plane = jnp.where(right, 8 - d, d - 1)
+        rows = [group(i, field, plane) for i in range(4)]
+        rows[0], rows[3] = rows[0][16 - halo :], rows[3][:halo]
+        for part in rows:
+            out_ref[first : first + part.shape[0], :] = part
+            first += part.shape[0]
+
+
+def join_kernel(*refs):
+    group = in_order(refs[:4])
+    for field, own_ref in enumerate(refs[5:]):
+        for p in range(8):
+            for i in range(4):
+                own_ref[p, 16 * i : 16 * i + 16, :] = group(i, field, p)
 
 
 def fine_kernel(
-    own_ref, even_ref, odd_ref,
+    kappas_ref, sources_ref, odd_ref,
     pay_ref, vb_ref, k1_ref, inv1_ref, k0_ref, b0_ref, v0_ref, inv0_ref,
-    kb, ax, ay, az, inv, va, vb, tmp64, tmp32, s1, sk, b1, ax1, ay1, az1, va1, vb1, sems,
+    kb, ax, ay, az, inv, va, vb, tmp64, tmp32, s1, sk, b1, ax1, ay1, az1, va1, vb1,
 ):
-    right_first = lax.axis_index("outer") % 2 == 0
-
-    @pl.when(right_first)
-    def _():
-        pltpu.make_async_copy(odd_ref, kb.at[:, pl.ds(0, 8)], sems.at[0]).start()
-        pltpu.make_async_copy(even_ref, kb.at[:, pl.ds(16, 8)], sems.at[1]).start()
-
-    @pl.when(jnp.logical_not(right_first))
-    def _():
-        pltpu.make_async_copy(even_ref, kb.at[:, pl.ds(0, 8)], sems.at[0]).start()
-        pltpu.make_async_copy(odd_ref, kb.at[:, pl.ds(16, 8)], sems.at[1]).start()
-
-    own = pltpu.make_async_copy(own_ref, kb.at[:, pl.ds(8, 8)], sems.at[2])
-    own.start()
-    pltpu.make_async_copy(odd_ref, kb.at[:, pl.ds(0, 8)], sems.at[0]).wait()
-    pltpu.make_async_copy(odd_ref, kb.at[:, pl.ds(16, 8)], sems.at[1]).wait()
-    own.wait()
+    core = lax.axis_index("outer") % 2
+    right_first = core == 0
+    chip_first = jnp.where(right_first, 8, 0)
+    zeros = jnp.zeros((64, 128), F32)
+    for field, far in ((0, (7, 8)), (1, (6, 7, 8))):
+        for d in far:
+            kb[field, jnp.where(right_first, 8 - d, 15 + d)] = zeros
+    for field, d, halo, first in sent_places():
+        kb[field, jnp.where(right_first, 8 - d, 15 + d), pl.ds(16 - halo, 32 + 2 * halo), :] = odd_ref[
+            pl.ds(first, 32 + 2 * halo), :
+        ]
+    for field, both in enumerate((kappas_ref, sources_ref)):
+        for i in range(2):
+            for p in range(8):
+                kb[field, chip_first + 8 * i + p] = both[i, p]
 
     k, b = kb.at[0], kb.at[1]
     consts = lane_consts(64, 128)
@@ -216,12 +257,12 @@
             place = 64 * part + 32 * half
             rows = pair_rows(tmp32, field[4 + 2 * half] + field[5 + 2 * half])
             pay = pay + dot(rows, pair_matrix(lambda i: jnp.where(i < 64, place + i // 2, -1), weight))
-    for i in range(32):
+    for i in range(16):
         pay_ref[i] = pay
 
 
 def middle_kernel(
-    all_ref, _even1, _odd1, pay_ref, up_ref, down_ref, kw_ref, invw_ref, bw_ref, vw_ref,
+    all_ref, pay_ref, edge_ref, kw_ref, invw_ref, bw_ref, vw_ref,
     k_ref, inv_ref, b_ref, v_ref, ax, ay, az, va, vb, tmp16, s, sk,
 ):
     group = iota((16, 128), 1) // 32
@@ -230,7 +271,7 @@
             place = 2 * part + xl % 2
             plane = None
             for xh in range(4):
-                block = all_ref[xl // 2 + 8 * xh]
+                block = all_ref[(xl // 2) % 2, xl // 4 + 4 * xh]
                 moved = block if xh == place else roll(block, 32 * (xh - place), 1)
                 plane = moved if plane is None else jnp.where(group == xh, moved, plane)
             field[xl + 1] = plane
@@ -254,9 +295,10 @@
         return 0
 
     apply_planes(1, 17, v_ref, k_ref, ax, ay, az, consts, use, 0)
-    first = 2 * lax.axis_index("outer") + 60
+    sends_b = lax.axis_index("outer") % 2 == 0
+    first = 4 * (lax.axis_index("outer") // 2) + 60
     near = []
-    for q in range(10):
+    for q in range(12):
         x = lax.rem(first + q, 64)
         place = lax.rem(x, 16) + 1
         back = lax.rem(128 - 32 * (x // 16), 128)
@@ -264,37 +306,37 @@
         for field, window in ((k_ref, kw_ref), (inv_ref, invw_ref), (b_ref, bw_ref), (v_ref, vw_ref)):
             window[q] = jnp.where(kept, pltpu.roll(field[place], back, 1), 0.0)
         near.append(vw_ref[q] + roll(bw_ref[q], 32, 1))
-    for q in range(5):
-        both = near[q] + roll(near[q + 5], 64, 1)
-        down_ref[4 * q : 4 * q + 4, :] = both[4:8]
-        up_ref[4 * q : 4 * q + 4, :] = both[8:12]
+    for q in range(6):
+        both = near[q] + roll(near[q + 6], 64, 1)
+        edge_ref[4 * q : 4 * q + 4, :] = jnp.where(sends_b, both[8:12], both[4:8])
     for t in range(8):
         s[t] = pair_rows(tmp16, vb[2 * t + 1] + vb[2 * t + 2])
         sk[t] = pair_rows(tmp16, k_ref[2 * t + 1] + k_ref[2 * t + 2])
 
-    for part, (field, weight) in enumerate(((s, 0.125), (sk, 0.03125))):
-        small = jnp.zeros((32, 128), F32)
-        for u in range(2):
-            m = pair_matrix(lambda i: (i // 32) * 32 + u * 16 + (i % 32) // 2, weight)
-            small = small + dot(field[pl.ds(4 * u, 4)].reshape(32, 128), m)
-        for t in range(4):
-            vb[0, 4 * t : 4 * t + 4, :] = small[8 * t + 2 : 8 * t + 6, :]
-        piece = vb[0]
-        for i in range(16):
-            pay_ref[i, 16 * part : 16 * part + 16, :] = piece
+    small = jnp.zeros((32, 128), F32)
+    for u in range(2):
+        m = pair_matrix(lambda i: (i // 32) * 32 + u * 16 + (i % 32) // 2, 0.03125)
+        rows = jnp.where(sends_b, 4.0 * s[pl.ds(4 * u, 4)], sk[pl.ds(4 * u, 4)])
+        small = small + dot(rows.reshape(32, 128), m)
+    for t in range(4):
+        vb[0, 4 * t : 4 * t + 4, :] = small[8 * t + 2 : 8 * t + 6, :]
+    piece = vb[0]
+    for i in range(16):
+        pay_ref[i] = piece
 
 
 def coarse_kernel(
-    all_ref, below_ref, above_ref, k2_ref, inv2_ref, b2_ref, v2_ref, vb1_ref, even_ref, odd_ref, k1_ref, inv1_ref,
+    chip_ref, k2_ref, inv2_ref, b2_ref, v2_ref, odd_ref, k1_ref, inv1_ref,
     k0, b0, v0_ref, inv0, v_out, r_out,
     k3, b3, ax3, ay3, az3, inv3, va3, vb3, c3, tmp16, ax2, ay2, az2, va2, vb2, b2,
     tmp32, b1, va1, vb1, ax1, ay1, az1, tmp64, c1, v0, ax0, ay0, az0, w0,
 ):
     outer, inner = lax.axis_index("outer"), lax.axis_index("inner")
+
     for i in range(16):
         for t in range(4):
-            b3[t + 1, 4 * i : 4 * i + 4, :] = all_ref[i, 4 * t : 4 * t + 4, :]
-            k3[t + 1, 4 * i : 4 * i + 4, :] = all_ref[i, 16 + 4 * t : 20 + 4 * t, :]
+            b3[t + 1, 4 * i : 4 * i + 4, :] = chip_ref[0, 16 * i + 4 * t : 16 * i + 4 * t + 4, :]
+            k3[t + 1, 4 * i : 4 * i + 4, :] = chip_ref[1, 16 * i + 4 * t : 16 * i + 4 * t + 4, :]
     ghosts(k3, 6, 16)
     b3[0] = jnp.zeros((64, 128), F32)
     consts3 = lane_consts(64, 16, True)
@@ -325,37 +367,39 @@
         c3[t, 72:80, :] = jnp.zeros((8, 128), F32)
 
     near = []
-    for q in range(5):
-        x = lax.rem(outer + 30 + q, 32)
+    core = lax.rem(outer, 2)
+    for q in range(6):
+        x = lax.rem(outer - core + 30 + q, 32)
         back = lax.rem(128 - 16 * (x // 4), 128)
         near.append(pltpu.roll(c3[lax.rem(x, 4), pl.ds(4 * inner + 6, 8), :], back, 1))
     wide = dot(jnp.concatenate(near, axis=0), gather_matrix(lambda j: jnp.where(j < 32, j // 2, -1), 1.0))
     lane = iota((16, 128), 1)
-    for q in range(10):
+    for q in range(12):
         rows = twice_rows(tmp16, wide[8 * (q // 2) : 8 * (q // 2) + 8])
-        below, above = (ref[4 * (q % 5) : 4 * (q % 5) + 4, :] for ref in (below_ref, above_ref))
-        if q >= 5:
+        below, above = (chip_ref[i, 256 + 4 * (q % 6) : 260 + 4 * (q % 6), :] for i in range(2))
+        if q >= 6:
             below, above = roll(below, 64, 1), roll(above, 64, 1)
         v2 = jnp.concatenate([below, v2_ref[q, 4:12, :], above], axis=0)
         b2[q] = jnp.concatenate([roll(below, 96, 1), b2_ref[q, 4:12, :], roll(above, 96, 1)], axis=0)
         va2[q] = jnp.where((lane < 32) & (k2_ref[q] > 0.0), v2 + rows, 0.0)
     consts2 = lane_consts(16, 32)
-    make_faces(10, k2_ref, ax2, ay2, az2, consts2)
-    sweep(1, 9, va2, vb2, b2, inv2_ref, k2_ref, ax2, ay2, az2, consts2)
-    sweep(2, 8, vb2, va2, b2, inv2_ref, k2_ref, ax2, ay2, az2, consts2)
-
-    wide = dot(va2[pl.ds(2, 6)].reshape(96, 128), gather_matrix(lambda j: jnp.where(j < 64, j // 2, -1), 1.0))
+    make_faces(12, k2_ref, ax2, ay2, az2, consts2)
+    sweep(1, 11, va2, vb2, b2, inv2_ref, k2_ref, ax2, ay2, az2, consts2)
+    sweep(2, 10, vb2, va2, b2, inv2_ref, k2_ref, ax2, ay2, az2, consts2)
+
+    wide = dot(va2[pl.ds(2 + 2 * core, 6)].reshape(96, 128), gather_matrix(lambda j: jnp.where(j < 64, j // 2, -1), 1.0))
     left_is_odd = outer % 2 == 0
     low = iota((32, 128), 1) < 64
     for q in range(6):
         rows = twice_rows(tmp32, wide[16 * q : 16 * q + 16])
         for p in (2 * q, 2 * q + 1):
+            first, second = (chip_ref[i, 280 + 32 * (p % 4) : 312 + 32 * (p % 4), :] for i in range(2))
             if p < 4:
-                both = jnp.where(left_is_odd, odd_ref[p], even_ref[p])
+                both = jnp.where(left_is_odd, odd_ref[p], first)
             elif p < 8:
-                both = vb1_ref[p - 4]
+                both = jnp.where(left_is_odd, first, second)
             else:
-                both = jnp.where(left_is_odd, even_ref[p - 8], odd_ref[p - 8])
+                both = jnp.where(left_is_odd, second, odd_ref[p - 8])
             b1[p] = roll(both, 64, 1)
             va1[p] = jnp.where(low & (k1_ref[p] > 0.0), both + rows, 0.0)
     consts1 = lane_consts(32, 64)
@@ -409,49 +453,57 @@
 
 def body(right_side, codes):
     groups, boxes = lax.axis_size("outer"), lax.axis_size("inner")
-    evens = [(i, i ^ 1) for i in range(groups)]
     odds = [(i, ((i + 1) ^ 1) - 1) for i in range(1, groups - 1)]
-    ups = [(i, i + 1) for i in range(boxes - 1)]
-    downs = [(i + 1, i) for i in range(boxes - 1)]
-
-    low, high = call(prep_kernel, "prep", "vv", [out(2, 8, 16, 128)] * 2, [], (right_side, codes))
-    below = lax.ppermute(high, "inner", ups)
-    above = lax.ppermute(low, "inner", downs)
-    own = jnp.concatenate([below, low, high, above], axis=2)
-    even = lax.ppermute(own, "outer", evens)
-    odd = lax.ppermute(own, "outer", odds)
+    evens_y = [(i, i ^ 1) for i in range(boxes)]
+    odds_y = [(i, ((i + 1) ^ 1) - 1) for i in range(1, boxes - 1)]
+
+    def on_chip(x):
+        return lax.all_gather(x, "outer", axis_index_groups=[[i, i + 1] for i in range(0, groups, 2)])
+
+    to_even, to_odd = call(prep_kernel, "prep", "vv", [out(2, 8, 16, 128)] * 2, [], (right_side, codes))
+    from_even = lax.ppermute(to_even, "inner", evens_y)
+    from_odd = lax.ppermute(to_odd, "inner", odds_y)
+    parts = (to_even, to_odd, from_even, from_odd)
+    (odd,) = call(pack_kernel, "pack", "vvvv", [out(SENT_ROWS, 128)], [], parts)
+    own = call(join_kernel, "join", "vvvva", [out(8, 64, 128)] * 2, [], parts + (odd,))
+    odd = lax.ppermute(odd, "outer", odds)
+    kappas, sources = (on_chip(x) for x in own)
 
     fine, level1 = (24, 64, 128), (12, 32, 128)
     pay, vb1, k1, inv1, k0, b0, v0, inv0 = call(
-        fine_kernel, "fine", "aaa",
-        [out(32, 16, 128), out(4, 32, 128), out(*level1), out(*level1)] + [out(16, 48, 128)] * 4,
+        fine_kernel, "fine", "vvv",
+        [out(16, 16, 128), out(4, 32, 128), out(*level1), out(*level1)] + [out(16, 48, 128)] * 4,
         [vmem(2, *fine)] + [vmem(*fine)] * 6 + [vmem(64, 128), vmem(32, 128), vmem(256, 128), vmem(384, 128)]
-        + [vmem(*level1)] * 6 + [pltpu.SemaphoreType.DMA((3,))],
-        (own, even, odd),
+        + [vmem(*level1)] * 6,
+        (kappas, sources, odd),
     )
-    even1 = lax.ppermute(vb1, "outer", evens)
+    same_core = [list(range(c, groups, 2)) for c in range(2)]
+    slab = lax.all_to_all(pay, "outer", 0, 0, tiled=True, axis_index_groups=same_core)
+
+    level2, window2 = (18, 16, 128), (12, 16, 128)
+    pay3, edge, k2, inv2, b2, v2 = call(
+        middle_kernel, "middle", "v",
+        [out(16, 16, 128), out(24, 128)] + [out(*window2)] * 4,
+        [vmem(*level2)] * 9 + [vmem(16, 128), vmem(8, 8, 128), vmem(8, 8, 128)],
+        (on_chip(slab),),
+    )
+    ups = [(i * boxes + j, i * boxes + j + 1) for i in range(0, groups, 2) for j in range(boxes - 1)]
+    downs = [(i * boxes + j + 1, i * boxes + j) for i in range(1, groups, 2) for j in range(boxes - 1)]
+    vb1, edge = lax.optimization_barrier((vb1, edge))
+    edge = lax.ppermute(edge, ("outer", "inner"), ups + downs)
     odd1 = lax.ppermute(vb1, "outer", odds)
-    slab = lax.all_to_all(pay, "outer", 0, 0, tiled=True)
-
-    level2, window2 = (18, 16, 128), (10, 16, 128)
-    pay3, up, down, k2, inv2, b2, v2 = call(
-        middle_kernel, "middle", "vaa",
-        [out(16, 32, 128), out(24, 128), out(24, 128)] + [out(*window2)] * 4,
-        [vmem(*level2)] * 9 + [vmem(16, 128), vmem(8, 8, 128), vmem(8, 8, 128)],
-        (slab, even1, odd1),
-    )
-    below2 = lax.ppermute(up, "inner", ups)
-    above2 = lax.ppermute(down, "inner", downs)
-    whole = lax.all_to_all(pay3, "inner", 0, 0, tiled=True)
+    half = lax.all_to_all(pay3, "inner", 0, 0, tiled=True)
+    half, edge, odd1 = lax.optimization_barrier((half, edge, odd1))
+    chip = on_chip(jnp.concatenate([half.reshape(256, 128), edge, vb1.reshape(128, 128)], axis=0))
 
     level3, window = (6, 64, 128), (16, 48, 128)
     return call(
-        coarse_kernel, "coarse", "v" * 16,
+        coarse_kernel, "coarse", "v" * 12,
         [out(8, 32, 128)] * 2,
         [vmem(*level3)] * 8 + [vmem(4, 80, 128), vmem(16, 128)] + [vmem(*window2)] * 6
         + [vmem(32, 128)] + [vmem(*level1)] * 6 + [vmem(64, 128), vmem(256, 128)]
         + [vmem(*window)] * 5,
-        (whole, below2, above2, k2, inv2, b2, v2, vb1, even1, odd1, k1, inv1, k0, b0, v0, inv0),
+        (chip, k2, inv2, b2, v2, odd1, k1, inv1, k0, b0, v0, inv0),
     )
 
 

time: 84.1 us -> 82.2 us (0.977)
  the two profiles are of different devices: /device:TPU:24 before, /device:TPU:1 now
where the time goes in v3:
time: 82.2 us; the launch traced here: 81.8 us
  starting transfers between devices  32.3 us (39%)
  blocking collectives  28.1 us (34%)
  waiting for transfers between devices  9.87 us (12%)
  Pallas kernels  9.05 us (11%)
  local copies, waits for them, and re-layouts  1.8 us (2%)
    all_to_all x1, starting transfers between devices, body(): half = lax.all_to_all(pay3, 'inner', 0, 0, tiled=True)  18.1 us
    all_to_all x1, blocking collectives, body(): lax.all_to_all(pay, 'outer', 0, 0, tiled=True, axis_index_groups=same_core)  14.2 us
    all_gather x4, blocking collectives, on_chip(): lax.all_gather(x, 'outer', axis_index_groups=[[i, i + 1] for i in range(0...  13.9 us
    pallas_call x6, Pallas kernels, call(): pl.pallas_call(kernel, name=name, out_shape=outs, in_specs=[spec[c] for c...  9.05 us
    ppermute x1, starting transfers between devices, body(): odd = lax.ppermute(odd, 'outer', odds)  5.18 us
    all_to_all x1, waiting for transfers between devices, body(): half = lax.all_to_all(pay3, 'inner', 0, 0, tiled=True)  4.58 us
    ppermute x1, starting transfers between devices, body(): from_even = lax.ppermute(to_even, 'inner', evens_y)  4.38 us
    ppermute x1, waiting for transfers between devices, body(): edge = lax.ppermute(edge, ('outer', 'inner'), ups + downs)  3.61 us
  transfers between devices with their start and end apart: 6, of which 3 were waited for; matrix products, arithmetic and copies ran while one was open for 0% of the time, Pallas kernels for 0%

profile of v3, /device:TPU:1, one launch (start us, length us, event | category | flops | bytes accessed | tf_op | source)
XLA Modules:
  0.0 81.8 jit_solution(16064621255708770173)
XLA Ops:
  0.6 0.0 copy-start
  0.6 0.9 %copy-done = f32[8,32,128]{2,1,0:T(8,128)S(1)} copy-done((f32[8,32,128]{2,1,0:T(8,128)S(1)}, f32[8,32,128]{2,1,0:T(8,128)}, u32[]{:S(2)}) %copy-start) | copy-done | bytes 131096
  1.5 0.9 %copy-done.1 = s32[8,32,128]{2,1,0:T(8,128)S(1)} copy-done((s32[8,32,128]{2,1,0:T(8,128)S(1)}, s32[8,32,128]{2,1,0:T(8,128)}, u32[]{:S(2)}) %copy-start.1) | copy-done | bytes 131096
  2.5 4.4 %collective-permute-start = (f32[2,8,16,128]{3,2,1,0:T(8,128)S(1)}, f32[2,8,16,128]{3,2,1,0:T(8,128)S(1)}, u32[]{:S(2)}, u32[]{:S(2)}) collective-permute-start(f32[2,8,16,128]{3,2,1,0:T(8,128)S(1)} %get-tuple-element.25.refs_0_), channel_id=1, source_target_pairs={{0,1},{1,0},{2,3},{3,2},{4,5},{5,4},{6,7},{7,6},{8,9},{9,8},{10,11... | collective-permute-start | bytes 393224 | tf_op jit(solution)/shard_map/ppermute | solution.py:464
  6.9 0.7 collective-permute-start.1
  7.5 1.7 %collective-permute-done.refs_2_ = f32[2,8,16,128]{3,2,1,0:T(8,128)S(1)} collective-permute-done((f32[2,8,16,128]{3,2,1,0:T(8,128)S(1)}, f32[2,8,16,128]{3,2,1,0:T(8,128)S(1)}, u32[]{:S(2)}, u32[]{:S(2)}) %collective-permute-start) | collective-permute-done | bytes 131104 | tf_op jit(solution)/shard_map/ppermute | solution.py:464
  9.2 0.0 collective-permute-done.1.refs_3_
  9.2 5.2 %collective-permute-start.2 = (f32[848,128]{1,0:T(8,128)S(1)}, f32[848,128]{1,0:T(8,128)S(1)}, u32[]{:S(2)}, u32[]{:S(2)}) collective-permute-start(f32[848,128]{1,0:T(8,128)S(1)} %pack.1.refs_4_), channel_id=1, source_target_pairs={{16,32},{32,16},{48,64},{64,48},{80,96},{96,80},{112,128},{128,112... | collective-permute-start | bytes 1302536 | tf_op jit(solution)/shard_map/ppermute | solution.py:469
  14.4 0.1 join.1
  14.5 4.3 %all-gather = f32[16,64,128]{2,1,0:T(8,128)S(1)} all-gather(f32[8,64,128]{2,1,0:T(8,128)S(1)} %get-tuple-element.27), channel_id=2, replica_groups={{0,16},{32,48},{64,80},{96,112},{128,144},{160,176},{192,208},{224,240}..., dimensions={0}, use_global_device_ids=true | all-gather | bytes 786432 | tf_op jit(solution)/shard_map/all_gather | solution.py:461
  18.8 2.2 %all-gather.1 = f32[16,64,128]{2,1,0:T(8,128)S(1)} all-gather(f32[8,64,128]{2,1,0:T(8,128)S(1)} %get-tuple-element.28), channel_id=3, replica_groups={{0,16},{32,48},{64,80},{96,112},{128,144},{160,176},{192,208},{224,240}..., dimensions={0}, use_global_device_ids=true | all-gather | bytes 786432 | tf_op jit(solution)/shard_map/all_gather | solution.py:461
  21.0 0.0 collective-permute-done.2.odd_ref
  21.0 3.1 %fine.1 = (f32[16,16,128]{2,1,0:T(8,128)S(1)}, f32[4,32,128]{2,1,0:T(8,128)S(1)}, f32[12,32,128]{2,1,0:T(8,128)S(1)}, f32[12,32,128]{2,1,0:T(8,128)S(1)}, f32[16...) custom-call(f32[2,8,64,128]{3,2,1,0:T(8,128)S(1)} %bitcast.6, ...), custom_call_target="tpu_custom_call" | custom-call | tf_op jit(solution)/shard_map/fine/pallas_call | solution.py:443
  24.1 14.2 %all_to_all.10 = f32[16,16,128]{2,1,0:T(8,128)S(1)} all-to-all(f32[16,16,128]{2,1,0:T(8,128)S(1)} %get-tuple-element.29), channel_id=1, replica_groups={{0,32,64,96,128,160,192,224,256,288,320,352,384,416,448,480},{16,48,80,..., dimensions={0} | all-to-all | bytes 262144 | tf_op jit(solution)/shard_map/all_to_all | solution.py:481
  38.3 2.4 %all-gather.2 = f32[32,16,128]{2,1,0:T(8,128)S(1)} all-gather(f32[16,16,128]{2,1,0:T(8,128)S(1)} %all_to_all.10), channel_id=4, replica_groups={{0,16},{32,48},{64,80},{96,112},{128,144},{160,176},{192,208},{224,240}..., dimensions={0}, use_global_device_ids=true | all-gather | bytes 393216 | tf_op jit(solution)/shard_map/all_gather | solution.py:461
  40.8 1.9 %middle.1 = (f32[16,16,128]{2,1,0:T(8,128)}, f32[24,128]{1,0:T(8,128)S(1)}, f32[12,16,128]{2,1,0:T(8,128)S(1)}, f32[12,16,128]{2,1,0:T(8,128)S(1)}, f32[12,16,12...) custom-call(f32[2,16,16,128]{3,2,1,0:T(8,128)S(1)} %bitcast.9), custom_call_target="tpu_custom_call" | custom-call | tf_op jit(solution)/shard_map/middle/pallas_call | solution.py:443
  42.6 18.1 %all-to-all-start.1 = ((f32[16,16,128]{2,1,0:T(8,128)}), f32[16,16,128]{2,1,0:T(8,128)S(1)}, u32[]{:S(2)}, u32[]{:S(2)}) async-start(f32[16,16,128]{2,1,0:T(8,128)} %get-tuple-element.30), calls=%async_computation.1 | async-start | bytes 262144 | tf_op jit(solution)/shard_map/all_to_all | solution.py:495
  60.7 2.6 %collective-permute-start.4 = (f32[4,32,128]{2,1,0:T(8,128)S(1)}, f32[4,32,128]{2,1,0:T(8,128)S(1)}, u32[]{:S(2)}, u32[]{:S(2)}) collective-permute-start(f32[4,32,128]{2,1,0:T(8,128)S(1)} %get-tuple-element.34), channel_id=1, source_target_pairs={{16,32},{32,16},{48,64},{64,48},{80,96},{96,80},{112,128},{128,112... | collective-permute-start | bytes 196616 | tf_op jit(solution)/shard_map/ppermute | solution.py:494
  63.4 1.3 %collective-permute-start.3 = (f32[24,128]{1,0:T(8,128)S(1)}, f32[24,128]{1,0:T(8,128)S(1)}, u32[]{:S(2)}, u32[]{:S(2)}) collective-permute-start(f32[24,128]{1,0:T(8,128)S(1)} %get-tuple-element.33), channel_id=1, source_target_pairs={{0,1},{1,2},{2,3},{3,4},{4,5},{5,6},{6,7},{7,8},{8,9},{9,10},{10,1... | collective-permute-start | bytes 36872 | tf_op jit(solution)/shard_map/ppermute | solution.py:493
  64.7 3.6 %collective-permute-done.3 = f32[24,128]{1,0:T(8,128)S(1)} collective-permute-done((f32[24,128]{1,0:T(8,128)S(1)}, f32[24,128]{1,0:T(8,128)S(1)}, u32[]{:S(2)}, u32[]{:S(2)}) %collective-permute-start.3) | collective-permute-done | bytes 12320 | tf_op jit(solution)/shard_map/ppermute | solution.py:493
  68.3 0.0 collective-permute-done.4.odd_ref
  68.3 4.6 %all-to-all-done.1 = f32[16,16,128]{2,1,0:T(8,128)S(1)} async-done(((f32[16,16,128]{2,1,0:T(8,128)}), f32[16,16,128]{2,1,0:T(8,128)S(1)}, u32[]{:S(2)}, u32[]{:S(2)}) %all-to-all-start.1) | async-done | bytes 131104 | tf_op jit(solution)/shard_map/all_to_all | solution.py:495
  72.9 5.0 %all-gather.3 = f32[816,128]{1,0:T(8,128)S(1)} all-gather(f32[408,128]{1,0:T(8,128)S(1)} %pad_maximum_fusion), channel_id=5, replica_groups={{0,16},{32,48},{64,80},{96,112},{128,144},{160,176},{192,208},{224,240}..., dimensions={0}, use_global_device_ids=true | all-gather | bytes 626688 | tf_op jit(solution)/shard_map/all_gather | solution.py:461
  77.9 4.0 %coarse.1 = (f32[8,32,128]{2,1,0:T(8,128)}, f32[8,32,128]{2,1,0:T(8,128)}) custom-call(f32[2,408,128]{2,1,0:T(8,128)S(1)} %bitcast.8, f32[12,16,128]{2,1,0:T(8,128)S(1)} %get-tuple-element.37.k2_ref, f32[12,16,128]{2,1,0:T(8,128)S(1)} %get-tuple-element.38.inv2_ref, f32[12,16,128]{2,1,0:T(8,128)S(1)} %get-tuple-element.39.b2_ref, ...), custom_call_target="tpu_custom_call" | custom-call | tf_op jit(solution)/shard_map/coarse/pallas_call | solution.py:443
  (4 shorter events, 0.1 us)
Async XLA Ops:
  0.6 0.9 %copy-start = (f32[8,32,128]{2,1,0:T(8,128)S(1)}, f32[8,32,128]{2,1,0:T(8,128)}, u32[]{:S(2)}) copy-start(f32[8,32,128]{2,1,0:T(8,128)} %b_ref.1) | copy-start | bytes 393220
  1.5 0.9 %copy-start.1 = (s32[8,32,128]{2,1,0:T(8,128)S(1)}, s32[8,32,128]{2,1,0:T(8,128)}, u32[]{:S(2)}) copy-start(s32[8,32,128]{2,1,0:T(8,128)} %codes_ref.1) | copy-start | bytes 393220
  2.5 6.7 %collective-permute-start = (f32[2,8,16,128]{3,2,1,0:T(8,128)S(1)}, f32[2,8,16,128]{3,2,1,0:T(8,128)S(1)}, u32[]{:S(2)}, u32[]{:S(2)}) collective-permute-start(f32[2,8,16,128]{3,2,1,0:T(8,128)S(1)} %get-tuple-element.25.refs_0_), channel_id=1, source_target_pairs={{0,1},{1,0},{2,3},{3,2},{4,5},{5,4},{6,7},{7,6},{8,9},{9,8},{10,11... | collective-permute-start | bytes 393224 | tf_op jit(solution)/shard_map/ppermute | solution.py:464
  6.9 2.3 %collective-permute-start.1 = (f32[2,8,16,128]{3,2,1,0:T(8,128)S(1)}, f32[2,8,16,128]{3,2,1,0:T(8,128)S(1)}, u32[]{:S(2)}, u32[]{:S(2)}) collective-permute-start(f32[2,8,16,128]{3,2,1,0:T(8,128)S(1)} %get-tuple-element.26.refs_1_), channel_id=1, source_target_pairs={{1,2},{2,1},{3,4},{4,3},{5,6},{6,5},{7,8},{8,7},{9,10},{10,9},{11,... | collective-permute-start | bytes 393224 | tf_op jit(solution)/shard_map/ppermute | solution.py:465
  9.2 11.8 %collective-permute-start.2 = (f32[848,128]{1,0:T(8,128)S(1)}, f32[848,128]{1,0:T(8,128)S(1)}, u32[]{:S(2)}, u32[]{:S(2)}) collective-permute-start(f32[848,128]{1,0:T(8,128)S(1)} %pack.1.refs_4_), channel_id=1, source_target_pairs={{16,32},{32,16},{48,64},{64,48},{80,96},{96,80},{112,128},{128,112... | collective-permute-start | bytes 1302536 | tf_op jit(solution)/shard_map/ppermute | solution.py:469
  42.6 30.3 %all-to-all-start.1 = ((f32[16,16,128]{2,1,0:T(8,128)}), f32[16,16,128]{2,1,0:T(8,128)S(1)}, u32[]{:S(2)}, u32[]{:S(2)}) async-start(f32[16,16,128]{2,1,0:T(8,128)} %get-tuple-element.30), calls=%async_computation.1 | async-start | bytes 262144 | tf_op jit(solution)/shard_map/all_to_all | solution.py:495
  60.7 7.6 %collective-permute-start.4 = (f32[4,32,128]{2,1,0:T(8,128)S(1)}, f32[4,32,128]{2,1,0:T(8,128)S(1)}, u32[]{:S(2)}, u32[]{:S(2)}) collective-permute-start(f32[4,32,128]{2,1,0:T(8,128)S(1)} %get-tuple-element.34), channel_id=1, source_target_pairs={{16,32},{32,16},{48,64},{64,48},{80,96},{96,80},{112,128},{128,112... | collective-permute-start | bytes 196616 | tf_op jit(solution)/shard_map/ppermute | solution.py:494
  63.4 4.9 %collective-permute-start.3 = (f32[24,128]{1,0:T(8,128)S(1)}, f32[24,128]{1,0:T(8,128)S(1)}, u32[]{:S(2)}, u32[]{:S(2)}) collective-permute-start(f32[24,128]{1,0:T(8,128)S(1)} %get-tuple-element.33), channel_id=1, source_target_pairs={{0,1},{1,2},{2,3},{3,4},{4,5},{5,6},{6,7},{7,8},{8,9},{9,10},{10,1... | collective-permute-start | bytes 36872 | tf_op jit(solution)/shard_map/ppermute | solution.py:493

commit v4 on v3

--- a/solution.py
+++ b/solution.py
@@ -129,77 +129,70 @@
     return jnp.where(iota((128, 128), 1) == target(iota((128, 128), 0)), weight, 0.0).astype(F32)
 
 
-def prep_kernel(b_ref, codes_ref, even_ref, odd_ref):
+SENT = [(0, d, h) for d, h in zip(range(1, 9), (16, 16, 12, 12, 12, 12, 8, 0))]
+SENT += [(1, d, h) for d, h in zip(range(1, 7), (16, 12, 12, 12, 12, 8))]
+CORNER_ROWS = sum(2 * h for _, _, h in SENT)
+
+
+def sent_plane(d):
+    return jnp.where(lax.axis_index("outer") % 2 == 1, 8 - d, d - 1)
+
+
+def prep_kernel(b_ref, codes_ref, even_ref, odd_ref, own_ref, side_ref):
     kappa = jnp.exp(0.5 * codes_ref[...].astype(F32))
     up_first = lax.axis_index("inner") % 2 == 0
     for part, field in enumerate((kappa, b_ref[...])):
         low, high = field[:, :16], field[:, 16:]
         even_ref[part] = jnp.where(up_first, high, low)
         odd_ref[part] = jnp.where(up_first, low, high)
-
-
-SENT = [(0, d, 16 if d <= 6 else 8) for d in range(1, 9)] + [(1, d, 16 if d <= 5 else 8) for d in range(1, 7)]
-SENT_ROWS = sum(32 + 2 * halo for _, _, halo in SENT)
-
-
-def sent_places():
+        own_ref[part] = field
+    for i, (field, d, _) in enumerate(SENT):
+        side_ref[i] = own_ref[field, sent_plane(d)]
+
+
+def pack_kernel(from_even_ref, from_odd_ref, corner_ref, halo_ref):
+    up_first = lax.axis_index("inner") % 2 == 0
+    for field in range(2):
+        for p in range(8):
+            even, odd = from_even_ref[field, p], from_odd_ref[field, p]
+            halo_ref[field, p, 0:16, :] = jnp.where(up_first, odd, even)
+            halo_ref[field, p, 16:32, :] = jnp.where(up_first, even, odd)
     first = 0
-    for field, d, halo in SENT:
-        yield field, d, halo, first
-        first += 32 + 2 * halo
-
-
-def in_order(refs):
-    even_ref, odd_ref, from_even_ref, from_odd_ref = refs
-    up_first = lax.axis_index("inner") % 2 == 0
-
-    def group(i, *place):
-        one, other = ((from_odd_ref, from_even_ref), (odd_ref, even_ref), (even_ref, odd_ref), (from_even_ref, from_odd_ref))[i]
-        return jnp.where(up_first, one[place], other[place])
-
-    return group
-
-
-def pack_kernel(*refs):
-    group, out_ref = in_order(refs[:4]), refs[4]
-    right = lax.axis_index("outer") % 2 == 1
-    for field, d, halo, first in sent_places():
-        plane = jnp.where(right, 8 - d, d - 1)
-        rows = [group(i, field, plane) for i in range(4)]
-        rows[0], rows[3] = rows[0][16 - halo :], rows[3][:halo]
-        for part in rows:
-            out_ref[first : first + part.shape[0], :] = part
-            first += part.shape[0]
-
-
-def join_kernel(*refs):
-    group = in_order(refs[:4])
-    for field, own_ref in enumerate(refs[5:]):
-        for p in range(8):
-            for i in range(4):
-                own_ref[p, 16 * i : 16 * i + 16, :] = group(i, field, p)
+    for field, d, h in SENT:
+        if h:
+            rows = halo_ref[field, sent_plane(d), 16 - h : 16 + h, :]
+            corner_ref[first : first + 2 * h, :] = rows
+            first += 2 * h
 
 
 def fine_kernel(
-    kappas_ref, sources_ref, odd_ref,
+    chip_ref, halo_ref, side_ref, corner_ref,
     pay_ref, vb_ref, k1_ref, inv1_ref, k0_ref, b0_ref, v0_ref, inv0_ref,
     kb, ax, ay, az, inv, va, vb, tmp64, tmp32, s1, sk, b1, ax1, ay1, az1, va1, vb1,
 ):
-    core = lax.axis_index("outer") % 2
-    right_first = core == 0
+    right_first = lax.axis_index("outer") % 2 == 0
     chip_first = jnp.where(right_first, 8, 0)
     zeros = jnp.zeros((64, 128), F32)
-    for field, far in ((0, (7, 8)), (1, (6, 7, 8))):
-        for d in far:
-            kb[field, jnp.where(right_first, 8 - d, 15 + d)] = zeros
-    for field, d, halo, first in sent_places():
-        kb[field, jnp.where(right_first, 8 - d, 15 + d), pl.ds(16 - halo, 32 + 2 * halo), :] = odd_ref[
-            pl.ds(first, 32 + 2 * halo), :
-        ]
-    for field, both in enumerate((kappas_ref, sources_ref)):
+    for field, d in ((1, 7), (1, 8)):
+        kb[field, jnp.where(right_first, 8 - d, 15 + d)] = zeros
+    first = 0
+    for i, (field, d, h) in enumerate(SENT):
+        place = jnp.where(right_first, 8 - d, 15 + d)
+        if h < 16:
+            kb[field, place, 0:16, :] = zeros[0:16]
+            kb[field, place, 48:64, :] = zeros[0:16]
+        kb[field, place, 16:48, :] = side_ref[i]
+        if h:
+            kb[field, place, 16 - h : 16, :] = corner_ref[first : first + h, :]
+            kb[field, place, 48 : 48 + h, :] = corner_ref[first + h : first + 2 * h, :]
+            first += 2 * h
+    for field in range(2):
         for i in range(2):
             for p in range(8):
-                kb[field, chip_first + 8 * i + p] = both[i, p]
+                place = chip_first + 8 * i + p
+                kb[field, place, 0:16, :] = halo_ref[i, field, p, 0:16, :]
+                kb[field, place, 16:48, :] = chip_ref[i, field, p]
+                kb[field, place, 48:64, :] = halo_ref[i, field, p, 16:32, :]
 
     k, b = kb.at[0], kb.at[1]
     consts = lane_consts(64, 128)
@@ -460,22 +453,27 @@
     def on_chip(x):
         return lax.all_gather(x, "outer", axis_index_groups=[[i, i + 1] for i in range(0, groups, 2)])
 
-    to_even, to_odd = call(prep_kernel, "prep", "vv", [out(2, 8, 16, 128)] * 2, [], (right_side, codes))
+    to_even, to_odd, own, side = call(
+        prep_kernel, "prep", "vv",
+        [out(2, 8, 16, 128)] * 2 + [out(2, 8, 32, 128), out(len(SENT), 32, 128)], [], (right_side, codes),
+    )
     from_even = lax.ppermute(to_even, "inner", evens_y)
     from_odd = lax.ppermute(to_odd, "inner", odds_y)
-    parts = (to_even, to_odd, from_even, from_odd)
-    (odd,) = call(pack_kernel, "pack", "vvvv", [out(SENT_ROWS, 128)], [], parts)
-    own = call(join_kernel, "join", "vvvva", [out(8, 64, 128)] * 2, [], parts + (odd,))
-    odd = lax.ppermute(odd, "outer", odds)
-    kappas, sources = (on_chip(x) for x in own)
+    side = lax.ppermute(side, "outer", odds)
+    chip = on_chip(own)
+    corner, halo = call(
+        pack_kernel, "pack", "vv", [out(CORNER_ROWS, 128), out(2, 8, 32, 128)], [], (from_even, from_odd)
+    )
+    corner = lax.ppermute(corner, "outer", odds)
+    halo = on_chip(halo)
 
     fine, level1 = (24, 64, 128), (12, 32, 128)
     pay, vb1, k1, inv1, k0, b0, v0, inv0 = call(
-        fine_kernel, "fine", "vvv",
+        fine_kernel, "fine", "vvvv",
         [out(16, 16, 128), out(4, 32, 128), out(*level1), out(*level1)] + [out(16, 48, 128)] * 4,
         [vmem(2, *fine)] + [vmem(*fine)] * 6 + [vmem(64, 128), vmem(32, 128), vmem(256, 128), vmem(384, 128)]
         + [vmem(*level1)] * 6,
-        (kappas, sources, odd),
+        (chip, halo, side, corner),
     )
     same_core = [list(range(c, groups, 2)) for c in range(2)]
     slab = lax.all_to_all(pay, "outer", 0, 0, tiled=True, axis_index_groups=same_core)
@@ -490,10 +488,10 @@
     ups = [(i * boxes + j, i * boxes + j + 1) for i in range(0, groups, 2) for j in range(boxes - 1)]
     downs = [(i * boxes + j + 1, i * boxes + j) for i in range(1, groups, 2) for j in range(boxes - 1)]
     vb1, edge = lax.optimization_barrier((vb1, edge))
+    odd1 = lax.ppermute(vb1, "outer", odds)
     edge = lax.ppermute(edge, ("outer", "inner"), ups + downs)
-    odd1 = lax.ppermute(vb1, "outer", odds)
     half = lax.all_to_all(pay3, "inner", 0, 0, tiled=True)
-    half, edge, odd1 = lax.optimization_barrier((half, edge, odd1))
+    half, edge = lax.optimization_barrier((half, edge))
     chip = on_chip(jnp.concatenate([half.reshape(256, 128), edge, vb1.reshape(128, 128)], axis=0))
 
     level3, window = (6, 64, 128), (16, 48, 128)

time: 82.2 us -> 80.1 us (0.974)
  waiting for transfers between devices: 9.87 us -> 5.71 us
  starting transfers between devices: 32.3 us -> 35.9 us
  blocking collectives: 28.1 us -> 26.5 us
    ppermute x1, waiting for transfers between devices: 3.61 us -> 0.01 us  [body(): edge = lax.ppermute(edge, ('outer', 'inner'), ups + downs)]
    ppermute x1, starting transfers between devices: 2.63 us -> 5.16 us  [body(): odd1 = lax.ppermute(vb1, 'outer', odds)]
    all_to_all x1, blocking collectives: 14.2 us -> 11.9 us  [body(): lax.all_to_all(pay, 'outer', 0, 0, tiled=True, axis_index_groups=same_core)]
    ppermute x1, waiting for transfers between devices: 1.67 us -> 0.01 us  [body(): from_even = lax.ppermute(to_even, 'inner', evens_y)]
    ppermute x1 -> x2, starting transfers between devices: 5.18 us -> 6.82 us  [the longest x1 4.05 us: body(): side = lax.ppermute(side, 'outer', odds)]
    all_to_all x1, waiting for transfers between devices: 4.58 us -> 5.69 us  [body(): half = lax.all_to_all(pay3, 'inner', 0, 0, tiled=True)]
    pallas_call x6 -> x5, Pallas kernels: 9.05 us -> 9.02 us  [call(): pl.pallas_call(kernel, name=name, out_shape=outs, in_specs=[spec[c] for c...]
  transfers between devices with their start and end apart: 6 -> 7, of which waited for: 3 -> 1; matrix products, arithmetic and copies ran while one was open for 0% -> 0% of each run, Pallas kernels for 0% -> 0%
where the time goes in v4:
time: 80.1 us; the launch traced here: 79.6 us
  starting transfers between devices  35.9 us (45%)
  blocking collectives  26.5 us (33%)
  Pallas kernels  9.02 us (11%)
  waiting for transfers between devices  5.71 us (7%)
  local copies, waits for them, and re-layouts  1.8 us (2%)
    all_to_all x1, starting transfers between devices, body(): half = lax.all_to_all(pay3, 'inner', 0, 0, tiled=True)  17.6 us
    all_gather x4, blocking collectives, on_chip(): lax.all_gather(x, 'outer', axis_index_groups=[[i, i + 1] for i in range(0...  14.5 us
    all_to_all x1, blocking collectives, body(): lax.all_to_all(pay, 'outer', 0, 0, tiled=True, axis_index_groups=same_core)  11.9 us
    pallas_call x5, Pallas kernels, call(): pl.pallas_call(kernel, name=name, out_shape=outs, in_specs=[spec[c] for c...  9.02 us
    all_to_all x1, waiting for transfers between devices, body(): half = lax.all_to_all(pay3, 'inner', 0, 0, tiled=True)  5.69 us
    ppermute x1, starting transfers between devices, body(): odd1 = lax.ppermute(vb1, 'outer', odds)  5.16 us
    ppermute x1, starting transfers between devices, body(): from_even = lax.ppermute(to_even, 'inner', evens_y)  4.38 us
    ppermute x1, starting transfers between devices, body(): side = lax.ppermute(side, 'outer', odds)  4.05 us
  transfers between devices with their start and end apart: 7, of which 1 were waited for; matrix products, arithmetic and copies ran while one was open for 0% of the time, Pallas kernels for 0%

profile of v4, /device:TPU:1, one launch (start us, length us, event | category | flops | bytes accessed | tf_op | source)
XLA Modules:
  0.0 79.6 jit_solution(11834380471570269878)
XLA Ops:
  0.6 0.9 %copy-done = f32[8,32,128]{2,1,0:T(8,128)S(1)} copy-done((f32[8,32,128]{2,1,0:T(8,128)S(1)}, f32[8,32,128]{2,1,0:T(8,128)}, u32[]{:S(2)}) %copy-start) | copy-done | bytes 131096
  1.5 0.9 %copy-done.1 = s32[8,32,128]{2,1,0:T(8,128)S(1)} copy-done((s32[8,32,128]{2,1,0:T(8,128)S(1)}, s32[8,32,128]{2,1,0:T(8,128)}, u32[]{:S(2)}) %copy-start.1) | copy-done | bytes 131096
  2.4 0.1 prep.1
  2.5 4.4 %collective-permute-start = (f32[2,8,16,128]{3,2,1,0:T(8,128)S(1)}, f32[2,8,16,128]{3,2,1,0:T(8,128)S(1)}, u32[]{:S(2)}, u32[]{:S(2)}) collective-permute-start(f32[2,8,16,128]{3,2,1,0:T(8,128)S(1)} %get-tuple-element.27), channel_id=1, source_target_pairs={{0,1},{1,0},{2,3},{3,2},{4,5},{5,4},{6,7},{7,6},{8,9},{9,8},{10,11... | collective-permute-start | bytes 393224 | tf_op jit(solution)/shard_map/ppermute | solution.py:460
  6.9 0.7 collective-permute-start.1
  7.6 4.0 %collective-permute-start.2 = (f32[14,32,128]{2,1,0:T(8,128)S(1)}, f32[14,32,128]{2,1,0:T(8,128)S(1)}, u32[]{:S(2)}, u32[]{:S(2)}) collective-permute-start(f32[14,32,128]{2,1,0:T(8,128)S(1)} %get-tuple-element.30), channel_id=1, source_target_pairs={{16,32},{32,16},{48,64},{64,48},{80,96},{96,80},{112,128},{128,112... | collective-permute-start | bytes 688136 | tf_op jit(solution)/shard_map/ppermute | solution.py:462
  11.6 0.0 collective-permute-done.from_even_ref
  11.6 0.0 collective-permute-done.1.from_odd_ref
  11.7 2.8 %collective-permute-start.3 = (f32[320,128]{1,0:T(8,128)S(1)}, f32[320,128]{1,0:T(8,128)S(1)}, u32[]{:S(2)}, u32[]{:S(2)}) collective-permute-start(f32[320,128]{1,0:T(8,128)S(1)} %get-tuple-element.31), channel_id=1, source_target_pairs={{16,32},{32,16},{48,64},{64,48},{80,96},{96,80},{112,128},{128,112... | collective-permute-start | bytes 491528 | tf_op jit(solution)/shard_map/ppermute | solution.py:467
  14.5 4.3 %all-gather = f32[4,8,32,128]{3,2,1,0:T(8,128)S(1)} all-gather(f32[2,8,32,128]{3,2,1,0:T(8,128)S(1)} %get-tuple-element.26), channel_id=2, replica_groups={{0,16},{32,48},{64,80},{96,112},{128,144},{160,176},{192,208},{224,240}..., dimensions={0}, use_global_device_ids=true | all-gather | bytes 786432 | tf_op jit(solution)/shard_map/all_gather | solution.py:454
  18.8 2.2 %all-gather.1 = f32[4,8,32,128]{3,2,1,0:T(8,128)S(1)} all-gather(f32[2,8,32,128]{3,2,1,0:T(8,128)S(1)} %get-tuple-element.29), channel_id=3, replica_groups={{0,16},{32,48},{64,80},{96,112},{128,144},{160,176},{192,208},{224,240}..., dimensions={0}, use_global_device_ids=true | all-gather | bytes 786432 | tf_op jit(solution)/shard_map/all_gather | solution.py:454
  21.0 0.0 collective-permute-done.2.side_ref
  21.0 0.0 collective-permute-done.3.corner_ref
  21.0 3.1 %fine.1 = (f32[16,16,128]{2,1,0:T(8,128)S(1)}, f32[4,32,128]{2,1,0:T(8,128)S(1)}, f32[12,32,128]{2,1,0:T(8,128)S(1)}, f32[12,32,128]{2,1,0:T(8,128)S(1)}, f32[16...) custom-call(f32[2,2,8,32,128]{4,3,2,1,0:T(8,128)S(1)} %bitcast.6, ...), custom_call_target="tpu_custom_call" | custom-call | tf_op jit(solution)/shard_map/fine/pallas_call | solution.py:436
  24.0 11.9 %all_to_all.10 = f32[16,16,128]{2,1,0:T(8,128)S(1)} all-to-all(f32[16,16,128]{2,1,0:T(8,128)S(1)} %get-tuple-element.32), channel_id=1, replica_groups={{0,32,64,96,128,160,192,224,256,288,320,352,384,416,448,480},{16,48,80,..., dimensions={0} | all-to-all | bytes 262144 | tf_op jit(solution)/shard_map/all_to_all | solution.py:479
  36.0 3.1 %all-gather.2 = f32[32,16,128]{2,1,0:T(8,128)S(1)} all-gather(f32[16,16,128]{2,1,0:T(8,128)S(1)} %all_to_all.10), channel_id=4, replica_groups={{0,16},{32,48},{64,80},{96,112},{128,144},{160,176},{192,208},{224,240}..., dimensions={0}, use_global_device_ids=true | all-gather | bytes 393216 | tf_op jit(solution)/shard_map/all_gather | solution.py:454
  39.1 1.9 %middle.1 = (f32[16,16,128]{2,1,0:T(8,128)}, f32[24,128]{1,0:T(8,128)S(1)}, f32[12,16,128]{2,1,0:T(8,128)S(1)}, f32[12,16,128]{2,1,0:T(8,128)S(1)}, f32[12,16,12...) custom-call(f32[2,16,16,128]{3,2,1,0:T(8,128)S(1)} %bitcast.9), custom_call_target="tpu_custom_call" | custom-call | tf_op jit(solution)/shard_map/middle/pallas_call | solution.py:436
  40.9 17.6 %all-to-all-start.1 = ((f32[16,16,128]{2,1,0:T(8,128)}), f32[16,16,128]{2,1,0:T(8,128)S(1)}, u32[]{:S(2)}, u32[]{:S(2)}) async-start(f32[16,16,128]{2,1,0:T(8,128)} %get-tuple-element.33), calls=%async_computation.1 | async-start | bytes 262144 | tf_op jit(solution)/shard_map/all_to_all | solution.py:493
  58.5 1.3 %collective-permute-start.4 = (f32[24,128]{1,0:T(8,128)S(1)}, f32[24,128]{1,0:T(8,128)S(1)}, u32[]{:S(2)}, u32[]{:S(2)}) collective-permute-start(f32[24,128]{1,0:T(8,128)S(1)} %get-tuple-element.36), channel_id=1, source_target_pairs={{0,1},{1,2},{2,3},{3,4},{4,5},{5,6},{6,7},{7,8},{8,9},{9,10},{10,1... | collective-permute-start | bytes 36872 | tf_op jit(solution)/shard_map/ppermute | solution.py:492
  59.8 5.2 %collective-permute-start.5 = (f32[4,32,128]{2,1,0:T(8,128)S(1)}, f32[4,32,128]{2,1,0:T(8,128)S(1)}, u32[]{:S(2)}, u32[]{:S(2)}) collective-permute-start(f32[4,32,128]{2,1,0:T(8,128)S(1)} %get-tuple-element.39), channel_id=1, source_target_pairs={{16,32},{32,16},{48,64},{64,48},{80,96},{96,80},{112,128},{128,112... | collective-permute-start | bytes 196616 | tf_op jit(solution)/shard_map/ppermute | solution.py:491
  65.0 5.7 %all-to-all-done.1 = f32[16,16,128]{2,1,0:T(8,128)S(1)} async-done(((f32[16,16,128]{2,1,0:T(8,128)}), f32[16,16,128]{2,1,0:T(8,128)S(1)}, u32[]{:S(2)}, u32[]{:S(2)}) %all-to-all-start.1) | async-done | bytes 131104 | tf_op jit(solution)/shard_map/all_to_all | solution.py:493
  70.7 4.9 %all-gather.3 = f32[816,128]{1,0:T(8,128)S(1)} all-gather(f32[408,128]{1,0:T(8,128)S(1)} %pad_maximum_fusion), channel_id=5, replica_groups={{0,16},{32,48},{64,80},{96,112},{128,144},{160,176},{192,208},{224,240}..., dimensions={0}, use_global_device_ids=true | all-gather | bytes 626688 | tf_op jit(solution)/shard_map/all_gather | solution.py:454
  75.7 0.0 collective-permute-done.5.odd_ref
  75.7 4.0 %coarse.1 = (f32[8,32,128]{2,1,0:T(8,128)}, f32[8,32,128]{2,1,0:T(8,128)}) custom-call(f32[2,408,128]{2,1,0:T(8,128)S(1)} %bitcast.8, f32[12,16,128]{2,1,0:T(8,128)S(1)} %get-tuple-element.40.k2_ref, f32[12,16,128]{2,1,0:T(8,128)S(1)} %get-tuple-element.41.inv2_ref, f32[12,16,128]{2,1,0:T(8,128)S(1)} %get-tuple-element.42.b2_ref, ...), custom_call_target="tpu_custom_call" | custom-call | tf_op jit(solution)/shard_map/coarse/pallas_call | solution.py:436
  (5 shorter events, 0.1 us)
Async XLA Ops:
  0.6 0.9 %copy-start = (f32[8,32,128]{2,1,0:T(8,128)S(1)}, f32[8,32,128]{2,1,0:T(8,128)}, u32[]{:S(2)}) copy-start(f32[8,32,128]{2,1,0:T(8,128)} %b_ref.1) | copy-start | bytes 393220
  1.5 0.9 %copy-start.1 = (s32[8,32,128]{2,1,0:T(8,128)S(1)}, s32[8,32,128]{2,1,0:T(8,128)}, u32[]{:S(2)}) copy-start(s32[8,32,128]{2,1,0:T(8,128)} %codes_ref.1) | copy-start | bytes 393220
  2.5 9.1 %collective-permute-start = (f32[2,8,16,128]{3,2,1,0:T(8,128)S(1)}, f32[2,8,16,128]{3,2,1,0:T(8,128)S(1)}, u32[]{:S(2)}, u32[]{:S(2)}) collective-permute-start(f32[2,8,16,128]{3,2,1,0:T(8,128)S(1)} %get-tuple-element.27), channel_id=1, source_target_pairs={{0,1},{1,0},{2,3},{3,2},{4,5},{5,4},{6,7},{7,6},{8,9},{9,8},{10,11... | collective-permute-start | bytes 393224 | tf_op jit(solution)/shard_map/ppermute | solution.py:460
  6.9 4.7 %collective-permute-start.1 = (f32[2,8,16,128]{3,2,1,0:T(8,128)S(1)}, f32[2,8,16,128]{3,2,1,0:T(8,128)S(1)}, u32[]{:S(2)}, u32[]{:S(2)}) collective-permute-start(f32[2,8,16,128]{3,2,1,0:T(8,128)S(1)} %get-tuple-element.28), channel_id=1, source_target_pairs={{1,2},{2,1},{3,4},{4,3},{5,6},{6,5},{7,8},{8,7},{9,10},{10,9},{11,... | collective-permute-start | bytes 393224 | tf_op jit(solution)/shard_map/ppermute | solution.py:461
  7.6 13.4 %collective-permute-start.2 = (f32[14,32,128]{2,1,0:T(8,128)S(1)}, f32[14,32,128]{2,1,0:T(8,128)S(1)}, u32[]{:S(2)}, u32[]{:S(2)}) collective-permute-start(f32[14,32,128]{2,1,0:T(8,128)S(1)} %get-tuple-element.30), channel_id=1, source_target_pairs={{16,32},{32,16},{48,64},{64,48},{80,96},{96,80},{112,128},{128,112... | collective-permute-start | bytes 688136 | tf_op jit(solution)/shard_map/ppermute | solution.py:462
  11.7 9.3 %collective-permute-start.3 = (f32[320,128]{1,0:T(8,128)S(1)}, f32[320,128]{1,0:T(8,128)S(1)}, u32[]{:S(2)}, u32[]{:S(2)}) collective-permute-start(f32[320,128]{1,0:T(8,128)S(1)} %get-tuple-element.31), channel_id=1, source_target_pairs={{16,32},{32,16},{48,64},{64,48},{80,96},{96,80},{112,128},{128,112... | collective-permute-start | bytes 491528 | tf_op jit(solution)/shard_map/ppermute | solution.py:467
  40.9 29.8 %all-to-all-start.1 = ((f32[16,16,128]{2,1,0:T(8,128)}), f32[16,16,128]{2,1,0:T(8,128)S(1)}, u32[]{:S(2)}, u32[]{:S(2)}) async-start(f32[16,16,128]{2,1,0:T(8,128)} %get-tuple-element.33), calls=%async_computation.1 | async-start | bytes 262144 | tf_op jit(solution)/shard_map/all_to_all | solution.py:493
  58.5 6.5 %collective-permute-start.4 = (f32[24,128]{1,0:T(8,128)S(1)}, f32[24,128]{1,0:T(8,128)S(1)}, u32[]{:S(2)}, u32[]{:S(2)}) collective-permute-start(f32[24,128]{1,0:T(8,128)S(1)} %get-tuple-element.36), channel_id=1, source_target_pairs={{0,1},{1,2},{2,3},{3,4},{4,5},{5,6},{6,7},{7,8},{8,9},{9,10},{10,1... | collective-permute-start | bytes 36872 | tf_op jit(solution)/shard_map/ppermute | solution.py:492
  59.8 15.8 %collective-permute-start.5 = (f32[4,32,128]{2,1,0:T(8,128)S(1)}, f32[4,32,128]{2,1,0:T(8,128)S(1)}, u32[]{:S(2)}, u32[]{:S(2)}) collective-permute-start(f32[4,32,128]{2,1,0:T(8,128)S(1)} %get-tuple-element.39), channel_id=1, source_target_pairs={{16,32},{32,16},{48,64},{64,48},{80,96},{96,80},{112,128},{128,112... | collective-permute-start | bytes 196616 | tf_op jit(solution)/shard_map/ppermute | solution.py:491

commit v5 on v4

--- a/solution.py
+++ b/solution.py
@@ -250,7 +250,7 @@
             place = 64 * part + 32 * half
             rows = pair_rows(tmp32, field[4 + 2 * half] + field[5 + 2 * half])
             pay = pay + dot(rows, pair_matrix(lambda i: jnp.where(i < 64, place + i // 2, -1), weight))
-    for i in range(16):
+    for i in range(32):
         pay_ref[i] = pay
 
 
@@ -264,7 +264,7 @@
             place = 2 * part + xl % 2
             plane = None
             for xh in range(4):
-                block = all_ref[(xl // 2) % 2, xl // 4 + 4 * xh]
+                block = all_ref[xl // 2 + 8 * xh]
                 moved = block if xh == place else roll(block, 32 * (xh - place), 1)
                 plane = moved if plane is None else jnp.where(group == xh, moved, plane)
             field[xl + 1] = plane
@@ -470,20 +470,19 @@
     fine, level1 = (24, 64, 128), (12, 32, 128)
     pay, vb1, k1, inv1, k0, b0, v0, inv0 = call(
         fine_kernel, "fine", "vvvv",
-        [out(16, 16, 128), out(4, 32, 128), out(*level1), out(*level1)] + [out(16, 48, 128)] * 4,
+        [out(32, 16, 128), out(4, 32, 128), out(*level1), out(*level1)] + [out(16, 48, 128)] * 4,
         [vmem(2, *fine)] + [vmem(*fine)] * 6 + [vmem(64, 128), vmem(32, 128), vmem(256, 128), vmem(384, 128)]
         + [vmem(*level1)] * 6,
         (chip, halo, side, corner),
     )
-    same_core = [list(range(c, groups, 2)) for c in range(2)]
-    slab = lax.all_to_all(pay, "outer", 0, 0, tiled=True, axis_index_groups=same_core)
+    slab = lax.all_to_all(pay, "outer", 0, 0, tiled=True)
 
     level2, window2 = (18, 16, 128), (12, 16, 128)
     pay3, edge, k2, inv2, b2, v2 = call(
         middle_kernel, "middle", "v",
         [out(16, 16, 128), out(24, 128)] + [out(*window2)] * 4,
         [vmem(*level2)] * 9 + [vmem(16, 128), vmem(8, 8, 128), vmem(8, 8, 128)],
-        (on_chip(slab),),
+        (slab,),
     )
     ups = [(i * boxes + j, i * boxes + j + 1) for i in range(0, groups, 2) for j in range(boxes - 1)]
     downs = [(i * boxes + j + 1, i * boxes + j) for i in range(1, groups, 2) for j in range(boxes - 1)]

time: 80.1 us -> 79.2 us (0.989)
  blocking collectives: 26.5 us -> 25.6 us
    all_gather x4 -> x3, blocking collectives: 14.5 us -> 11 us  [on_chip(): lax.all_gather(x, 'outer', axis_index_groups=[[i, i + 1] for i in range(0...]
    all_to_all x1, blocking collectives: 11.9 us -> 14.6 us  [body(): slab = lax.all_to_all(pay, 'outer', 0, 0, tiled=True)]
  transfers between devices with their start and end apart: 7 -> 7, of which waited for: 1 -> 2; matrix products, arithmetic and copies ran while one was open for 0% -> 0% of each run, Pallas kernels for 0% -> 0%
where the time goes in v5:
time: 79.2 us; the launch traced here: 78.8 us
  starting transfers between devices  35.5 us (45%)
  blocking collectives  25.6 us (32%)
  Pallas kernels  9.04 us (11%)
  waiting for transfers between devices  6.2 us (8%)
  local copies, waits for them, and re-layouts  1.8 us (2%)
    all_to_all x1, starting transfers between devices, body(): half = lax.all_to_all(pay3, 'inner', 0, 0, tiled=True)  17.6 us
    all_to_all x1, blocking collectives, body(): slab = lax.all_to_all(pay, 'outer', 0, 0, tiled=True)  14.6 us
    all_gather x3, blocking collectives, on_chip(): lax.all_gather(x, 'outer', axis_index_groups=[[i, i + 1] for i in range(0...  11 us
    pallas_call x5, Pallas kernels, call(): pl.pallas_call(kernel, name=name, out_shape=outs, in_specs=[spec[c] for c...  9.04 us
    all_to_all x1, waiting for transfers between devices, body(): half = lax.all_to_all(pay3, 'inner', 0, 0, tiled=True)  5.93 us
    ppermute x1, starting transfers between devices, body(): odd1 = lax.ppermute(vb1, 'outer', odds)  4.7 us
    ppermute x1, starting transfers between devices, body(): from_even = lax.ppermute(to_even, 'inner', evens_y)  4.38 us
    ppermute x1, starting transfers between devices, body(): side = lax.ppermute(side, 'outer', odds)  4.05 us
  transfers between devices with their start and end apart: 7, of which 2 were waited for; matrix products, arithmetic and copies ran while one was open for 0% of the time, Pallas kernels for 0%

profile of v5, /device:TPU:1, one launch (start us, length us, event | category | flops | bytes accessed | tf_op | source)
XLA Modules:
  0.0 78.8 jit_solution(16563965748203179388)
XLA Ops:
  0.6 0.9 %copy-done = f32[8,32,128]{2,1,0:T(8,128)S(1)} copy-done((f32[8,32,128]{2,1,0:T(8,128)S(1)}, f32[8,32,128]{2,1,0:T(8,128)}, u32[]{:S(2)}) %copy-start) | copy-done | bytes 131096
  1.5 0.9 %copy-done.1 = s32[8,32,128]{2,1,0:T(8,128)S(1)} copy-done((s32[8,32,128]{2,1,0:T(8,128)S(1)}, s32[8,32,128]{2,1,0:T(8,128)}, u32[]{:S(2)}) %copy-start.1) | copy-done | bytes 131096
  2.4 0.1 prep.1
  2.5 4.4 %collective-permute-start = (f32[2,8,16,128]{3,2,1,0:T(8,128)S(1)}, f32[2,8,16,128]{3,2,1,0:T(8,128)S(1)}, u32[]{:S(2)}, u32[]{:S(2)}) collective-permute-start(f32[2,8,16,128]{3,2,1,0:T(8,128)S(1)} %get-tuple-element.27), channel_id=1, source_target_pairs={{0,1},{1,0},{2,3},{3,2},{4,5},{5,4},{6,7},{7,6},{8,9},{9,8},{10,11... | collective-permute-start | bytes 393224 | tf_op jit(solution)/shard_map/ppermute | solution.py:460
  6.9 0.7 collective-permute-start.1
  7.6 4.0 %collective-permute-start.2 = (f32[14,32,128]{2,1,0:T(8,128)S(1)}, f32[14,32,128]{2,1,0:T(8,128)S(1)}, u32[]{:S(2)}, u32[]{:S(2)}) collective-permute-start(f32[14,32,128]{2,1,0:T(8,128)S(1)} %get-tuple-element.30), channel_id=1, source_target_pairs={{16,32},{32,16},{48,64},{64,48},{80,96},{96,80},{112,128},{128,112... | collective-permute-start | bytes 688136 | tf_op jit(solution)/shard_map/ppermute | solution.py:462
  11.6 0.0 collective-permute-done.from_even_ref
  11.6 0.0 collective-permute-done.1.from_odd_ref
  11.7 2.8 %collective-permute-start.3 = (f32[320,128]{1,0:T(8,128)S(1)}, f32[320,128]{1,0:T(8,128)S(1)}, u32[]{:S(2)}, u32[]{:S(2)}) collective-permute-start(f32[320,128]{1,0:T(8,128)S(1)} %get-tuple-element.31), channel_id=1, source_target_pairs={{16,32},{32,16},{48,64},{64,48},{80,96},{96,80},{112,128},{128,112... | collective-permute-start | bytes 491528 | tf_op jit(solution)/shard_map/ppermute | solution.py:467
  14.5 4.3 %all-gather = f32[4,8,32,128]{3,2,1,0:T(8,128)S(1)} all-gather(f32[2,8,32,128]{3,2,1,0:T(8,128)S(1)} %get-tuple-element.26), channel_id=2, replica_groups={{0,16},{32,48},{64,80},{96,112},{128,144},{160,176},{192,208},{224,240}..., dimensions={0}, use_global_device_ids=true | all-gather | bytes 786432 | tf_op jit(solution)/shard_map/all_gather | solution.py:454
  18.8 2.2 %all-gather.1 = f32[4,8,32,128]{3,2,1,0:T(8,128)S(1)} all-gather(f32[2,8,32,128]{3,2,1,0:T(8,128)S(1)} %get-tuple-element.29), channel_id=3, replica_groups={{0,16},{32,48},{64,80},{96,112},{128,144},{160,176},{192,208},{224,240}..., dimensions={0}, use_global_device_ids=true | all-gather | bytes 786432 | tf_op jit(solution)/shard_map/all_gather | solution.py:454
  21.0 0.0 collective-permute-done.2.side_ref
  21.0 0.0 collective-permute-done.3.corner_ref
  21.0 3.1 %fine.1 = (f32[32,16,128]{2,1,0:T(8,128)S(1)}, f32[4,32,128]{2,1,0:T(8,128)S(1)}, f32[12,32,128]{2,1,0:T(8,128)S(1)}, f32[12,32,128]{2,1,0:T(8,128)S(1)}, f32[16...) custom-call(f32[2,2,8,32,128]{4,3,2,1,0:T(8,128)S(1)} %bitcast.5, ...), custom_call_target="tpu_custom_call" | custom-call | tf_op jit(solution)/shard_map/fine/pallas_call | solution.py:436
  24.1 14.6 %all_to_all.10.all_ref = f32[32,16,128]{2,1,0:T(8,128)S(1)} all-to-all(f32[32,16,128]{2,1,0:T(8,128)S(1)} %get-tuple-element.32), channel_id=1, replica_groups=mesh['outer'=32,'inner'=16] {'outer'}, dimensions={0} | all-to-all | bytes 524288 | tf_op jit(solution)/shard_map/all_to_all | solution.py:478
  38.7 1.9 %middle.1 = (f32[16,16,128]{2,1,0:T(8,128)}, f32[24,128]{1,0:T(8,128)S(1)}, f32[12,16,128]{2,1,0:T(8,128)S(1)}, f32[12,16,128]{2,1,0:T(8,128)S(1)}, f32[12,16,12...) custom-call(f32[32,16,128]{2,1,0:T(8,128)S(1)} %all_to_all.10.all_ref), custom_call_target="tpu_custom_call" | custom-call | tf_op jit(solution)/shard_map/middle/pallas_call | solution.py:436
  40.5 17.6 %all-to-all-start.1 = ((f32[16,16,128]{2,1,0:T(8,128)}), f32[16,16,128]{2,1,0:T(8,128)S(1)}, u32[]{:S(2)}, u32[]{:S(2)}) async-start(f32[16,16,128]{2,1,0:T(8,128)} %get-tuple-element.33), calls=%async_computation.1 | async-start | bytes 262144 | tf_op jit(solution)/shard_map/all_to_all | solution.py:492
  58.1 1.3 %collective-permute-start.4 = (f32[24,128]{1,0:T(8,128)S(1)}, f32[24,128]{1,0:T(8,128)S(1)}, u32[]{:S(2)}, u32[]{:S(2)}) collective-permute-start(f32[24,128]{1,0:T(8,128)S(1)} %get-tuple-element.36), channel_id=1, source_target_pairs={{0,1},{1,2},{2,3},{3,4},{4,5},{5,6},{6,7},{7,8},{8,9},{9,10},{10,1... | collective-permute-start | bytes 36872 | tf_op jit(solution)/shard_map/ppermute | solution.py:491
  59.4 4.7 %collective-permute-start.5 = (f32[4,32,128]{2,1,0:T(8,128)S(1)}, f32[4,32,128]{2,1,0:T(8,128)S(1)}, u32[]{:S(2)}, u32[]{:S(2)}) collective-permute-start(f32[4,32,128]{2,1,0:T(8,128)S(1)} %get-tuple-element.39), channel_id=1, source_target_pairs={{16,32},{32,16},{48,64},{64,48},{80,96},{96,80},{112,128},{128,112... | collective-permute-start | bytes 196616 | tf_op jit(solution)/shard_map/ppermute | solution.py:490
  64.2 0.3 collective-permute-done.4
  64.4 5.9 %all-to-all-done.1 = f32[16,16,128]{2,1,0:T(8,128)S(1)} async-done(((f32[16,16,128]{2,1,0:T(8,128)}), f32[16,16,128]{2,1,0:T(8,128)S(1)}, u32[]{:S(2)}, u32[]{:S(2)}) %all-to-all-start.1) | async-done | bytes 131104 | tf_op jit(solution)/shard_map/all_to_all | solution.py:492
  70.4 4.5 %all-gather.2 = f32[816,128]{1,0:T(8,128)S(1)} all-gather(f32[408,128]{1,0:T(8,128)S(1)} %pad_maximum_fusion), channel_id=4, replica_groups={{0,16},{32,48},{64,80},{96,112},{128,144},{160,176},{192,208},{224,240}..., dimensions={0}, use_global_device_ids=true | all-gather | bytes 626688 | tf_op jit(solution)/shard_map/all_gather | solution.py:454
  74.9 0.0 collective-permute-done.5.odd_ref
  74.9 4.0 %coarse.1 = (f32[8,32,128]{2,1,0:T(8,128)}, f32[8,32,128]{2,1,0:T(8,128)}) custom-call(f32[2,408,128]{2,1,0:T(8,128)S(1)} %bitcast.7, f32[12,16,128]{2,1,0:T(8,128)S(1)} %get-tuple-element.40.k2_ref, f32[12,16,128]{2,1,0:T(8,128)S(1)} %get-tuple-element.41.inv2_ref, f32[12,16,128]{2,1,0:T(8,128)S(1)} %get-tuple-element.42.b2_ref, ...), custom_call_target="tpu_custom_call" | custom-call | tf_op jit(solution)/shard_map/coarse/pallas_call | solution.py:436
  (4 shorter events, 0.1 us)
Async XLA Ops:
  0.6 0.9 %copy-start = (f32[8,32,128]{2,1,0:T(8,128)S(1)}, f32[8,32,128]{2,1,0:T(8,128)}, u32[]{:S(2)}) copy-start(f32[8,32,128]{2,1,0:T(8,128)} %b_ref.1) | copy-start | bytes 393220
  1.5 0.9 %copy-start.1 = (s32[8,32,128]{2,1,0:T(8,128)S(1)}, s32[8,32,128]{2,1,0:T(8,128)}, u32[]{:S(2)}) copy-start(s32[8,32,128]{2,1,0:T(8,128)} %codes_ref.1) | copy-start | bytes 393220
  2.5 9.1 %collective-permute-start = (f32[2,8,16,128]{3,2,1,0:T(8,128)S(1)}, f32[2,8,16,128]{3,2,1,0:T(8,128)S(1)}, u32[]{:S(2)}, u32[]{:S(2)}) collective-permute-start(f32[2,8,16,128]{3,2,1,0:T(8,128)S(1)} %get-tuple-element.27), channel_id=1, source_target_pairs={{0,1},{1,0},{2,3},{3,2},{4,5},{5,4},{6,7},{7,6},{8,9},{9,8},{10,11... | collective-permute-start | bytes 393224 | tf_op jit(solution)/shard_map/ppermute | solution.py:460
  6.9 4.7 %collective-permute-start.1 = (f32[2,8,16,128]{3,2,1,0:T(8,128)S(1)}, f32[2,8,16,128]{3,2,1,0:T(8,128)S(1)}, u32[]{:S(2)}, u32[]{:S(2)}) collective-permute-start(f32[2,8,16,128]{3,2,1,0:T(8,128)S(1)} %get-tuple-element.28), channel_id=1, source_target_pairs={{1,2},{2,1},{3,4},{4,3},{5,6},{6,5},{7,8},{8,7},{9,10},{10,9},{11,... | collective-permute-start | bytes 393224 | tf_op jit(solution)/shard_map/ppermute | solution.py:461
  7.6 13.4 %collective-permute-start.2 = (f32[14,32,128]{2,1,0:T(8,128)S(1)}, f32[14,32,128]{2,1,0:T(8,128)S(1)}, u32[]{:S(2)}, u32[]{:S(2)}) collective-permute-start(f32[14,32,128]{2,1,0:T(8,128)S(1)} %get-tuple-element.30), channel_id=1, source_target_pairs={{16,32},{32,16},{48,64},{64,48},{80,96},{96,80},{112,128},{128,112... | collective-permute-start | bytes 688136 | tf_op jit(solution)/shard_map/ppermute | solution.py:462
  11.7 9.3 %collective-permute-start.3 = (f32[320,128]{1,0:T(8,128)S(1)}, f32[320,128]{1,0:T(8,128)S(1)}, u32[]{:S(2)}, u32[]{:S(2)}) collective-permute-start(f32[320,128]{1,0:T(8,128)S(1)} %get-tuple-element.31), channel_id=1, source_target_pairs={{16,32},{32,16},{48,64},{64,48},{80,96},{96,80},{112,128},{128,112... | collective-permute-start | bytes 491528 | tf_op jit(solution)/shard_map/ppermute | solution.py:467
  40.5 29.8 %all-to-all-start.1 = ((f32[16,16,128]{2,1,0:T(8,128)}), f32[16,16,128]{2,1,0:T(8,128)S(1)}, u32[]{:S(2)}, u32[]{:S(2)}) async-start(f32[16,16,128]{2,1,0:T(8,128)} %get-tuple-element.33), calls=%async_computation.1 | async-start | bytes 262144 | tf_op jit(solution)/shard_map/all_to_all | solution.py:492
  58.1 6.3 %collective-permute-start.4 = (f32[24,128]{1,0:T(8,128)S(1)}, f32[24,128]{1,0:T(8,128)S(1)}, u32[]{:S(2)}, u32[]{:S(2)}) collective-permute-start(f32[24,128]{1,0:T(8,128)S(1)} %get-tuple-element.36), channel_id=1, source_target_pairs={{0,1},{1,2},{2,3},{3,4},{4,5},{5,6},{6,7},{7,8},{8,9},{9,10},{10,1... | collective-permute-start | bytes 36872 | tf_op jit(solution)/shard_map/ppermute | solution.py:491
  59.4 15.4 %collective-permute-start.5 = (f32[4,32,128]{2,1,0:T(8,128)S(1)}, f32[4,32,128]{2,1,0:T(8,128)S(1)}, u32[]{:S(2)}, u32[]{:S(2)}) collective-permute-start(f32[4,32,128]{2,1,0:T(8,128)S(1)} %get-tuple-element.39), channel_id=1, source_target_pairs={{16,32},{32,16},{48,64},{64,48},{80,96},{96,80},{112,128},{128,112... | collective-permute-start | bytes 196616 | tf_op jit(solution)/shard_map/ppermute | solution.py:490

commit v6 on v5

--- a/solution.py
+++ b/solution.py
@@ -134,8 +134,8 @@
 CORNER_ROWS = sum(2 * h for _, _, h in SENT)
 
 
-def sent_plane(d):
-    return jnp.where(lax.axis_index("outer") % 2 == 1, 8 - d, d - 1)
+def sent_plane(d, on_chip):
+    return jnp.where(lax.axis_index("outer") % 2 == (0 if on_chip else 1), 8 - d, d - 1)
 
 
 def prep_kernel(b_ref, codes_ref, even_ref, odd_ref, own_ref, side_ref):
@@ -147,10 +147,10 @@
         odd_ref[part] = jnp.where(up_first, low, high)
         own_ref[part] = field
     for i, (field, d, _) in enumerate(SENT):
-        side_ref[i] = own_ref[field, sent_plane(d)]
-
-
-def pack_kernel(from_even_ref, from_odd_ref, corner_ref, halo_ref):
+        side_ref[i] = own_ref[field, sent_plane(d, False)]
+
+
+def pack_kernel(from_even_ref, from_odd_ref, own_ref, corner_ref, halo_ref, chip_ref):
     up_first = lax.axis_index("inner") % 2 == 0
     for field in range(2):
         for p in range(8):
@@ -158,41 +158,42 @@
             halo_ref[field, p, 0:16, :] = jnp.where(up_first, odd, even)
             halo_ref[field, p, 16:32, :] = jnp.where(up_first, even, odd)
     first = 0
-    for field, d, h in SENT:
+    for i, (field, d, h) in enumerate(SENT):
+        chip_ref[32 * i : 32 * i + 32, :] = own_ref[field, sent_plane(d, True)]
         if h:
-            rows = halo_ref[field, sent_plane(d), 16 - h : 16 + h, :]
-            corner_ref[first : first + 2 * h, :] = rows
+            corner_ref[first : first + 2 * h, :] = halo_ref[field, sent_plane(d, False), 16 - h : 16 + h, :]
+            place = 32 * len(SENT) + first
+            chip_ref[place : place + 2 * h, :] = halo_ref[field, sent_plane(d, True), 16 - h : 16 + h, :]
             first += 2 * h
 
 
 def fine_kernel(
-    chip_ref, halo_ref, side_ref, corner_ref,
+    own_ref, halo_ref, chip_ref, side_ref, corner_ref,
     pay_ref, vb_ref, k1_ref, inv1_ref, k0_ref, b0_ref, v0_ref, inv0_ref,
     kb, ax, ay, az, inv, va, vb, tmp64, tmp32, s1, sk, b1, ax1, ay1, az1, va1, vb1,
 ):
-    right_first = lax.axis_index("outer") % 2 == 0
-    chip_first = jnp.where(right_first, 8, 0)
+    core = lax.axis_index("outer") % 2
     zeros = jnp.zeros((64, 128), F32)
-    for field, d in ((1, 7), (1, 8)):
-        kb[field, jnp.where(right_first, 8 - d, 15 + d)] = zeros
+    for place in (0, 1, 22, 23):
+        kb[1, place] = zeros
     first = 0
     for i, (field, d, h) in enumerate(SENT):
-        place = jnp.where(right_first, 8 - d, 15 + d)
-        if h < 16:
-            kb[field, place, 0:16, :] = zeros[0:16]
-            kb[field, place, 48:64, :] = zeros[0:16]
-        kb[field, place, 16:48, :] = side_ref[i]
-        if h:
-            kb[field, place, 16 - h : 16, :] = corner_ref[first : first + h, :]
-            kb[field, place, 48 : 48 + h, :] = corner_ref[first + h : first + 2 * h, :]
-            first += 2 * h
+        for on_chip in (False, True):
+            place = jnp.where(core == (1 if on_chip else 0), 8 - d, 15 + d)
+            if h < 16:
+                kb[field, place, 0:16, :] = zeros[0:16]
+                kb[field, place, 48:64, :] = zeros[0:16]
+            kb[field, place, 16:48, :] = chip_ref[1 - core, 32 * i : 32 * i + 32, :] if on_chip else side_ref[i]
+            if h:
+                corners, start = (chip_ref.at[1 - core], 32 * len(SENT) + first) if on_chip else (corner_ref, first)
+                kb[field, place, 16 - h : 16, :] = corners[start : start + h, :]
+                kb[field, place, 48 : 48 + h, :] = corners[start + h : start + 2 * h, :]
+        first += 2 * h
     for field in range(2):
-        for i in range(2):
-            for p in range(8):
-                place = chip_first + 8 * i + p
-                kb[field, place, 0:16, :] = halo_ref[i, field, p, 0:16, :]
-                kb[field, place, 16:48, :] = chip_ref[i, field, p]
-                kb[field, place, 48:64, :] = halo_ref[i, field, p, 16:32, :]
+        for p in range(8):
+            kb[field, 8 + p, 0:16, :] = halo_ref[field, p, 0:16, :]
+            kb[field, 8 + p, 16:48, :] = own_ref[field, p]
+            kb[field, 8 + p, 48:64, :] = halo_ref[field, p, 16:32, :]
 
     k, b = kb.at[0], kb.at[1]
     consts = lane_consts(64, 128)
@@ -460,20 +461,21 @@
     from_even = lax.ppermute(to_even, "inner", evens_y)
     from_odd = lax.ppermute(to_odd, "inner", odds_y)
     side = lax.ppermute(side, "outer", odds)
-    chip = on_chip(own)
-    corner, halo = call(
-        pack_kernel, "pack", "vv", [out(CORNER_ROWS, 128), out(2, 8, 32, 128)], [], (from_even, from_odd)
+    corner, halo, chip = call(
+        pack_kernel, "pack", "vvv",
+        [out(CORNER_ROWS, 128), out(2, 8, 32, 128), out(32 * len(SENT) + CORNER_ROWS, 128)], [],
+        (from_even, from_odd, own),
     )
     corner = lax.ppermute(corner, "outer", odds)
-    halo = on_chip(halo)
+    chip = on_chip(chip)
 
     fine, level1 = (24, 64, 128), (12, 32, 128)
     pay, vb1, k1, inv1, k0, b0, v0, inv0 = call(
-        fine_kernel, "fine", "vvvv",
+        fine_kernel, "fine", "vvvvv",
         [out(32, 16, 128), out(4, 32, 128), out(*level1), out(*level1)] + [out(16, 48, 128)] * 4,
         [vmem(2, *fine)] + [vmem(*fine)] * 6 + [vmem(64, 128), vmem(32, 128), vmem(256, 128), vmem(384, 128)]
         + [vmem(*level1)] * 6,
-        (chip, halo, side, corner),
+        (own, halo, chip, side, corner),
     )
     slab = lax.all_to_all(pay, "outer", 0, 0, tiled=True)
 

time: 79.2 us -> 78.5 us (level)
    all_gather x3 -> x2, blocking collectives: 11 us -> 9 us  [on_chip(): lax.all_gather(x, 'outer', axis_index_groups=[[i, i + 1] for i in range(0...]
    all_to_all x1, blocking collectives: 14.6 us -> 16.5 us  [body(): slab = lax.all_to_all(pay, 'outer', 0, 0, tiled=True)]
where the time goes in v6:
time: 78.5 us; the launch traced here: 78.1 us
  starting transfers between devices  34.8 us (44%)
  blocking collectives  25.5 us (32%)
  Pallas kernels  8.96 us (11%)
  waiting for transfers between devices  6.2 us (8%)
  local copies, waits for them, and re-layouts  1.8 us (2%)
    all_to_all x1, starting transfers between devices, body(): half = lax.all_to_all(pay3, 'inner', 0, 0, tiled=True)  17 us
    all_to_all x1, blocking collectives, body(): slab = lax.all_to_all(pay, 'outer', 0, 0, tiled=True)  16.5 us
    all_gather x2, blocking collectives, on_chip(): lax.all_gather(x, 'outer', axis_index_groups=[[i, i + 1] for i in range(0...  9 us
    pallas_call x5, Pallas kernels, call(): pl.pallas_call(kernel, name=name, out_shape=outs, in_specs=[spec[c] for c...  8.96 us
    all_to_all x1, waiting for transfers between devices, body(): half = lax.all_to_all(pay3, 'inner', 0, 0, tiled=True)  5.93 us
    ppermute x1, starting transfers between devices, body(): odd1 = lax.ppermute(vb1, 'outer', odds)  4.7 us
    ppermute x1, starting transfers between devices, body(): from_even = lax.ppermute(to_even, 'inner', evens_y)  4.38 us
    ppermute x1, starting transfers between devices, body(): side = lax.ppermute(side, 'outer', odds)  4.05 us
  transfers between devices with their start and end apart: 7, of which 2 were waited for; matrix products, arithmetic and copies ran while one was open for 0% of the time, Pallas kernels for 0%

profile of v6, /device:TPU:1, one launch (start us, length us, event | category | flops | bytes accessed | tf_op | source)
XLA Modules:
  0.0 78.1 jit_solution(18369577545444559850)
XLA Ops:
  0.6 0.9 %copy-done = f32[8,32,128]{2,1,0:T(8,128)S(1)} copy-done((f32[8,32,128]{2,1,0:T(8,128)S(1)}, f32[8,32,128]{2,1,0:T(8,128)}, u32[]{:S(2)}) %copy-start) | copy-done | bytes 131096
  1.5 0.9 %copy-done.1 = s32[8,32,128]{2,1,0:T(8,128)S(1)} copy-done((s32[8,32,128]{2,1,0:T(8,128)S(1)}, s32[8,32,128]{2,1,0:T(8,128)}, u32[]{:S(2)}) %copy-start.1) | copy-done | bytes 131096
  2.4 0.1 prep.1
  2.5 4.4 %collective-permute-start = (f32[2,8,16,128]{3,2,1,0:T(8,128)S(1)}, f32[2,8,16,128]{3,2,1,0:T(8,128)S(1)}, u32[]{:S(2)}, u32[]{:S(2)}) collective-permute-start(f32[2,8,16,128]{3,2,1,0:T(8,128)S(1)} %get-tuple-element.28), channel_id=1, source_target_pairs={{0,1},{1,0},{2,3},{3,2},{4,5},{5,4},{6,7},{7,6},{8,9},{9,8},{10,11... | collective-permute-start | bytes 393224 | tf_op jit(solution)/shard_map/ppermute | solution.py:461
  6.9 0.7 collective-permute-start.1
  7.6 4.0 %collective-permute-start.2 = (f32[14,32,128]{2,1,0:T(8,128)S(1)}, f32[14,32,128]{2,1,0:T(8,128)S(1)}, u32[]{:S(2)}, u32[]{:S(2)}) collective-permute-start(f32[14,32,128]{2,1,0:T(8,128)S(1)} %get-tuple-element.32), channel_id=1, source_target_pairs={{16,32},{32,16},{48,64},{64,48},{80,96},{96,80},{112,128},{128,112... | collective-permute-start | bytes 688136 | tf_op jit(solution)/shard_map/ppermute | solution.py:463
  11.6 0.0 collective-permute-done.from_even_ref
  11.6 0.0 collective-permute-done.1.from_odd_ref
  11.6 0.1 pack.1
  11.7 2.8 %collective-permute-start.3 = (f32[320,128]{1,0:T(8,128)S(1)}, f32[320,128]{1,0:T(8,128)S(1)}, u32[]{:S(2)}, u32[]{:S(2)}) collective-permute-start(f32[320,128]{1,0:T(8,128)S(1)} %get-tuple-element.33), channel_id=1, source_target_pairs={{16,32},{32,16},{48,64},{64,48},{80,96},{96,80},{112,128},{128,112... | collective-permute-start | bytes 491528 | tf_op jit(solution)/shard_map/ppermute | solution.py:469
  14.5 4.5 %all-gather = f32[1536,128]{1,0:T(8,128)S(1)} all-gather(f32[768,128]{1,0:T(8,128)S(1)} %get-tuple-element.31), channel_id=2, replica_groups={{0,16},{32,48},{64,80},{96,112},{128,144},{160,176},{192,208},{224,240}..., dimensions={0}, use_global_device_ids=true | all-gather | bytes 1179648 | tf_op jit(solution)/shard_map/all_gather | solution.py:455
  19.0 0.0 collective-permute-done.2.side_ref
  19.0 0.0 collective-permute-done.3.corner_ref
  19.0 3.0 %fine.1 = (f32[32,16,128]{2,1,0:T(8,128)S(1)}, f32[4,32,128]{2,1,0:T(8,128)S(1)}, f32[12,32,128]{2,1,0:T(8,128)S(1)}, f32[12,32,128]{2,1,0:T(8,128)S(1)}, f32[16...) custom-call(f32[2,8,32,128]{3,2,1,0:T(8,128)S(1)} %get-tuple-element, ...), custom_call_target="tpu_custom_call" | custom-call | tf_op jit(solution)/shard_map/fine/pallas_call | solution.py:437
  22.0 16.5 %all_to_all.10.all_ref = f32[32,16,128]{2,1,0:T(8,128)S(1)} all-to-all(f32[32,16,128]{2,1,0:T(8,128)S(1)} %get-tuple-element.34), channel_id=1, replica_groups=mesh['outer'=32,'inner'=16] {'outer'}, dimensions={0} | all-to-all | bytes 524288 | tf_op jit(solution)/shard_map/all_to_all | solution.py:480
  38.6 1.9 %middle.1 = (f32[16,16,128]{2,1,0:T(8,128)}, f32[24,128]{1,0:T(8,128)S(1)}, f32[12,16,128]{2,1,0:T(8,128)S(1)}, f32[12,16,128]{2,1,0:T(8,128)S(1)}, f32[12,16,12...) custom-call(f32[32,16,128]{2,1,0:T(8,128)S(1)} %all_to_all.10.all_ref), custom_call_target="tpu_custom_call" | custom-call | tf_op jit(solution)/shard_map/middle/pallas_call | solution.py:437
  40.4 17.0 %all-to-all-start.1 = ((f32[16,16,128]{2,1,0:T(8,128)}), f32[16,16,128]{2,1,0:T(8,128)S(1)}, u32[]{:S(2)}, u32[]{:S(2)}) async-start(f32[16,16,128]{2,1,0:T(8,128)} %get-tuple-element.35), calls=%async_computation.1 | async-start | bytes 262144 | tf_op jit(solution)/shard_map/all_to_all | solution.py:494
  57.4 1.3 %collective-permute-start.4 = (f32[24,128]{1,0:T(8,128)S(1)}, f32[24,128]{1,0:T(8,128)S(1)}, u32[]{:S(2)}, u32[]{:S(2)}) collective-permute-start(f32[24,128]{1,0:T(8,128)S(1)} %get-tuple-element.38), channel_id=1, source_target_pairs={{0,1},{1,2},{2,3},{3,4},{4,5},{5,6},{6,7},{7,8},{8,9},{9,10},{10,1... | collective-permute-start | bytes 36872 | tf_op jit(solution)/shard_map/ppermute | solution.py:493
  58.7 4.7 %collective-permute-start.5 = (f32[4,32,128]{2,1,0:T(8,128)S(1)}, f32[4,32,128]{2,1,0:T(8,128)S(1)}, u32[]{:S(2)}, u32[]{:S(2)}) collective-permute-start(f32[4,32,128]{2,1,0:T(8,128)S(1)} %get-tuple-element.41), channel_id=1, source_target_pairs={{16,32},{32,16},{48,64},{64,48},{80,96},{96,80},{112,128},{128,112... | collective-permute-start | bytes 196616 | tf_op jit(solution)/shard_map/ppermute | solution.py:492
  63.4 0.3 collective-permute-done.4
  63.7 5.9 %all-to-all-done.1 = f32[16,16,128]{2,1,0:T(8,128)S(1)} async-done(((f32[16,16,128]{2,1,0:T(8,128)}), f32[16,16,128]{2,1,0:T(8,128)S(1)}, u32[]{:S(2)}, u32[]{:S(2)}) %all-to-all-start.1) | async-done | bytes 131104 | tf_op jit(solution)/shard_map/all_to_all | solution.py:494
  69.6 4.5 %all-gather.1 = f32[816,128]{1,0:T(8,128)S(1)} all-gather(f32[408,128]{1,0:T(8,128)S(1)} %pad_maximum_fusion), channel_id=3, replica_groups={{0,16},{32,48},{64,80},{96,112},{128,144},{160,176},{192,208},{224,240}..., dimensions={0}, use_global_device_ids=true | all-gather | bytes 626688 | tf_op jit(solution)/shard_map/all_gather | solution.py:455
  74.1 0.0 collective-permute-done.5.odd_ref
  74.1 4.0 %coarse.1 = (f32[8,32,128]{2,1,0:T(8,128)}, f32[8,32,128]{2,1,0:T(8,128)}) custom-call(f32[2,408,128]{2,1,0:T(8,128)S(1)} %bitcast.5, f32[12,16,128]{2,1,0:T(8,128)S(1)} %get-tuple-element.42.k2_ref, f32[12,16,128]{2,1,0:T(8,128)S(1)} %get-tuple-element.43.inv2_ref, f32[12,16,128]{2,1,0:T(8,128)S(1)} %get-tuple-element.44.b2_ref, ...), custom_call_target="tpu_custom_call" | custom-call | tf_op jit(solution)/shard_map/coarse/pallas_call | solution.py:437
  (3 shorter events, 0.0 us)
Async XLA Ops:
  0.6 0.9 %copy-start = (f32[8,32,128]{2,1,0:T(8,128)S(1)}, f32[8,32,128]{2,1,0:T(8,128)}, u32[]{:S(2)}) copy-start(f32[8,32,128]{2,1,0:T(8,128)} %b_ref.1) | copy-start | bytes 393220
  1.5 0.9 %copy-start.1 = (s32[8,32,128]{2,1,0:T(8,128)S(1)}, s32[8,32,128]{2,1,0:T(8,128)}, u32[]{:S(2)}) copy-start(s32[8,32,128]{2,1,0:T(8,128)} %codes_ref.1) | copy-start | bytes 393220
  2.5 9.1 %collective-permute-start = (f32[2,8,16,128]{3,2,1,0:T(8,128)S(1)}, f32[2,8,16,128]{3,2,1,0:T(8,128)S(1)}, u32[]{:S(2)}, u32[]{:S(2)}) collective-permute-start(f32[2,8,16,128]{3,2,1,0:T(8,128)S(1)} %get-tuple-element.28), channel_id=1, source_target_pairs={{0,1},{1,0},{2,3},{3,2},{4,5},{5,4},{6,7},{7,6},{8,9},{9,8},{10,11... | collective-permute-start | bytes 393224 | tf_op jit(solution)/shard_map/ppermute | solution.py:461
  6.9 4.7 %collective-permute-start.1 = (f32[2,8,16,128]{3,2,1,0:T(8,128)S(1)}, f32[2,8,16,128]{3,2,1,0:T(8,128)S(1)}, u32[]{:S(2)}, u32[]{:S(2)}) collective-permute-start(f32[2,8,16,128]{3,2,1,0:T(8,128)S(1)} %get-tuple-element.29), channel_id=1, source_target_pairs={{1,2},{2,1},{3,4},{4,3},{5,6},{6,5},{7,8},{8,7},{9,10},{10,9},{11,... | collective-permute-start | bytes 393224 | tf_op jit(solution)/shard_map/ppermute | solution.py:462
  7.6 11.4 %collective-permute-start.2 = (f32[14,32,128]{2,1,0:T(8,128)S(1)}, f32[14,32,128]{2,1,0:T(8,128)S(1)}, u32[]{:S(2)}, u32[]{:S(2)}) collective-permute-start(f32[14,32,128]{2,1,0:T(8,128)S(1)} %get-tuple-element.32), channel_id=1, source_target_pairs={{16,32},{32,16},{48,64},{64,48},{80,96},{96,80},{112,128},{128,112... | collective-permute-start | bytes 688136 | tf_op jit(solution)/shard_map/ppermute | solution.py:463
  11.7 7.3 %collective-permute-start.3 = (f32[320,128]{1,0:T(8,128)S(1)}, f32[320,128]{1,0:T(8,128)S(1)}, u32[]{:S(2)}, u32[]{:S(2)}) collective-permute-start(f32[320,128]{1,0:T(8,128)S(1)} %get-tuple-element.33), channel_id=1, source_target_pairs={{16,32},{32,16},{48,64},{64,48},{80,96},{96,80},{112,128},{128,112... | collective-permute-start | bytes 491528 | tf_op jit(solution)/shard_map/ppermute | solution.py:469
  40.4 29.2 %all-to-all-start.1 = ((f32[16,16,128]{2,1,0:T(8,128)}), f32[16,16,128]{2,1,0:T(8,128)S(1)}, u32[]{:S(2)}, u32[]{:S(2)}) async-start(f32[16,16,128]{2,1,0:T(8,128)} %get-tuple-element.35), calls=%async_computation.1 | async-start | bytes 262144 | tf_op jit(solution)/shard_map/all_to_all | solution.py:494
  57.4 6.3 %collective-permute-start.4 = (f32[24,128]{1,0:T(8,128)S(1)}, f32[24,128]{1,0:T(8,128)S(1)}, u32[]{:S(2)}, u32[]{:S(2)}) collective-permute-start(f32[24,128]{1,0:T(8,128)S(1)} %get-tuple-element.38), channel_id=1, source_target_pairs={{0,1},{1,2},{2,3},{3,4},{4,5},{5,6},{6,7},{7,8},{8,9},{9,10},{10,1... | collective-permute-start | bytes 36872 | tf_op jit(solution)/shard_map/ppermute | solution.py:493
  58.7 15.4 %collective-permute-start.5 = (f32[4,32,128]{2,1,0:T(8,128)S(1)}, f32[4,32,128]{2,1,0:T(8,128)S(1)}, u32[]{:S(2)}, u32[]{:S(2)}) collective-permute-start(f32[4,32,128]{2,1,0:T(8,128)S(1)} %get-tuple-element.41), channel_id=1, source_target_pairs={{16,32},{32,16},{48,64},{64,48},{80,96},{96,80},{112,128},{128,112... | collective-permute-start | bytes 196616 | tf_op jit(solution)/shard_map/ppermute | solution.py:492

commit v7 on v6

--- a/solution.py
+++ b/solution.py
@@ -21,7 +21,14 @@
 
 
 def dot(a, b):
-    return jnp.dot(a, b, precision=lax.Precision.HIGHEST, preferred_element_type=F32)
+    b = b.astype(jnp.bfloat16)
+    total = None
+    for _ in range(3):
+        part = a.astype(jnp.bfloat16)
+        a = a - part.astype(F32)
+        product = jnp.dot(part, b, preferred_element_type=F32)
+        total = product if total is None else total + product
+    return total
 
 
 def lane_consts(rows, group, domain_rows=False):
@@ -320,7 +327,7 @@
 
 
 def coarse_kernel(
-    chip_ref, k2_ref, inv2_ref, b2_ref, v2_ref, odd_ref, k1_ref, inv1_ref,
+    half_ref, edges_ref, k2_ref, inv2_ref, b2_ref, v2_ref, odd_ref, k1_ref, inv1_ref,
     k0, b0, v0_ref, inv0, v_out, r_out,
     k3, b3, ax3, ay3, az3, inv3, va3, vb3, c3, tmp16, ax2, ay2, az2, va2, vb2, b2,
     tmp32, b1, va1, vb1, ax1, ay1, az1, tmp64, c1, v0, ax0, ay0, az0, w0,
@@ -329,8 +336,8 @@
 
     for i in range(16):
         for t in range(4):
-            b3[t + 1, 4 * i : 4 * i + 4, :] = chip_ref[0, 16 * i + 4 * t : 16 * i + 4 * t + 4, :]
-            k3[t + 1, 4 * i : 4 * i + 4, :] = chip_ref[1, 16 * i + 4 * t : 16 * i + 4 * t + 4, :]
+            b3[t + 1, 4 * i : 4 * i + 4, :] = half_ref[0, i, 4 * t : 4 * t + 4, :]
+            k3[t + 1, 4 * i : 4 * i + 4, :] = half_ref[1, i, 4 * t : 4 * t + 4, :]
     ghosts(k3, 6, 16)
     b3[0] = jnp.zeros((64, 128), F32)
     consts3 = lane_consts(64, 16, True)
@@ -370,7 +377,7 @@
     lane = iota((16, 128), 1)
     for q in range(12):
         rows = twice_rows(tmp16, wide[8 * (q // 2) : 8 * (q // 2) + 8])
-        below, above = (chip_ref[i, 256 + 4 * (q % 6) : 260 + 4 * (q % 6), :] for i in range(2))
+        below, above = (edges_ref[i, 4 * (q % 6) : 4 * (q % 6) + 4, :] for i in range(2))
         if q >= 6:
             below, above = roll(below, 64, 1), roll(above, 64, 1)
         v2 = jnp.concatenate([below, v2_ref[q, 4:12, :], above], axis=0)
@@ -387,7 +394,7 @@
     for q in range(6):
         rows = twice_rows(tmp32, wide[16 * q : 16 * q + 16])
         for p in (2 * q, 2 * q + 1):
-            first, second = (chip_ref[i, 280 + 32 * (p % 4) : 312 + 32 * (p % 4), :] for i in range(2))
+            first, second = (edges_ref[i, 24 + 32 * (p % 4) : 56 + 32 * (p % 4), :] for i in range(2))
             if p < 4:
                 both = jnp.where(left_is_odd, odd_ref[p], first)
             elif p < 8:
@@ -492,17 +499,17 @@
     odd1 = lax.ppermute(vb1, "outer", odds)
     edge = lax.ppermute(edge, ("outer", "inner"), ups + downs)
     half = lax.all_to_all(pay3, "inner", 0, 0, tiled=True)
-    half, edge = lax.optimization_barrier((half, edge))
-    chip = on_chip(jnp.concatenate([half.reshape(256, 128), edge, vb1.reshape(128, 128)], axis=0))
+    edges = on_chip(jnp.concatenate([edge, vb1.reshape(128, 128)], axis=0))
+    half, edges = lax.optimization_barrier((half, edges))
 
     level3, window = (6, 64, 128), (16, 48, 128)
     return call(
-        coarse_kernel, "coarse", "v" * 12,
+        coarse_kernel, "coarse", "v" * 13,
         [out(8, 32, 128)] * 2,
         [vmem(*level3)] * 8 + [vmem(4, 80, 128), vmem(16, 128)] + [vmem(*window2)] * 6
         + [vmem(32, 128)] + [vmem(*level1)] * 6 + [vmem(64, 128), vmem(256, 128)]
         + [vmem(*window)] * 5,
-        (chip, k2, inv2, b2, v2, odd1, k1, inv1, k0, b0, v0, inv0),
+        (on_chip(half), edges, k2, inv2, b2, v2, odd1, k1, inv1, k0, b0, v0, inv0),
     )
 
 

time: 78.5 us -> 78.1 us (level)
  waiting for transfers between devices: 6.2 us -> 4.29 us
  blocking collectives: 25.5 us -> 27.3 us
    all_to_all x1, waiting for transfers between devices: 5.93 us -> 4.02 us  [body(): half = lax.all_to_all(pay3, 'inner', 0, 0, tiled=True)]
    all_gather x2 -> x3, blocking collectives: 9 us -> 10.8 us  [on_chip(): lax.all_gather(x, 'outer', axis_index_groups=[[i, i + 1] for i in range(0...]
where the time goes in v7:
time: 78.1 us; the launch traced here: 77.7 us
  starting transfers between devices  34.8 us (45%)
  blocking collectives  27.3 us (35%)
  Pallas kernels  8.73 us (11%)
  waiting for transfers between devices  4.29 us (5%)
  local copies, waits for them, and re-layouts  1.8 us (2%)
    all_to_all x1, starting transfers between devices, body(): half = lax.all_to_all(pay3, 'inner', 0, 0, tiled=True)  17 us
    all_to_all x1, blocking collectives, body(): slab = lax.all_to_all(pay, 'outer', 0, 0, tiled=True)  16.5 us
    all_gather x3, blocking collectives, on_chip(): lax.all_gather(x, 'outer', axis_index_groups=[[i, i + 1] for i in range(0...  10.8 us
    pallas_call x5, Pallas kernels, call(): pl.pallas_call(kernel, name=name, out_shape=outs, in_specs=[spec[c] for c...  8.73 us
    ppermute x1, starting transfers between devices, body(): odd1 = lax.ppermute(vb1, 'outer', odds)  4.7 us
    ppermute x1, starting transfers between devices, body(): from_even = lax.ppermute(to_even, 'inner', evens_y)  4.38 us
    ppermute x1, starting transfers between devices, body(): side = lax.ppermute(side, 'outer', odds)  4.05 us
    all_to_all x1, waiting for transfers between devices, body(): half = lax.all_to_all(pay3, 'inner', 0, 0, tiled=True)  4.02 us
  transfers between devices with their start and end apart: 7, of which 2 were waited for; matrix products, arithmetic and copies ran while one was open for 0% of the time, Pallas kernels for 0%

profile of v7, /device:TPU:1, one launch (start us, length us, event | category | flops | bytes accessed | tf_op | source)
XLA Modules:
  0.0 77.7 jit_solution(17448157517229364496)
XLA Ops:
  0.6 0.9 %copy-done = f32[8,32,128]{2,1,0:T(8,128)S(1)} copy-done((f32[8,32,128]{2,1,0:T(8,128)S(1)}, f32[8,32,128]{2,1,0:T(8,128)}, u32[]{:S(2)}) %copy-start) | copy-done | bytes 131096
  1.5 0.9 %copy-done.1 = s32[8,32,128]{2,1,0:T(8,128)S(1)} copy-done((s32[8,32,128]{2,1,0:T(8,128)S(1)}, s32[8,32,128]{2,1,0:T(8,128)}, u32[]{:S(2)}) %copy-start.1) | copy-done | bytes 131096
  2.4 0.1 prep.1
  2.5 4.4 %collective-permute-start = (f32[2,8,16,128]{3,2,1,0:T(8,128)S(1)}, f32[2,8,16,128]{3,2,1,0:T(8,128)S(1)}, u32[]{:S(2)}, u32[]{:S(2)}) collective-permute-start(f32[2,8,16,128]{3,2,1,0:T(8,128)S(1)} %get-tuple-element.28), channel_id=1, source_target_pairs={{0,1},{1,0},{2,3},{3,2},{4,5},{5,4},{6,7},{7,6},{8,9},{9,8},{10,11... | collective-permute-start | bytes 393224 | tf_op jit(solution)/shard_map/ppermute | solution.py:468
  6.9 0.7 collective-permute-start.1
  7.6 4.0 %collective-permute-start.2 = (f32[14,32,128]{2,1,0:T(8,128)S(1)}, f32[14,32,128]{2,1,0:T(8,128)S(1)}, u32[]{:S(2)}, u32[]{:S(2)}) collective-permute-start(f32[14,32,128]{2,1,0:T(8,128)S(1)} %get-tuple-element.32), channel_id=1, source_target_pairs={{16,32},{32,16},{48,64},{64,48},{80,96},{96,80},{112,128},{128,112... | collective-permute-start | bytes 688136 | tf_op jit(solution)/shard_map/ppermute | solution.py:470
  11.6 0.0 collective-permute-done.from_even_ref
  11.6 0.0 collective-permute-done.1.from_odd_ref
  11.6 0.1 pack.1
  11.7 2.8 %collective-permute-start.3 = (f32[320,128]{1,0:T(8,128)S(1)}, f32[320,128]{1,0:T(8,128)S(1)}, u32[]{:S(2)}, u32[]{:S(2)}) collective-permute-start(f32[320,128]{1,0:T(8,128)S(1)} %get-tuple-element.33), channel_id=1, source_target_pairs={{16,32},{32,16},{48,64},{64,48},{80,96},{96,80},{112,128},{128,112... | collective-permute-start | bytes 491528 | tf_op jit(solution)/shard_map/ppermute | solution.py:476
  14.5 4.5 %all-gather = f32[1536,128]{1,0:T(8,128)S(1)} all-gather(f32[768,128]{1,0:T(8,128)S(1)} %get-tuple-element.31), channel_id=2, replica_groups={{0,16},{32,48},{64,80},{96,112},{128,144},{160,176},{192,208},{224,240}..., dimensions={0}, use_global_device_ids=true | all-gather | bytes 1179648 | tf_op jit(solution)/shard_map/all_gather | solution.py:462
  19.0 0.0 collective-permute-done.2.side_ref
  19.0 0.0 collective-permute-done.3.corner_ref
  19.0 2.8 %fine.1 = (f32[32,16,128]{2,1,0:T(8,128)S(1)}, f32[4,32,128]{2,1,0:T(8,128)S(1)}, f32[12,32,128]{2,1,0:T(8,128)S(1)}, f32[12,32,128]{2,1,0:T(8,128)S(1)}, f32[16...) custom-call(f32[2,8,32,128]{3,2,1,0:T(8,128)S(1)} %get-tuple-element, ...), custom_call_target="tpu_custom_call" | custom-call | tf_op jit(solution)/shard_map/fine/pallas_call | solution.py:444
  21.9 16.5 %all_to_all.10.all_ref = f32[32,16,128]{2,1,0:T(8,128)S(1)} all-to-all(f32[32,16,128]{2,1,0:T(8,128)S(1)} %get-tuple-element.34), channel_id=1, replica_groups=mesh['outer'=32,'inner'=16] {'outer'}, dimensions={0} | all-to-all | bytes 524288 | tf_op jit(solution)/shard_map/all_to_all | solution.py:487
  38.4 1.9 %middle.1 = (f32[16,16,128]{2,1,0:T(8,128)}, f32[24,128]{1,0:T(8,128)S(1)}, f32[12,16,128]{2,1,0:T(8,128)S(1)}, f32[12,16,128]{2,1,0:T(8,128)S(1)}, f32[12,16,12...) custom-call(f32[32,16,128]{2,1,0:T(8,128)S(1)} %all_to_all.10.all_ref), custom_call_target="tpu_custom_call" | custom-call | tf_op jit(solution)/shard_map/middle/pallas_call | solution.py:444
  40.3 17.0 %all-to-all-start.1 = ((f32[16,16,128]{2,1,0:T(8,128)}), f32[16,16,128]{2,1,0:T(8,128)S(1)}, u32[]{:S(2)}, u32[]{:S(2)}) async-start(f32[16,16,128]{2,1,0:T(8,128)} %get-tuple-element.35), calls=%async_computation.1 | async-start | bytes 262144 | tf_op jit(solution)/shard_map/all_to_all | solution.py:501
  57.2 1.3 %collective-permute-start.4 = (f32[24,128]{1,0:T(8,128)S(1)}, f32[24,128]{1,0:T(8,128)S(1)}, u32[]{:S(2)}, u32[]{:S(2)}) collective-permute-start(f32[24,128]{1,0:T(8,128)S(1)} %get-tuple-element.38), channel_id=1, source_target_pairs={{0,1},{1,2},{2,3},{3,4},{4,5},{5,6},{6,7},{7,8},{8,9},{9,10},{10,1... | collective-permute-start | bytes 36872 | tf_op jit(solution)/shard_map/ppermute | solution.py:500
  58.5 4.7 %collective-permute-start.5 = (f32[4,32,128]{2,1,0:T(8,128)S(1)}, f32[4,32,128]{2,1,0:T(8,128)S(1)}, u32[]{:S(2)}, u32[]{:S(2)}) collective-permute-start(f32[4,32,128]{2,1,0:T(8,128)S(1)} %get-tuple-element.39), channel_id=1, source_target_pairs={{16,32},{32,16},{48,64},{64,48},{80,96},{96,80},{112,128},{128,112... | collective-permute-start | bytes 196616 | tf_op jit(solution)/shard_map/ppermute | solution.py:499
  63.2 0.3 collective-permute-done.4
  63.5 1.9 %all-gather.1 = f32[304,128]{1,0:T(8,128)S(1)} all-gather(f32[152,128]{1,0:T(8,128)S(1)} %pad_maximum_fusion), channel_id=3, replica_groups={{0,16},{32,48},{64,80},{96,112},{128,144},{160,176},{192,208},{224,240}..., dimensions={0}, use_global_device_ids=true | all-gather | bytes 233472 | tf_op jit(solution)/shard_map/all_gather | solution.py:462
  65.4 4.0 %all-to-all-done.1 = f32[16,16,128]{2,1,0:T(8,128)S(1)} async-done(((f32[16,16,128]{2,1,0:T(8,128)}), f32[16,16,128]{2,1,0:T(8,128)S(1)}, u32[]{:S(2)}, u32[]{:S(2)}) %all-to-all-start.1) | async-done | bytes 131104 | tf_op jit(solution)/shard_map/all_to_all | solution.py:501
  69.4 4.4 %all-gather.2 = f32[32,16,128]{2,1,0:T(8,128)S(1)} all-gather(f32[16,16,128]{2,1,0:T(8,128)S(1)} %all-to-all-done.1), channel_id=4, replica_groups={{0,16},{32,48},{64,80},{96,112},{128,144},{160,176},{192,208},{224,240}..., dimensions={0}, use_global_device_ids=true | all-gather | bytes 393216 | tf_op jit(solution)/shard_map/all_gather | solution.py:462
  73.8 3.9 %coarse.1 = (f32[8,32,128]{2,1,0:T(8,128)}, f32[8,32,128]{2,1,0:T(8,128)}) custom-call(f32[2,16,16,128]{3,2,1,0:T(8,128)S(1)} %bitcast.5, f32[2,152,128]{2,1,0:T(8,128)S(1)} %bitcast.6, f32[12,16,128]{2,1,0:T(8,128)S(1)} %get-tuple-element.42.k2_ref, f32[12,16,128]{2,1,0:T(8,128)S(1)} %get-tuple-element.43.inv2_ref, ...), custom_call_target="tpu_custom_call" | custom-call | tf_op jit(solution)/shard_map/coarse/pallas_call | solution.py:444
  (4 shorter events, 0.0 us)
Async XLA Ops:
  0.6 0.9 %copy-start = (f32[8,32,128]{2,1,0:T(8,128)S(1)}, f32[8,32,128]{2,1,0:T(8,128)}, u32[]{:S(2)}) copy-start(f32[8,32,128]{2,1,0:T(8,128)} %b_ref.1) | copy-start | bytes 393220
  1.5 0.9 %copy-start.1 = (s32[8,32,128]{2,1,0:T(8,128)S(1)}, s32[8,32,128]{2,1,0:T(8,128)}, u32[]{:S(2)}) copy-start(s32[8,32,128]{2,1,0:T(8,128)} %codes_ref.1) | copy-start | bytes 393220
  2.5 9.1 %collective-permute-start = (f32[2,8,16,128]{3,2,1,0:T(8,128)S(1)}, f32[2,8,16,128]{3,2,1,0:T(8,128)S(1)}, u32[]{:S(2)}, u32[]{:S(2)}) collective-permute-start(f32[2,8,16,128]{3,2,1,0:T(8,128)S(1)} %get-tuple-element.28), channel_id=1, source_target_pairs={{0,1},{1,0},{2,3},{3,2},{4,5},{5,4},{6,7},{7,6},{8,9},{9,8},{10,11... | collective-permute-start | bytes 393224 | tf_op jit(solution)/shard_map/ppermute | solution.py:468
  6.9 4.7 %collective-permute-start.1 = (f32[2,8,16,128]{3,2,1,0:T(8,128)S(1)}, f32[2,8,16,128]{3,2,1,0:T(8,128)S(1)}, u32[]{:S(2)}, u32[]{:S(2)}) collective-permute-start(f32[2,8,16,128]{3,2,1,0:T(8,128)S(1)} %get-tuple-element.29), channel_id=1, source_target_pairs={{1,2},{2,1},{3,4},{4,3},{5,6},{6,5},{7,8},{8,7},{9,10},{10,9},{11,... | collective-permute-start | bytes 393224 | tf_op jit(solution)/shard_map/ppermute | solution.py:469
  7.6 11.4 %collective-permute-start.2 = (f32[14,32,128]{2,1,0:T(8,128)S(1)}, f32[14,32,128]{2,1,0:T(8,128)S(1)}, u32[]{:S(2)}, u32[]{:S(2)}) collective-permute-start(f32[14,32,128]{2,1,0:T(8,128)S(1)} %get-tuple-element.32), channel_id=1, source_target_pairs={{16,32},{32,16},{48,64},{64,48},{80,96},{96,80},{112,128},{128,112... | collective-permute-start | bytes 688136 | tf_op jit(solution)/shard_map/ppermute | solution.py:470
  11.7 7.3 %collective-permute-start.3 = (f32[320,128]{1,0:T(8,128)S(1)}, f32[320,128]{1,0:T(8,128)S(1)}, u32[]{:S(2)}, u32[]{:S(2)}) collective-permute-start(f32[320,128]{1,0:T(8,128)S(1)} %get-tuple-element.33), channel_id=1, source_target_pairs={{16,32},{32,16},{48,64},{64,48},{80,96},{96,80},{112,128},{128,112... | collective-permute-start | bytes 491528 | tf_op jit(solution)/shard_map/ppermute | solution.py:476
  40.3 29.2 %all-to-all-start.1 = ((f32[16,16,128]{2,1,0:T(8,128)}), f32[16,16,128]{2,1,0:T(8,128)S(1)}, u32[]{:S(2)}, u32[]{:S(2)}) async-start(f32[16,16,128]{2,1,0:T(8,128)} %get-tuple-element.35), calls=%async_computation.1 | async-start | bytes 262144 | tf_op jit(solution)/shard_map/all_to_all | solution.py:501
  57.2 6.3 %collective-permute-start.4 = (f32[24,128]{1,0:T(8,128)S(1)}, f32[24,128]{1,0:T(8,128)S(1)}, u32[]{:S(2)}, u32[]{:S(2)}) collective-permute-start(f32[24,128]{1,0:T(8,128)S(1)} %get-tuple-element.38), channel_id=1, source_target_pairs={{0,1},{1,2},{2,3},{3,4},{4,5},{5,6},{6,7},{7,8},{8,9},{9,10},{10,1... | collective-permute-start | bytes 36872 | tf_op jit(solution)/shard_map/ppermute | solution.py:500
  58.5 15.3 %collective-permute-start.5 = (f32[4,32,128]{2,1,0:T(8,128)S(1)}, f32[4,32,128]{2,1,0:T(8,128)S(1)}, u32[]{:S(2)}, u32[]{:S(2)}) collective-permute-start(f32[4,32,128]{2,1,0:T(8,128)S(1)} %get-tuple-element.39), channel_id=1, source_target_pairs={{16,32},{32,16},{48,64},{64,48},{80,96},{96,80},{112,128},{128,112... | collective-permute-start | bytes 196616 | tf_op jit(solution)/shard_map/ppermute | solution.py:499

commit v8 on v7

--- a/solution.py
+++ b/solution.py
@@ -136,8 +136,8 @@
     return jnp.where(iota((128, 128), 1) == target(iota((128, 128), 0)), weight, 0.0).astype(F32)
 
 
-SENT = [(0, d, h) for d, h in zip(range(1, 9), (16, 16, 12, 12, 12, 12, 8, 0))]
-SENT += [(1, d, h) for d, h in zip(range(1, 7), (16, 12, 12, 12, 12, 8))]
+SENT = [(0, d, h) for d, h in zip(range(1, 9), (14, 14, 12, 12, 10, 10, 8, 0))]
+SENT += [(1, d, h) for d, h in zip(range(1, 7), (14, 12, 12, 10, 10, 8))]
 CORNER_ROWS = sum(2 * h for _, _, h in SENT)
 
 

time: 78.1 us -> 78 us (level)
  no operation moved by 1% of the time
where the time goes in v8:
time: 78 us; the launch traced here: 77.6 us
  starting transfers between devices  34.8 us (45%)
  blocking collectives  27.2 us (35%)
  Pallas kernels  8.75 us (11%)
  waiting for transfers between devices  4.29 us (6%)
  local copies, waits for them, and re-layouts  1.8 us (2%)
    all_to_all x1, starting transfers between devices, body(): half = lax.all_to_all(pay3, 'inner', 0, 0, tiled=True)  17 us
    all_to_all x1, blocking collectives, body(): slab = lax.all_to_all(pay, 'outer', 0, 0, tiled=True)  16.4 us
    all_gather x3, blocking collectives, on_chip(): lax.all_gather(x, 'outer', axis_index_groups=[[i, i + 1] for i in range(0...  10.8 us
    pallas_call x5, Pallas kernels, call(): pl.pallas_call(kernel, name=name, out_shape=outs, in_specs=[spec[c] for c...  8.75 us
    ppermute x1, starting transfers between devices, body(): odd1 = lax.ppermute(vb1, 'outer', odds)  4.7 us
    ppermute x1, starting transfers between devices, body(): from_even = lax.ppermute(to_even, 'inner', evens_y)  4.38 us
    ppermute x1, starting transfers between devices, body(): side = lax.ppermute(side, 'outer', odds)  4.05 us
    all_to_all x1, waiting for transfers between devices, body(): half = lax.all_to_all(pay3, 'inner', 0, 0, tiled=True)  4.02 us
  transfers between devices with their start and end apart: 7, of which 2 were waited for; matrix products, arithmetic and copies ran while one was open for 0% of the time, Pallas kernels for 0%

profile of v8, /device:TPU:1, one launch (start us, length us, event | category | flops | bytes accessed | tf_op | source)
XLA Modules:
  0.0 77.6 jit_solution(1930190485049103819)
XLA Ops:
  0.6 0.9 %copy-done = f32[8,32,128]{2,1,0:T(8,128)S(1)} copy-done((f32[8,32,128]{2,1,0:T(8,128)S(1)}, f32[8,32,128]{2,1,0:T(8,128)}, u32[]{:S(2)}) %copy-start) | copy-done | bytes 131096
  1.5 0.9 %copy-done.1 = s32[8,32,128]{2,1,0:T(8,128)S(1)} copy-done((s32[8,32,128]{2,1,0:T(8,128)S(1)}, s32[8,32,128]{2,1,0:T(8,128)}, u32[]{:S(2)}) %copy-start.1) | copy-done | bytes 131096
  2.4 0.1 prep.1
  2.5 4.4 %collective-permute-start = (f32[2,8,16,128]{3,2,1,0:T(8,128)S(1)}, f32[2,8,16,128]{3,2,1,0:T(8,128)S(1)}, u32[]{:S(2)}, u32[]{:S(2)}) collective-permute-start(f32[2,8,16,128]{3,2,1,0:T(8,128)S(1)} %get-tuple-element.28), channel_id=1, source_target_pairs={{0,1},{1,0},{2,3},{3,2},{4,5},{5,4},{6,7},{7,6},{8,9},{9,8},{10,11... | collective-permute-start | bytes 393224 | tf_op jit(solution)/shard_map/ppermute | solution.py:468
  6.9 0.7 collective-permute-start.1
  7.6 4.0 %collective-permute-start.2 = (f32[14,32,128]{2,1,0:T(8,128)S(1)}, f32[14,32,128]{2,1,0:T(8,128)S(1)}, u32[]{:S(2)}, u32[]{:S(2)}) collective-permute-start(f32[14,32,128]{2,1,0:T(8,128)S(1)} %get-tuple-element.32), channel_id=1, source_target_pairs={{16,32},{32,16},{48,64},{64,48},{80,96},{96,80},{112,128},{128,112... | collective-permute-start | bytes 688136 | tf_op jit(solution)/shard_map/ppermute | solution.py:470
  11.6 0.0 collective-permute-done.from_even_ref
  11.6 0.1 pack.1
  11.7 2.8 %collective-permute-start.3 = (f32[292,128]{1,0:T(8,128)S(1)}, f32[292,128]{1,0:T(8,128)S(1)}, u32[]{:S(2)}, u32[]{:S(2)}) collective-permute-start(f32[292,128]{1,0:T(8,128)S(1)} %get-tuple-element.33), channel_id=1, source_target_pairs={{16,32},{32,16},{48,64},{64,48},{80,96},{96,80},{112,128},{128,112... | collective-permute-start | bytes 448520 | tf_op jit(solution)/shard_map/ppermute | solution.py:476
  14.5 4.5 %all-gather.3.chip_ref = f32[2,740,128]{2,1,0:T(8,128)S(1)} all-gather(f32[1,740,128]{2,1,0:T(8,128)S(1)} %bitcast.6), channel_id=2, replica_groups={{0,16},{32,48},{64,80},{96,112},{128,144},{160,176},{192,208},{224,240}..., dimensions={0}, use_global_device_ids=true | all-gather | bytes 1136640 | tf_op jit(solution)/shard_map/all_gather | solution.py:462
  19.0 0.0 collective-permute-done.2.side_ref
  19.0 0.0 collective-permute-done.3.corner_ref
  19.0 2.9 %fine.1 = (f32[32,16,128]{2,1,0:T(8,128)S(1)}, f32[4,32,128]{2,1,0:T(8,128)S(1)}, f32[12,32,128]{2,1,0:T(8,128)S(1)}, f32[12,32,128]{2,1,0:T(8,128)S(1)}, f32[16...) custom-call(f32[2,8,32,128]{3,2,1,0:T(8,128)S(1)} %get-tuple-element, ...), custom_call_target="tpu_custom_call" | custom-call | tf_op jit(solution)/shard_map/fine/pallas_call | solution.py:444
  21.9 16.4 %all_to_all.10.all_ref = f32[32,16,128]{2,1,0:T(8,128)S(1)} all-to-all(f32[32,16,128]{2,1,0:T(8,128)S(1)} %get-tuple-element.34), channel_id=1, replica_groups=mesh['outer'=32,'inner'=16] {'outer'}, dimensions={0} | all-to-all | bytes 524288 | tf_op jit(solution)/shard_map/all_to_all | solution.py:487
  38.3 1.9 %middle.1 = (f32[16,16,128]{2,1,0:T(8,128)}, f32[24,128]{1,0:T(8,128)S(1)}, f32[12,16,128]{2,1,0:T(8,128)S(1)}, f32[12,16,128]{2,1,0:T(8,128)S(1)}, f32[12,16,12...) custom-call(f32[32,16,128]{2,1,0:T(8,128)S(1)} %all_to_all.10.all_ref), custom_call_target="tpu_custom_call" | custom-call | tf_op jit(solution)/shard_map/middle/pallas_call | solution.py:444
  40.1 17.0 %all-to-all-start.1 = ((f32[16,16,128]{2,1,0:T(8,128)}), f32[16,16,128]{2,1,0:T(8,128)S(1)}, u32[]{:S(2)}, u32[]{:S(2)}) async-start(f32[16,16,128]{2,1,0:T(8,128)} %get-tuple-element.35), calls=%async_computation.1 | async-start | bytes 262144 | tf_op jit(solution)/shard_map/all_to_all | solution.py:501
  57.1 1.3 %collective-permute-start.4 = (f32[24,128]{1,0:T(8,128)S(1)}, f32[24,128]{1,0:T(8,128)S(1)}, u32[]{:S(2)}, u32[]{:S(2)}) collective-permute-start(f32[24,128]{1,0:T(8,128)S(1)} %get-tuple-element.38), channel_id=1, source_target_pairs={{0,1},{1,2},{2,3},{3,4},{4,5},{5,6},{6,7},{7,8},{8,9},{9,10},{10,1... | collective-permute-start | bytes 36872 | tf_op jit(solution)/shard_map/ppermute | solution.py:500
  58.4 4.7 %collective-permute-start.5 = (f32[4,32,128]{2,1,0:T(8,128)S(1)}, f32[4,32,128]{2,1,0:T(8,128)S(1)}, u32[]{:S(2)}, u32[]{:S(2)}) collective-permute-start(f32[4,32,128]{2,1,0:T(8,128)S(1)} %get-tuple-element.39), channel_id=1, source_target_pairs={{16,32},{32,16},{48,64},{64,48},{80,96},{96,80},{112,128},{128,112... | collective-permute-start | bytes 196616 | tf_op jit(solution)/shard_map/ppermute | solution.py:499
  63.1 0.3 collective-permute-done.4
  63.4 1.9 %all-gather.1 = f32[304,128]{1,0:T(8,128)S(1)} all-gather(f32[152,128]{1,0:T(8,128)S(1)} %pad_maximum_fusion), channel_id=3, replica_groups={{0,16},{32,48},{64,80},{96,112},{128,144},{160,176},{192,208},{224,240}..., dimensions={0}, use_global_device_ids=true | all-gather | bytes 233472 | tf_op jit(solution)/shard_map/all_gather | solution.py:462
  65.3 4.0 %all-to-all-done.1 = f32[16,16,128]{2,1,0:T(8,128)S(1)} async-done(((f32[16,16,128]{2,1,0:T(8,128)}), f32[16,16,128]{2,1,0:T(8,128)S(1)}, u32[]{:S(2)}, u32[]{:S(2)}) %all-to-all-start.1) | async-done | bytes 131104 | tf_op jit(solution)/shard_map/all_to_all | solution.py:501
  69.3 4.4 %all-gather.2 = f32[32,16,128]{2,1,0:T(8,128)S(1)} all-gather(f32[16,16,128]{2,1,0:T(8,128)S(1)} %all-to-all-done.1), channel_id=4, replica_groups={{0,16},{32,48},{64,80},{96,112},{128,144},{160,176},{192,208},{224,240}..., dimensions={0}, use_global_device_ids=true | all-gather | bytes 393216 | tf_op jit(solution)/shard_map/all_gather | solution.py:462
  73.7 0.0 collective-permute-done.5.odd_ref
  73.7 3.9 %coarse.1 = (f32[8,32,128]{2,1,0:T(8,128)}, f32[8,32,128]{2,1,0:T(8,128)}) custom-call(f32[2,16,16,128]{3,2,1,0:T(8,128)S(1)} %bitcast.4, f32[2,152,128]{2,1,0:T(8,128)S(1)} %bitcast.5, f32[12,16,128]{2,1,0:T(8,128)S(1)} %get-tuple-element.42.k2_ref, f32[12,16,128]{2,1,0:T(8,128)S(1)} %get-tuple-element.43.inv2_ref, ...), custom_call_target="tpu_custom_call" | custom-call | tf_op jit(solution)/shard_map/coarse/pallas_call | solution.py:444
  (4 shorter events, 0.0 us)
Async XLA Ops:
  0.6 0.9 %copy-start = (f32[8,32,128]{2,1,0:T(8,128)S(1)}, f32[8,32,128]{2,1,0:T(8,128)}, u32[]{:S(2)}) copy-start(f32[8,32,128]{2,1,0:T(8,128)} %b_ref.1) | copy-start | bytes 393220
  1.5 0.9 %copy-start.1 = (s32[8,32,128]{2,1,0:T(8,128)S(1)}, s32[8,32,128]{2,1,0:T(8,128)}, u32[]{:S(2)}) copy-start(s32[8,32,128]{2,1,0:T(8,128)} %codes_ref.1) | copy-start | bytes 393220
  2.5 9.1 %collective-permute-start = (f32[2,8,16,128]{3,2,1,0:T(8,128)S(1)}, f32[2,8,16,128]{3,2,1,0:T(8,128)S(1)}, u32[]{:S(2)}, u32[]{:S(2)}) collective-permute-start(f32[2,8,16,128]{3,2,1,0:T(8,128)S(1)} %get-tuple-element.28), channel_id=1, source_target_pairs={{0,1},{1,0},{2,3},{3,2},{4,5},{5,4},{6,7},{7,6},{8,9},{9,8},{10,11... | collective-permute-start | bytes 393224 | tf_op jit(solution)/shard_map/ppermute | solution.py:468
  6.9 4.7 %collective-permute-start.1 = (f32[2,8,16,128]{3,2,1,0:T(8,128)S(1)}, f32[2,8,16,128]{3,2,1,0:T(8,128)S(1)}, u32[]{:S(2)}, u32[]{:S(2)}) collective-permute-start(f32[2,8,16,128]{3,2,1,0:T(8,128)S(1)} %get-tuple-element.29), channel_id=1, source_target_pairs={{1,2},{2,1},{3,4},{4,3},{5,6},{6,5},{7,8},{8,7},{9,10},{10,9},{11,... | collective-permute-start | bytes 393224 | tf_op jit(solution)/shard_map/ppermute | solution.py:469
  7.6 11.4 %collective-permute-start.2 = (f32[14,32,128]{2,1,0:T(8,128)S(1)}, f32[14,32,128]{2,1,0:T(8,128)S(1)}, u32[]{:S(2)}, u32[]{:S(2)}) collective-permute-start(f32[14,32,128]{2,1,0:T(8,128)S(1)} %get-tuple-element.32), channel_id=1, source_target_pairs={{16,32},{32,16},{48,64},{64,48},{80,96},{96,80},{112,128},{128,112... | collective-permute-start | bytes 688136 | tf_op jit(solution)/shard_map/ppermute | solution.py:470
  11.7 7.3 %collective-permute-start.3 = (f32[292,128]{1,0:T(8,128)S(1)}, f32[292,128]{1,0:T(8,128)S(1)}, u32[]{:S(2)}, u32[]{:S(2)}) collective-permute-start(f32[292,128]{1,0:T(8,128)S(1)} %get-tuple-element.33), channel_id=1, source_target_pairs={{16,32},{32,16},{48,64},{64,48},{80,96},{96,80},{112,128},{128,112... | collective-permute-start | bytes 448520 | tf_op jit(solution)/shard_map/ppermute | solution.py:476
  40.1 29.2 %all-to-all-start.1 = ((f32[16,16,128]{2,1,0:T(8,128)}), f32[16,16,128]{2,1,0:T(8,128)S(1)}, u32[]{:S(2)}, u32[]{:S(2)}) async-start(f32[16,16,128]{2,1,0:T(8,128)} %get-tuple-element.35), calls=%async_computation.1 | async-start | bytes 262144 | tf_op jit(solution)/shard_map/all_to_all | solution.py:501
  57.1 6.3 %collective-permute-start.4 = (f32[24,128]{1,0:T(8,128)S(1)}, f32[24,128]{1,0:T(8,128)S(1)}, u32[]{:S(2)}, u32[]{:S(2)}) collective-permute-start(f32[24,128]{1,0:T(8,128)S(1)} %get-tuple-element.38), channel_id=1, source_target_pairs={{0,1},{1,2},{2,3},{3,4},{4,5},{5,6},{6,7},{7,8},{8,9},{9,10},{10,1... | collective-permute-start | bytes 36872 | tf_op jit(solution)/shard_map/ppermute | solution.py:500
  58.4 15.3 %collective-permute-start.5 = (f32[4,32,128]{2,1,0:T(8,128)S(1)}, f32[4,32,128]{2,1,0:T(8,128)S(1)}, u32[]{:S(2)}, u32[]{:S(2)}) collective-permute-start(f32[4,32,128]{2,1,0:T(8,128)S(1)} %get-tuple-element.39), channel_id=1, source_target_pairs={{16,32},{32,16},{48,64},{64,48},{80,96},{96,80},{112,128},{128,112... | collective-permute-start | bytes 196616 | tf_op jit(solution)/shard_map/ppermute | solution.py:499
